TPU v7x, 512 devices: a whole 4x4x16 slice. The times are simulated.
512 devices in a mesh: dp: 128 (over y, z, core), mp: 4 (over x).
Axes of the slice: x: 4, y: 4, z: 16, core: 2. Of those that a mesh axis runs over, the one named last changes fastest.
Arguments:
- queries: bfloat16 [16384, 2048], P('dp', 'mp'), may hold values from -400 to 400
- encodings: bfloat16 [16384, 896], P('dp'), may hold values from -24 to 24
- kv_weight: bfloat16 [896, 2, 2048], P('dp', None, 'mp'), may hold values from -0.1875 to 0.1875
- pair_list: int32 [256, 2], P('dp'), may hold values from 0 to 127, as said below
- cotangent: bfloat16 [16384, 2048], P('dp', 'mp'), may hold values from -6 to 6
Outputs:
- attended: bfloat16 [16384, 2048], P('dp', 'mp')
- query_grad: bfloat16 [16384, 2048], P('dp', 'mp')
- encoding_grad: bfloat16 [16384, 896], P('dp', 'mp')
- weight_grad: float32 [896, 2, 2048], P('dp', None, 'mp')
Inputs may be any that keep to these rules, and one draw needn't show every extreme that they name: Each dp device owns one neighbour block, block n belongs to dp device n, and pair_list[c, j] is at most 2 positions away from c // 2 along dp, counted around the cycle of 128 devices.
All inputs are finite; a program needn't handle non-finite values.
Results may differ from a plain program's by a relative error of at most 0.034.
The roundings to bfloat16 on the way count: a program that leaves them out, or rounds other values in their place, can miss the bound.
Values may be sent and summed in bfloat16 or wider, within the bound.
No kernel may reach another device: no remote copies, remote signals or barrier semaphores. Data moves between devices by JAX's collectives and lax.ppermute only.
A program may use at most 64 MiB of HBM per device.

v0:
```python
import jax
import jax.numpy as jnp
from jax import lax
from jax.sharding import PartitionSpec as P

HD = 128
SPAN = 64
NROWS = 128
NBR = 2
REACH = 2


def shifted(value, axis, steps):
    count = lax.axis_size(axis)
    pairs = [(source, (source + steps) % count) for source in range(count)]
    return lax.ppermute(value, axis, pairs)


def project(rows, weights):
    return jnp.einsum("re,etx->rtx", rows, weights, preferred_element_type=jnp.float32).astype(
        jnp.bfloat16
    )


def fetch_window(block, reach):
    pieces = []
    for offset in range(-reach, reach + 1):
        if offset == 0:
            pieces.append(block)
        else:
            pieces.append(shifted(block, "dp", -offset))
    return pieces


def return_grads(contrib, reach):
    total = contrib[reach]
    for offset in range(-reach, reach + 1):
        if offset != 0:
            total = total + shifted(contrib[offset + reach], "dp", offset)
    return total


def per_device(queries, encodings, kv_weight, pair_list, cotangent):
    reach = REACH
    device_count = lax.axis_size("dp")
    my_index = lax.axis_index("dp")
    factor = 1.0 / HD**0.5
    weights = lax.all_gather(kv_weight, "dp", axis=0, tiled=True)
    columns = weights.shape[2]
    heads_here = columns // HD
    owned_rows = encodings.shape[0]
    slot_count = owned_rows // NROWS
    window_size = 2 * reach + 1
    own_blocks = project(encodings, weights)
    window = jnp.stack(fetch_window(own_blocks, reach), axis=0)
    pair_ids = pair_list.reshape(-1)
    owners = pair_ids // slot_count
    slot_index = pair_ids % slot_count
    offsets = (owners - my_index + reach) % device_count
    window_index = offsets * slot_count + slot_index
    span_count = pair_list.shape[0]
    chosen = jnp.take(window, window_index, axis=0).reshape(
        span_count, NBR * NROWS, 2, heads_here, HD
    )
    keys = chosen[:, :, 0]
    values = chosen[:, :, 1]
    query_rows = queries.reshape(span_count, SPAN, heads_here, HD)
    grad_rows = cotangent.reshape(span_count, SPAN, heads_here, HD)
    scores = (
        jnp.einsum("cqhd,ckhd->chqk", query_rows, keys, preferred_element_type=jnp.float32) * factor
    )
    probs = jax.nn.softmax(scores, axis=-1)
    probs_b = probs.astype(jnp.bfloat16)
    attended = jnp.einsum(
        "chqk,ckhd->cqhd", probs_b, values, preferred_element_type=jnp.float32
    ).astype(jnp.bfloat16)
    dprobs = jnp.einsum("cqhd,ckhd->chqk", grad_rows, values, preferred_element_type=jnp.float32)
    delta = jnp.sum(probs * dprobs, axis=-1, keepdims=True)
    dscores = (probs * (dprobs - delta) * factor).astype(jnp.bfloat16)
    query_grad = jnp.einsum(
        "chqk,ckhd->cqhd", dscores, keys, preferred_element_type=jnp.float32
    ).astype(jnp.bfloat16)
    key_grad = jnp.einsum(
        "chqk,cqhd->ckhd", dscores, query_rows, preferred_element_type=jnp.float32
    )
    value_grad = jnp.einsum(
        "chqk,cqhd->ckhd", probs_b, grad_rows, preferred_element_type=jnp.float32
    )
    pair_grads = jnp.stack([key_grad, value_grad], axis=2).reshape(
        span_count * NBR, NROWS * 2 * columns
    )
    one_hot = (
        window_index[:, None] == jnp.arange(window_size * slot_count, dtype=jnp.int32)[None, :]
    ).astype(jnp.float32)
    contrib = jnp.einsum("pw,pr->wr", one_hot, pair_grads, precision=lax.Precision.HIGHEST)
    contrib = contrib.reshape(window_size, owned_rows, 2, columns)
    block_grad = return_grads([contrib[index] for index in range(window_size)], reach)
    block_grad_b = block_grad.astype(jnp.bfloat16)
    partial_sum = jnp.einsum(
        "rtx,etx->re", block_grad_b, weights, preferred_element_type=jnp.float32
    )
    encoding_grad = lax.psum_scatter(
        partial_sum.astype(jnp.bfloat16), "mp", scatter_dimension=1, tiled=True
    )
    flat_grad = block_grad_b.reshape(owned_rows, 2 * columns)
    product = jnp.einsum("rc,rx->cx", encodings, flat_grad, preferred_element_type=jnp.float32)
    weight_grad = lax.psum_scatter(
        product.reshape(kv_weight.shape[0] * lax.axis_size("dp"), 2, columns),
        "dp",
        scatter_dimension=0,
        tiled=True,
    )
    return (
        attended.reshape(span_count * SPAN, columns),
        query_grad.reshape(span_count * SPAN, columns),
        encoding_grad,
        weight_grad,
    )


def solution(mesh):
    return jax.shard_map(
        per_device,
        mesh=mesh,
        in_specs=(P("dp", "mp"), P("dp", None), P("dp", None, "mp"), P("dp", None), P("dp", "mp")),
        out_specs=(P("dp", "mp"), P("dp", "mp"), P("dp", "mp"), P("dp", None, "mp")),
        check_vma=False,
    )
```

profile of v0, /device:TPU:6, one launch (start us, length us, event | category | flops | bytes accessed | tf_op | source)
XLA Modules:
  0.0 642.5 jit_solution(6850920196117562361)
XLA Ops:
  8.9 146.0 %all-gather.2.cloned.1.call-done = bf16[896,2,512]{2,1,0:T(2,128)(2,1)} async-done(((bf16[7,2,512]{2,1,0:T(2,128)(2,1)}), bf16[896,2,512]{2,1,0:T(2,128)(2,1)}) %all-gather.2.cloned.1.call-update) | async-done | bytes 1835024 | tf_op jit(solution)/shard_map/all_gather | solution.py:48
  156.9 2.5 collective-permute-start
  162.2 7.0 %collective-permute-start.2 = (bf16[128,2,512]{2,0,1:T(8,128)(2,1)S(1)}, bf16[128,2,512]{2,0,1:T(8,128)(2,1)S(1)}, u32[]{:S(2)}, u32[]{:S(2)}) collective-permute-start(bf16[128,2,512]{2,0,1:T(8,128)(2,1)S(1)} %fusion.16), channel_id=1, source_target_pairs={{0,508},{4,0},{8,4},{12,8},{16,12},{20,16},{24,20},{28,24},{32,28}... | collective-permute-start | bytes 786440 | tf_op jit(solution)/shard_map/ppermute | solution.py:16
  169.1 3.3 collective-permute-start.3
  174.4 4.2 collective-permute-done.3
  184.2 5.7 convolution_bitcast_fusion.1
  191.3 2.7 copy.46
  194.0 3.0 reshape.127
  197.0 2.8 fusion.37
  199.8 10.1 %slice_reduce_fusion.3 = (f32[131072]{0:T(1024)S(1)}, f32[131072]{0:T(1024)}, f32[131072]{0:T(1024)S(1)}, f32[131072]{0:T(1024)S(1)}, f32[131072]{0:T(1024)S(1)}) fusion(f32[5,131072]{1,0:T(8,128)S(1)} %fusion.37), kind=kLoop, calls=%fused_computation.33 | loop fusion | bytes 5242880 | tf_op jit(solution)/shard_map/slice | solution.py:97
  209.9 2.1 squeeze.27
  212.0 2.1 copy.51
  217.0 2.1 copy.50
  222.3 7.0 %collective-permute-start.5 = (f32[128,2,512]{0,2,1:T(8,128)}, f32[128,2,512]{0,2,1:T(8,128)}, u32[]{:S(2)}, u32[]{:S(2)}) collective-permute-start(f32[128,2,512]{0,2,1:T(8,128)} %copy.49), channel_id=1, source_target_pairs={{0,508},{4,0},{8,4},{12,8},{16,12},{20,16},{24,20},{28,24},{32,28}... | collective-permute-start | bytes 1572872 | tf_op jit(solution)/shard_map/ppermute | solution.py:16
  229.8 4.4 collective-permute-start.4
  234.9 3.6 collective-permute-done.6
  239.3 8.1 %collective-permute-done.4 = f32[128,2,512]{0,2,1:T(8,128)S(1)} collective-permute-done((f32[128,2,512]{0,2,1:T(8,128)S(1)}, f32[128,2,512]{0,2,1:T(8,128)S(1)}, u32[]{:S(2)}, u32[]{:S(2)}) %collective-permute-start.4) | collective-permute-done | bytes 524320 | tf_op jit(solution)/shard_map/ppermute | solution.py:16
  248.9 2.5 fusion.48
  251.4 6.6 %copy.54 = f32[896,2,512]{2,1,0:T(2,128)} copy(f32[896,2,512]{0,2,1:T(8,128)} %bitcast.72) | data formatting | bytes 7340032 | tf_op jit(solution)/shard_map/reshape | solution.py:108
  260.0 4.0 fusion.23
  264.0 2.9 fusion.19
  266.9 2.2 fusion.22
  270.0 337.8 %all-reduce.3.cloned.1.call-done = f32[896,2,512]{2,1,0:T(2,128)} async-done(((f32[896,2,512]{2,1,0:T(2,128)}), f32[896,2,512]{2,1,0:T(2,128)}) %all-reduce.3.cloned.1.call-update) | async-done | bytes 3670032
  609.2 26.7 %reduce-scatter.2.cloned.1.call-done = bf16[128,224]{0,1:T(8,128)(2,1)} async-done(((bf16[128,896]{0,1:T(8,128)(2,1)}), bf16[128,224]{0,1:T(8,128)(2,1)}) %reduce-scatter.2.cloned.1.call-update) | async-done | bytes 57360 | tf_op jit(solution)/shard_map/reduce_scatter | solution.py:102
  (62 shorter events, 28.6 us)
Async XLA Ops:
  7.2 147.8 %copy-start = (bf16[128,896]{1,0:T(8,128)(2,1)S(1)}, bf16[128,896]{1,0:T(8,128)(2,1)}, u32[]{:S(2)}) copy-start(bf16[128,896]{1,0:T(8,128)(2,1)} %param.6) | copy-start | bytes 688132
  7.2 154.2 %copy-start.3 = (bf16[128,512]{1,0:T(8,128)(2,1)S(1)}, bf16[128,512]{1,0:T(8,128)(2,1)}, u32[]{:S(2)}) copy-start(bf16[128,512]{1,0:T(8,128)(2,1)} %param.9) | copy-start | bytes 393220
  7.2 154.9 %copy-start.4 = (bf16[128,512]{1,0:T(8,128)(2,1)S(1)}, bf16[128,512]{1,0:T(8,128)(2,1)}, u32[]{:S(2)}) copy-start(bf16[128,512]{1,0:T(8,128)(2,1)} %param.5) | copy-start | bytes 393220
  7.2 147.7 %all-gather.2.cloned.1.call-start = ((), (), s32[]{:S(2)}) async-start(), calls=%async_computation.1 | async-start | bytes 1849344 | tf_op jit(solution)/shard_map/all_gather | solution.py:48
  7.9 599.9 %all-reduce.3.cloned.1.call-start = ((), (), s32[]{:S(2)}) async-start(), calls=%async_computation.3 | async-start | bytes 7340032
  156.9 15.5 %collective-permute-start = (bf16[128,2,512]{2,0,1:T(8,128)(2,1)S(1)}, bf16[128,2,512]{2,0,1:T(8,128)(2,1)S(1)}, u32[]{:S(2)}, u32[]{:S(2)}) collective-permute-start(bf16[128,2,512]{2,0,1:T(8,128)(2,1)S(1)} %fusion.16), channel_id=1, source_target_pairs={{0,8},{4,12},{8,16},{12,20},{16,24},{20,28},{24,32},{28,36},{32,40... | collective-permute-start | bytes 786440 | tf_op jit(solution)/shard_map/ppermute | solution.py:16
  159.5 13.9 %collective-permute-start.1 = (bf16[128,2,512]{2,0,1:T(8,128)(2,1)S(1)}, bf16[128,2,512]{2,0,1:T(8,128)(2,1)S(1)}, u32[]{:S(2)}, u32[]{:S(2)}) collective-permute-start(bf16[128,2,512]{2,0,1:T(8,128)(2,1)S(1)} %fusion.16), channel_id=1, source_target_pairs={{0,4},{4,8},{8,12},{12,16},{16,20},{20,24},{24,28},{28,32},{32,36}... | collective-permute-start | bytes 786440 | tf_op jit(solution)/shard_map/ppermute | solution.py:16
  162.2 12.2 %collective-permute-start.2 = (bf16[128,2,512]{2,0,1:T(8,128)(2,1)S(1)}, bf16[128,2,512]{2,0,1:T(8,128)(2,1)S(1)}, u32[]{:S(2)}, u32[]{:S(2)}) collective-permute-start(bf16[128,2,512]{2,0,1:T(8,128)(2,1)S(1)} %fusion.16), channel_id=1, source_target_pairs={{0,508},{4,0},{8,4},{12,8},{16,12},{20,16},{24,20},{28,24},{32,28}... | collective-permute-start | bytes 786440 | tf_op jit(solution)/shard_map/ppermute | solution.py:16
  169.1 9.5 %collective-permute-start.3 = (bf16[128,2,512]{2,0,1:T(8,128)(2,1)S(1)}, bf16[128,2,512]{2,0,1:T(8,128)(2,1)S(1)}, u32[]{:S(2)}, u32[]{:S(2)}) collective-permute-start(bf16[128,2,512]{2,0,1:T(8,128)(2,1)S(1)} %fusion.16), channel_id=1, source_target_pairs={{0,504},{4,508},{8,0},{12,4},{16,8},{20,12},{24,16},{28,20},{32,24... | collective-permute-start | bytes 786440 | tf_op jit(solution)/shard_map/ppermute | solution.py:16
  179.7 0.9 copy-start.2
  182.0 7.9 %copy-start.1 = (f32[2,4,64,256]{3,2,1,0:T(8,128)}, f32[2,4,64,256]{3,2,1,0:T(8,128)S(1)}, u32[]{:S(2)}) copy-start(f32[2,4,64,256]{3,2,1,0:T(8,128)S(1)} %fusion.11) | copy-start | bytes 1572868
  214.0 20.9 %collective-permute-start.7 = (f32[128,2,512]{0,2,1:T(8,128)}, f32[128,2,512]{0,2,1:T(8,128)}, u32[]{:S(2)}, u32[]{:S(2)}) collective-permute-start(f32[128,2,512]{0,2,1:T(8,128)} %copy.51), channel_id=1, source_target_pairs={{0,8},{4,12},{8,16},{12,20},{16,24},{20,28},{24,32},{28,36},{32,40... | collective-permute-start | bytes 1572872 | tf_op jit(solution)/shard_map/ppermute | solution.py:16
  219.1 19.4 %collective-permute-start.6 = (f32[128,2,512]{0,2,1:T(8,128)}, f32[128,2,512]{0,2,1:T(8,128)}, u32[]{:S(2)}, u32[]{:S(2)}) collective-permute-start(f32[128,2,512]{0,2,1:T(8,128)} %copy.50), channel_id=1, source_target_pairs={{0,4},{4,8},{8,12},{12,16},{16,20},{20,24},{24,28},{28,32},{32,36}... | collective-permute-start | bytes 1572872 | tf_op jit(solution)/shard_map/ppermute | solution.py:16
  222.3 17.0 %collective-permute-start.5 = (f32[128,2,512]{0,2,1:T(8,128)}, f32[128,2,512]{0,2,1:T(8,128)}, u32[]{:S(2)}, u32[]{:S(2)}) collective-permute-start(f32[128,2,512]{0,2,1:T(8,128)} %copy.49), channel_id=1, source_target_pairs={{0,508},{4,0},{8,4},{12,8},{16,12},{20,16},{24,20},{28,24},{32,28}... | collective-permute-start | bytes 1572872 | tf_op jit(solution)/shard_map/ppermute | solution.py:16
  229.8 17.6 %collective-permute-start.4 = (f32[128,2,512]{0,2,1:T(8,128)S(1)}, f32[128,2,512]{0,2,1:T(8,128)S(1)}, u32[]{:S(2)}, u32[]{:S(2)}) collective-permute-start(f32[128,2,512]{0,2,1:T(8,128)S(1)} %copy.47), channel_id=1, source_target_pairs={{0,504},{4,508},{8,0},{12,4},{16,8},{20,12},{24,16},{28,20},{32,24... | collective-permute-start | bytes 1572872 | tf_op jit(solution)/shard_map/ppermute | solution.py:16
  258.0 378.0 %reduce-scatter.2.cloned.1.call-start = ((), (), s32[]{:S(2)}) async-start(), calls=%async_computation.2 | async-start | bytes 286720 | tf_op jit(solution)/shard_map/reduce_scatter | solution.py:102
Sparse Core Ops, SparseCore 0:
  11.1 143.8 all-gather.1
  258.1 349.6 all-reduce.2
  611.2 24.6 reduce-scatter.1
where the time goes:
time: 645 us; the launch traced here: 642 us
  waiting for transfers between devices  530 us (82%)
  local copies, waits for them, and re-layouts  38.3 us (6%)
  starting transfers between devices  30 us (5%)
  matrix products  24.6 us (4%)
  between operations  14.7 us (2%)
    unnamed x4, waiting for transfers between devices  339 us
    all_gather x1, waiting for transfers between devices, per_device(): weights = lax.all_gather(kv_weight, 'dp', axis=0, tiled=True)  146 us
    ppermute x8, starting transfers between devices, shifted(): return lax.ppermute(value, axis, pairs)  29.9 us
    reduce_scatter x1, waiting for transfers between devices, per_device(): lax.psum_scatter(partial_sum.astype(jnp.bfloat16), 'mp', scatter_dimensio...  26.7 us
    ppermute x8, waiting for transfers between devices, shifted(): return lax.ppermute(value, axis, pairs)  18.8 us
  transfers between devices with their start and end apart: 11, of which 10 were waited for; matrix products, arithmetic and copies ran while one was open for 3% of the time, Pallas kernels for 0%

commit v1 on v0

v1 whole, which is shorter than its diff:
```python
import jax
import jax.numpy as jnp
from jax import lax
from jax.experimental import pallas as pl
from jax.experimental.pallas import tpu as pltpu
from jax.sharding import Mesh
from jax.sharding import PartitionSpec as P

HD = 128
SPAN = 64
NROWS = 128
NBR = 2
NY = 4
NZ = 16
NC = 2
NX = 4
DP = ("y", "z", "c")
ENC = 896
OWN = 7
PAD = 8
COLS = 1024
HALF = NY * NZ * PAD
NT = (((1,), (1,)), ((), ()))
TN = (((0,), (0,)), ((), ()))
SLOT_OWN, SLOT_RIGHT, SLOT_LEFT, SLOT_SWAP, SLOT_CROSS = range(5)


def swap_cores(value):
    return lax.ppermute(value, "c", [(0, 1), (1, 0)])


def shifted(value, steps):
    count = NY * NZ * NC
    return lax.ppermute(value, DP, [(i, (i + steps) % count) for i in range(count)])


def crossed(value):
    count = NY * NZ * NC
    return lax.ppermute(
        value, DP, [(i, (i + (1 if i % 2 else -1)) % count) for i in range(count)]
    )


def spread(value, axis, count):
    return lax.all_to_all(
        jnp.broadcast_to(value[None], (count,) + value.shape), axis, 0, 0
    )


def natural_column(core):
    place = jnp.arange(NC * HALF, dtype=jnp.int32)
    row = place % PAD
    z = place // PAD % NZ
    y = place // (PAD * NZ) % NY
    c = (place // HALF + core) % NC
    return jnp.where(row < OWN, ((y * NZ + z) * NC + c) * OWN + row, -1)


def attention_kernel(
    sel_ref, core_ref, x_ref, xt_ref, wa_ref, wb_ref, q_ref, g_ref,
    att_ref, qg_ref, keep_ref, send_ref, ekeep_ref, kv_ref, cb_ref, acc_ref,
):
    f32, b16 = jnp.float32, jnp.bfloat16
    factor = 1.0 / HD**0.5
    kv = jnp.dot(x_ref[:, :HALF], wa_ref[...], preferred_element_type=f32)
    kv = kv + jnp.dot(x_ref[:, HALF:], wb_ref[...], preferred_element_type=f32)
    kv_ref[...] = kv.astype(b16)
    keys_here = NBR * NROWS
    heads = COLS // 2 // HD
    for span in range(2):
        rows = slice(span * SPAN, (span + 1) * SPAN)
        krows = slice(span * keys_here, (span + 1) * keys_here)
        for head in range(heads):
            kc = slice(head * HD, (head + 1) * HD)
            vc = slice((heads + head) * HD, (heads + head + 1) * HD)
            q, g = q_ref[rows, kc], g_ref[rows, kc]
            k, v = kv_ref[krows, kc], kv_ref[krows, vc]
            scores = lax.dot_general(q, k, NT, preferred_element_type=f32) * factor
            top = jnp.max(scores, axis=-1, keepdims=True)
            raised = jnp.exp(scores - top)
            probs = raised / jnp.sum(raised, axis=-1, keepdims=True)
            probs_b = probs.astype(b16)
            att_ref[rows, kc] = jnp.dot(probs_b, v, preferred_element_type=f32).astype(b16)
            dprobs = lax.dot_general(g, v, NT, preferred_element_type=f32)
            delta = jnp.sum(probs * dprobs, axis=-1, keepdims=True)
            dscores = (probs * (dprobs - delta) * factor).astype(b16)
            qg_ref[rows, kc] = jnp.dot(dscores, k, preferred_element_type=f32).astype(b16)
            kgrad = lax.dot_general(dscores, q, TN, preferred_element_type=f32)
            vgrad = lax.dot_general(probs_b, g, TN, preferred_element_type=f32)
            cb_ref[krows, kc] = kgrad.astype(b16)
            cb_ref[krows, vc] = vgrad.astype(b16)
    keep_ref[...] = jnp.dot(
        xt_ref[:HALF, :], cb_ref[...], preferred_element_type=f32
    ).astype(b16)
    send_ref[:HALF, :] = jnp.dot(
        xt_ref[HALF:, :], cb_ref[...], preferred_element_type=f32
    ).astype(b16)
    acc_ref[...] = jnp.zeros_like(acc_ref)
    core = core_ref[0]
    for half, w_ref in ((0, wa_ref), (1, wb_ref)):
        part = lax.dot_general(cb_ref[...], w_ref[...], NT, preferred_element_type=f32)
        c = (core + half) % NC
        for pair in range(2 * NBR):
            for y in range(NY):
                lanes = pl.ds(pl.multiple_of(y * 256 + c * 128, 128), 128)
                acc_ref[sel_ref[pair], :, lanes] += part[
                    pair * NROWS : (pair + 1) * NROWS, y * 128 : (y + 1) * 128
                ]
    for place in range(3):
        ekeep_ref[place * NROWS : (place + 1) * NROWS, :] = acc_ref[place].astype(b16)
    for place in range(2):
        send_ref[HALF + place * NROWS : HALF + (place + 1) * NROWS, :] = acc_ref[
            3 + place
        ].astype(b16)


def attend(sel, core, x, xt, wa, wb, q, g):
    b16 = jnp.bfloat16
    vmem = pl.BlockSpec(memory_space=pltpu.VMEM)
    smem = pl.BlockSpec(memory_space=pltpu.SMEM)
    return pl.pallas_call(
        attention_kernel,
        out_shape=(
            jax.ShapeDtypeStruct(q.shape, b16),
            jax.ShapeDtypeStruct(q.shape, b16),
            jax.ShapeDtypeStruct((HALF, COLS), b16),
            jax.ShapeDtypeStruct((HALF + 2 * NROWS, COLS), b16),
            jax.ShapeDtypeStruct((3 * NROWS, COLS), b16),
        ),
        in_specs=[smem, smem] + [vmem] * 6,
        out_specs=(vmem,) * 5,
        scratch_shapes=[
            pltpu.VMEM((4 * NROWS, COLS), b16),
            pltpu.VMEM((4 * NROWS, COLS), b16),
            pltpu.VMEM((5, NROWS, COLS), jnp.float32),
        ],
        compiler_params=pltpu.CompilerParams(vmem_limit_bytes=40 * 2**20),
        cost_estimate=pl.CostEstimate(
            flops=4_000_000_000, bytes_accessed=8_000_000, transcendentals=131072
        ),
    )(sel, core, x, xt, wa, wb, q, g)


def per_device(queries, encodings, kv_weight, pair_list, cotangent):
    f32, b16 = jnp.float32, jnp.bfloat16
    core = lax.axis_index("c")
    me = (lax.axis_index("y") * NZ + lax.axis_index("z")) * NC + core
    count = NY * NZ * NC

    shard = jnp.pad(kv_weight.reshape(OWN, COLS), ((0, PAD - OWN), (0, 0)))
    w = spread(shard, "z", NZ).reshape(NZ * PAD, COLS)
    w = spread(w, "y", NY).reshape(HALF, COLS)
    w_other = swap_cores(w)

    window = jnp.stack(
        [
            encodings,
            shifted(encodings, -2),
            shifted(encodings, 2),
            swap_cores(encodings),
            crossed(encodings),
        ]
    )
    offset = (pair_list.reshape(-1) - me + count) % count
    near = jnp.where(core == 0, 1, count - 1)
    sel = jnp.where(
        offset == 0,
        SLOT_OWN,
        jnp.where(
            offset == 2,
            SLOT_RIGHT,
            jnp.where(
                offset == count - 2,
                SLOT_LEFT,
                jnp.where(offset == near, SLOT_SWAP, SLOT_CROSS),
            ),
        ),
    ).astype(jnp.int32)
    chosen = jnp.take(window, sel, axis=0, mode="clip").reshape(4 * NROWS, ENC)
    column = natural_column(core)
    pick = (jnp.arange(ENC, dtype=jnp.int32)[:, None] == column[None, :]).astype(b16)
    x = jnp.dot(chosen, pick, preferred_element_type=f32).astype(b16)
    xt = lax.dot_general(pick, chosen, (((0,), (1,)), ((), ())), preferred_element_type=f32)
    xt = xt.astype(b16)

    attended, query_grad, keep, send, ekeep = attend(
        sel, core.reshape(1), x, xt, w, w_other, queries, cotangent
    )

    got = swap_cores(send)
    total = (keep.astype(f32) + got[:HALF].astype(f32)).astype(b16)
    parts = lax.all_to_all(total.reshape(NY, NZ * PAD, COLS), "y", 0, 0)
    total = jnp.sum(parts.astype(f32), axis=0).astype(b16)
    parts = lax.all_to_all(total.reshape(NZ, PAD, COLS), "z", 0, 0)
    weight_grad = jnp.sum(parts.astype(f32), axis=0)[:OWN].reshape(OWN, 2, COLS // 2)

    own = ekeep[:NROWS].astype(f32) + got[HALF : HALF + NROWS].astype(f32)
    cross = got[HALF + NROWS :].astype(f32)
    right = ekeep[NROWS : 2 * NROWS].astype(f32) + jnp.where(core == 0, cross, 0.0)
    left = ekeep[2 * NROWS :].astype(f32) + jnp.where(core == 1, cross, 0.0)
    from_left = shifted(right.astype(b16), 2)
    from_right = shifted(left.astype(b16), -2)
    mine = (own + from_left.astype(f32) + from_right.astype(f32)).astype(b16)
    mine = mine.reshape(NROWS, NX, COLS // NX).transpose(1, 0, 2)
    groups = lax.all_to_all(mine, "x", 0, 0)
    summed = jnp.sum(groups.astype(f32), axis=0).astype(b16)
    place = jnp.arange(COLS // NX, dtype=jnp.int32)
    row, z, c = place % PAD, place // PAD % NZ, place // (PAD * NZ)
    column = jnp.where(row < OWN, (z * NC + c) * OWN + row, -1)
    pick = (column[:, None] == jnp.arange(ENC // NX, dtype=jnp.int32)[None, :]).astype(b16)
    encoding_grad = jnp.dot(summed, pick, preferred_element_type=f32).astype(b16)
    return attended, query_grad, encoding_grad, weight_grad


def solution(mesh):
    mesh = Mesh(mesh.devices.reshape(NY, NZ, NC, NX), ("y", "z", "c", "x"))
    return jax.shard_map(
        per_device,
        mesh=mesh,
        in_specs=(P(DP, "x"), P(DP, None), P(DP, None, "x"), P(DP, None), P(DP, "x")),
        out_specs=(P(DP, "x"), P(DP, "x"), P(DP, "x"), P(DP, None, "x")),
        check_vma=False,
    )
```

time: 645 us -> 139 us (0.22)
  the two profiles are of different devices: /device:TPU:6 before, /device:TPU:56 now
where the time goes in v1:
time: 139 us; the launch traced here: 138 us
  starting transfers between devices  61.4 us (44%)
  waiting for transfers between devices  48.8 us (35%)
  local copies, waits for them, and re-layouts  10 us (7%)
  Pallas kernels  8.67 us (6%)
  matrix products  4.81 us (3%)
  other arithmetic  3.47 us (2%)
    all_to_all x2, starting transfers between devices, spread(): lax.all_to_all(jnp.broadcast_to(value[None], (count,) + value.shape), axi...  19.9 us
    all_to_all x2, waiting for transfers between devices, spread(): lax.all_to_all(jnp.broadcast_to(value[None], (count,) + value.shape), axi...  16.8 us
    all_to_all x1, waiting for transfers between devices, per_device(): parts = lax.all_to_all(total.reshape(NZ, PAD, COLS), 'z', 0, 0)  16.4 us
    ppermute x4, starting transfers between devices, shifted(): lax.ppermute(value, DP, [(i, (i + steps) % count) for i in range(count)])  11.7 us
    all_to_all x1, starting transfers between devices, per_device(): parts = lax.all_to_all(total.reshape(NZ, PAD, COLS), 'z', 0, 0)  10.3 us
    pallas_call x1, Pallas kernels, attend(): pl.pallas_call(attention_kernel, out_shape=(jax.ShapeDtypeStruct(q.shape,...  8.67 us
    ppermute x4, waiting for transfers between devices, shifted(): lax.ppermute(value, DP, [(i, (i + steps) % count) for i in range(count)])  6.78 us
    ppermute x3, starting transfers between devices, swap_cores(): return lax.ppermute(value, 'c', [(0, 1), (1, 0)])  6.23 us
  transfers between devices with their start and end apart: 13, of which 8 were waited for; matrix products, arithmetic and copies ran while one was open for 11% of the time, Pallas kernels for 0%

profile of v1, /device:TPU:56, one launch (start us, length us, event | category | flops | bytes accessed | tf_op | source)
XLA Modules:
  0.0 138.0 jit_solution(10756059042324594347)
XLA Ops:
  2.1 15.2 %all-to-all-start = ((bf16[16,8,1024]{2,1,0:T(8,128)(2,1)}), bf16[16,8,1024]{2,1,0:T(8,128)(2,1)S(1)}, u32[]{:S(2)}, u32[]{:S(2)}) async-start(bf16[16,8,1024]{2,1,0:T(8,128)(2,1)} %broadcast_in_dim.54), calls=%async_computation | async-start | bytes 524288 | tf_op jit(solution)/shard_map/all_to_all | solution.py:45
  17.3 2.0 %collective-permute-start = (bf16[128,896]{1,0:T(8,128)(2,1)}, bf16[128,896]{1,0:T(8,128)(2,1)S(1)}, u32[]{:S(2)}, u32[]{:S(2)}) collective-permute-start(bf16[128,896]{1,0:T(8,128)(2,1)} %param.6), channel_id=1, source_target_pairs={{0,504},{4,508},{8,0},{12,4},{16,8},{20,12},{24,16},{28,20},{32,24... | collective-permute-start | bytes 688136 | tf_op jit(solution)/shard_map/ppermute | solution.py:34
  19.3 3.8 %collective-permute-start.1 = (bf16[128,896]{1,0:T(8,128)(2,1)}, bf16[128,896]{1,0:T(8,128)(2,1)S(1)}, u32[]{:S(2)}, u32[]{:S(2)}) collective-permute-start(bf16[128,896]{1,0:T(8,128)(2,1)} %param.6), channel_id=1, source_target_pairs={{0,8},{4,12},{8,16},{12,20},{16,24},{20,28},{24,32},{28,36},{32,40... | collective-permute-start | bytes 688136 | tf_op jit(solution)/shard_map/ppermute | solution.py:34
  23.1 1.9 %collective-permute-start.2 = (bf16[128,896]{1,0:T(8,128)(2,1)}, bf16[128,896]{1,0:T(8,128)(2,1)S(1)}, u32[]{:S(2)}, u32[]{:S(2)}) collective-permute-start(bf16[128,896]{1,0:T(8,128)(2,1)} %param.6), channel_id=1, source_target_pairs={{0,4},{4,0},{1,5},{5,1},{2,6},{6,2},{3,7},{7,3},{8,12},{12,8},{9,1... | collective-permute-start | bytes 688136 | tf_op jit(solution)/shard_map/ppermute | solution.py:29
  25.1 3.4 %collective-permute-start.3 = (bf16[128,896]{1,0:T(8,128)(2,1)}, bf16[128,896]{1,0:T(8,128)(2,1)S(1)}, u32[]{:S(2)}, u32[]{:S(2)}) collective-permute-start(bf16[128,896]{1,0:T(8,128)(2,1)} %param.6), channel_id=1, source_target_pairs={{0,508},{4,8},{8,4},{12,16},{16,12},{20,24},{24,20},{28,32},{32,28... | collective-permute-start | bytes 688136 | tf_op jit(solution)/shard_map/ppermute | solution.py:39
  30.3 6.0 %all-to-all-done = bf16[16,8,1024]{2,1,0:T(8,128)(2,1)S(1)} async-done(((bf16[16,8,1024]{2,1,0:T(8,128)(2,1)}), bf16[16,8,1024]{2,1,0:T(8,128)(2,1)S(1)}, u32[]{:S(2)}, u32[]{:S(2)}) %all-to-all-start) | async-done | bytes 262176 | tf_op jit(solution)/shard_map/all_to_all | solution.py:45
  37.3 4.7 %all-to-all-start.1 = ((bf16[4,128,1024]{2,1,0:T(8,128)(2,1)}), bf16[4,128,1024]{2,1,0:T(8,128)(2,1)S(1)}, u32[]{:S(2)}, u32[]{:S(2)}) async-start(bf16[4,128,1024]{2,1,0:T(8,128)(2,1)} %broadcast_in_dim.56), calls=%async_computation.1 | async-start | bytes 2097152 | tf_op jit(solution)/shard_map/all_to_all | solution.py:45
  42.2 10.8 %all-to-all-done.1 = bf16[4,128,1024]{2,1,0:T(8,128)(2,1)S(1)} async-done(((bf16[4,128,1024]{2,1,0:T(8,128)(2,1)}), bf16[4,128,1024]{2,1,0:T(8,128)(2,1)S(1)}, u32[]{:S(2)}, u32[]{:S(2)}) %all-to-all-start.1) | async-done | bytes 1048608 | tf_op jit(solution)/shard_map/all_to_all | solution.py:45
  53.0 1.9 %collective-permute-start.4 = (bf16[512,1024]{1,0:T(8,128)(2,1)S(1)}, bf16[512,1024]{1,0:T(8,128)(2,1)S(1)}, u32[]{:S(2)}, u32[]{:S(2)}) collective-permute-start(bf16[512,1024]{1,0:T(8,128)(2,1)S(1)} %bitcast.31), channel_id=1, source_target_pairs={{0,4},{4,0},{1,5},{5,1},{2,6},{6,2},{3,7},{7,3},{8,12},{12,8},{9,1... | collective-permute-start | bytes 3145736 | tf_op jit(solution)/shard_map/ppermute | solution.py:29
  57.0 2.8 %gather_fusion = bf16[4,128,896]{2,1,0:T(8,128)(2,1)} fusion(bf16[5,128,896]{2,1,0:T(8,128)(2,1)} %bitcast_dynamic-update-slice_fusion, s32[1024]{0:T(1024)S(1)} %pad_clamp_fusion), kind=kCustom, calls=%fused_computation | custom fusion | bytes 1835024 | tf_op jit(solution)/shard_map/jit(_take)/gather | solution.py:179
  59.9 2.6 %fusion.6.xt_ref = bf16[1024,512]{1,0:T(8,128)(2,1)S(1)} fusion(bf16[512,896]{1,0:T(8,128)(2,1)} %bitcast.35, s32[1024]{0:T(1024)S(1)} %fusion.22), kind=kOutput, calls=%fused_computation.8 | convolution fusion | flops 941883392 | bytes 1970176 | tf_op jit(solution)/shard_map/dot_general | solution.py:183
  63.8 8.7 %shard_map.84 = (bf16[128,512]{1,0:T(8,128)(2,1)}, bf16[128,512]{1,0:T(8,128)(2,1)}, bf16[512,1024]{1,0:T(8,128)(2,1)S(1)}, bf16[768,1024]{1,0:T(8,128)(2,1)S(1)}, bf16[384,1024]{1,0:T(8,128)(2,1)S(1)}) custom-call(s32[4]{0:T(128)S(1)} %compare_select_fusion.14.sel_ref, s32[1]{0:T(128)} %bitcast.core_ref, bf16[512,1024]{1,0:T(8,128)(2,1)S(1)} %fusion.9.x_ref, ...), custom_call_target="tpu_custom_call" | custom-call | flops 4000000000 | bytes 8000000 | tf_op jit(solution)/shard_map/pallas_call | solution.py:121
  72.5 2.4 %collective-permute-start.5 = (bf16[768,1024]{1,0:T(8,128)(2,1)S(1)}, bf16[768,1024]{1,0:T(8,128)(2,1)S(1)}, u32[]{:S(2)}, u32[]{:S(2)}) collective-permute-start(bf16[768,1024]{1,0:T(8,128)(2,1)S(1)} %get-tuple-element.12), channel_id=1, source_target_pairs={{0,4},{4,0},{1,5},{5,1},{2,6},{6,2},{3,7},{7,3},{8,12},{12,8},{9,1... | collective-permute-start | bytes 4718600 | tf_op jit(solution)/shard_map/ppermute | solution.py:29
  74.9 3.0 %collective-permute-done.5 = bf16[768,1024]{1,0:T(8,128)(2,1)S(1)} collective-permute-done((bf16[768,1024]{1,0:T(8,128)(2,1)S(1)}, bf16[768,1024]{1,0:T(8,128)(2,1)S(1)}, u32[]{:S(2)}, u32[]{:S(2)}) %collective-permute-start.5) | collective-permute-done | bytes 1572896 | tf_op jit(solution)/shard_map/ppermute | solution.py:29
  77.9 1.4 %add_convert_fusion = bf16[512,1024]{1,0:T(8,128)(2,1)} fusion(bf16[512,1024]{1,0:T(8,128)(2,1)S(1)} %get-tuple-element.13, bf16[768,1024]{1,0:T(8,128)(2,1)S(1)} %collective-permute-done.5), kind=kLoop, calls=%fused_computation.4 | loop fusion | flops 2097152 | bytes 3145728 | tf_op jit(solution)/shard_map/convert_element_type | solution.py:191
  79.3 5.6 %all-to-all-start.3 = ((bf16[4,128,1024]{2,1,0:T(8,128)(2,1)}), bf16[4,128,1024]{2,1,0:T(8,128)(2,1)S(1)}, u32[]{:S(2)}, u32[]{:S(2)}) async-start(bf16[4,128,1024]{2,1,0:T(8,128)(2,1)} %bitcast.11), calls=%async_computation.3 | async-start | bytes 2097152 | tf_op jit(solution)/shard_map/all_to_all | solution.py:192
  85.1 1.9 %collective-permute-start.6 = (bf16[128,1024]{1,0:T(8,128)(2,1)S(1)}, bf16[128,1024]{1,0:T(8,128)(2,1)S(1)}, u32[]{:S(2)}, u32[]{:S(2)}) collective-permute-start(bf16[128,1024]{1,0:T(8,128)(2,1)S(1)} %get-tuple-element.14), channel_id=1, source_target_pairs={{0,8},{4,12},{8,16},{12,20},{16,24},{20,28},{24,32},{28,36},{32,40... | collective-permute-start | bytes 786440 | tf_op jit(solution)/shard_map/ppermute | solution.py:34
  87.0 3.9 %collective-permute-start.7 = (bf16[128,1024]{1,0:T(8,128)(2,1)S(1)}, bf16[128,1024]{1,0:T(8,128)(2,1)S(1)}, u32[]{:S(2)}, u32[]{:S(2)}) collective-permute-start(bf16[128,1024]{1,0:T(8,128)(2,1)S(1)} %get-tuple-element.15), channel_id=1, source_target_pairs={{0,504},{4,508},{8,0},{12,4},{16,8},{20,12},{24,16},{28,20},{32,24... | collective-permute-start | bytes 786440 | tf_op jit(solution)/shard_map/ppermute | solution.py:34
  90.9 4.3 %collective-permute-done.6 = bf16[128,1024]{1,0:T(8,128)(2,1)S(1)} collective-permute-done((bf16[128,1024]{1,0:T(8,128)(2,1)S(1)}, bf16[128,1024]{1,0:T(8,128)(2,1)S(1)}, u32[]{:S(2)}, u32[]{:S(2)}) %collective-permute-start.6) | collective-permute-done | bytes 262176 | tf_op jit(solution)/shard_map/ppermute | solution.py:34
  95.2 2.5 %collective-permute-done.7 = bf16[128,1024]{1,0:T(8,128)(2,1)S(1)} collective-permute-done((bf16[128,1024]{1,0:T(8,128)(2,1)S(1)}, bf16[128,1024]{1,0:T(8,128)(2,1)S(1)}, u32[]{:S(2)}, u32[]{:S(2)}) %collective-permute-start.7) | collective-permute-done | bytes 262176 | tf_op jit(solution)/shard_map/ppermute | solution.py:34
  98.7 4.3 %all-to-all-start.2 = ((bf16[4,128,256]{2,1,0:T(8,128)(2,1)}), bf16[4,128,256]{2,1,0:T(8,128)(2,1)S(1)}, u32[]{:S(2)}, u32[]{:S(2)}) async-start(bf16[4,128,256]{2,1,0:T(8,128)(2,1)} %bitcast.29), calls=%async_computation.2 | async-start | bytes 524288 | tf_op jit(solution)/shard_map/all_to_all | solution.py:205
  103.9 5.8 %all-to-all-done.2 = bf16[4,128,256]{2,1,0:T(8,128)(2,1)S(1)} async-done(((bf16[4,128,256]{2,1,0:T(8,128)(2,1)}), bf16[4,128,256]{2,1,0:T(8,128)(2,1)S(1)}, u32[]{:S(2)}, u32[]{:S(2)}) %all-to-all-start.2) | async-done | bytes 262176 | tf_op jit(solution)/shard_map/all_to_all | solution.py:205
  109.7 10.3 %all-to-all-start.4 = ((bf16[16,8,1024]{2,1,0:T(8,128)(2,1)}), bf16[16,8,1024]{2,1,0:T(8,128)(2,1)S(1)}, u32[]{:S(2)}, u32[]{:S(2)}) async-start(bf16[16,8,1024]{2,1,0:T(8,128)(2,1)} %bitcast.12), calls=%async_computation.4 | async-start | bytes 524288 | tf_op jit(solution)/shard_map/all_to_all | solution.py:194
  120.9 16.4 %all-to-all-done.4 = bf16[16,8,1024]{2,1,0:T(8,128)(2,1)S(1)} async-done(((bf16[16,8,1024]{2,1,0:T(8,128)(2,1)}), bf16[16,8,1024]{2,1,0:T(8,128)(2,1)S(1)}, u32[]{:S(2)}, u32[]{:S(2)}) %all-to-all-start.4) | async-done | bytes 262176 | tf_op jit(solution)/shard_map/all_to_all | solution.py:194
  (40 shorter events, 11.7 us)
Async XLA Ops:
  2.1 34.1 %all-to-all-start = ((bf16[16,8,1024]{2,1,0:T(8,128)(2,1)}), bf16[16,8,1024]{2,1,0:T(8,128)(2,1)S(1)}, u32[]{:S(2)}, u32[]{:S(2)}) async-start(bf16[16,8,1024]{2,1,0:T(8,128)(2,1)} %broadcast_in_dim.54), calls=%async_computation | async-start | bytes 524288 | tf_op jit(solution)/shard_map/all_to_all | solution.py:45
  17.3 24.8 %collective-permute-start = (bf16[128,896]{1,0:T(8,128)(2,1)}, bf16[128,896]{1,0:T(8,128)(2,1)S(1)}, u32[]{:S(2)}, u32[]{:S(2)}) collective-permute-start(bf16[128,896]{1,0:T(8,128)(2,1)} %param.6), channel_id=1, source_target_pairs={{0,504},{4,508},{8,0},{12,4},{16,8},{20,12},{24,16},{28,20},{32,24... | collective-permute-start | bytes 688136 | tf_op jit(solution)/shard_map/ppermute | solution.py:34
  19.3 35.6 %collective-permute-start.1 = (bf16[128,896]{1,0:T(8,128)(2,1)}, bf16[128,896]{1,0:T(8,128)(2,1)S(1)}, u32[]{:S(2)}, u32[]{:S(2)}) collective-permute-start(bf16[128,896]{1,0:T(8,128)(2,1)} %param.6), channel_id=1, source_target_pairs={{0,8},{4,12},{8,16},{12,20},{16,24},{20,28},{24,32},{28,36},{32,40... | collective-permute-start | bytes 688136 | tf_op jit(solution)/shard_map/ppermute | solution.py:34
  23.1 32.5 %collective-permute-start.2 = (bf16[128,896]{1,0:T(8,128)(2,1)}, bf16[128,896]{1,0:T(8,128)(2,1)S(1)}, u32[]{:S(2)}, u32[]{:S(2)}) collective-permute-start(bf16[128,896]{1,0:T(8,128)(2,1)} %param.6), channel_id=1, source_target_pairs={{0,4},{4,0},{1,5},{5,1},{2,6},{6,2},{3,7},{7,3},{8,12},{12,8},{9,1... | collective-permute-start | bytes 688136 | tf_op jit(solution)/shard_map/ppermute | solution.py:29
  25.1 31.3 %collective-permute-start.3 = (bf16[128,896]{1,0:T(8,128)(2,1)}, bf16[128,896]{1,0:T(8,128)(2,1)S(1)}, u32[]{:S(2)}, u32[]{:S(2)}) collective-permute-start(bf16[128,896]{1,0:T(8,128)(2,1)} %param.6), channel_id=1, source_target_pairs={{0,508},{4,8},{8,4},{12,16},{16,12},{20,24},{24,20},{28,32},{32,28... | collective-permute-start | bytes 688136 | tf_op jit(solution)/shard_map/ppermute | solution.py:39
  37.3 15.7 %all-to-all-start.1 = ((bf16[4,128,1024]{2,1,0:T(8,128)(2,1)}), bf16[4,128,1024]{2,1,0:T(8,128)(2,1)S(1)}, u32[]{:S(2)}, u32[]{:S(2)}) async-start(bf16[4,128,1024]{2,1,0:T(8,128)(2,1)} %broadcast_in_dim.56), calls=%async_computation.1 | async-start | bytes 2097152 | tf_op jit(solution)/shard_map/all_to_all | solution.py:45
  42.2 10.8 %copy-start.2 = (bf16[5,128,896]{2,1,0:T(8,128)(2,1)}, bf16[5,128,896]{2,1,0:T(8,128)(2,1)S(1)}, u32[]{:S(2)}) copy-start(bf16[5,128,896]{2,1,0:T(8,128)(2,1)S(1)} %bitcast_dynamic-update-slice_fusion.3) | copy-start | bytes 3440644
  53.0 10.8 %collective-permute-start.4 = (bf16[512,1024]{1,0:T(8,128)(2,1)S(1)}, bf16[512,1024]{1,0:T(8,128)(2,1)S(1)}, u32[]{:S(2)}, u32[]{:S(2)}) collective-permute-start(bf16[512,1024]{1,0:T(8,128)(2,1)S(1)} %bitcast.31), channel_id=1, source_target_pairs={{0,4},{4,0},{1,5},{5,1},{2,6},{6,2},{3,7},{7,3},{8,12},{12,8},{9,1... | collective-permute-start | bytes 3145736 | tf_op jit(solution)/shard_map/ppermute | solution.py:29
  59.9 2.6 %copy-start.3 = (bf16[4,128,896]{2,1,0:T(8,128)(2,1)S(1)}, bf16[4,128,896]{2,1,0:T(8,128)(2,1)}, u32[]{:S(2)}) copy-start(bf16[4,128,896]{2,1,0:T(8,128)(2,1)} %gather_fusion) | copy-start | bytes 2752516
  62.5 1.4 copy-start
  62.5 1.4 copy-start.1
  72.5 5.4 %collective-permute-start.5 = (bf16[768,1024]{1,0:T(8,128)(2,1)S(1)}, bf16[768,1024]{1,0:T(8,128)(2,1)S(1)}, u32[]{:S(2)}, u32[]{:S(2)}) collective-permute-start(bf16[768,1024]{1,0:T(8,128)(2,1)S(1)} %get-tuple-element.12), channel_id=1, source_target_pairs={{0,4},{4,0},{1,5},{5,1},{2,6},{6,2},{3,7},{7,3},{8,12},{12,8},{9,1... | collective-permute-start | bytes 4718600 | tf_op jit(solution)/shard_map/ppermute | solution.py:29
  79.3 19.4 %all-to-all-start.3 = ((bf16[4,128,1024]{2,1,0:T(8,128)(2,1)}), bf16[4,128,1024]{2,1,0:T(8,128)(2,1)S(1)}, u32[]{:S(2)}, u32[]{:S(2)}) async-start(bf16[4,128,1024]{2,1,0:T(8,128)(2,1)} %bitcast.11), calls=%async_computation.3 | async-start | bytes 2097152 | tf_op jit(solution)/shard_map/all_to_all | solution.py:192
  85.1 10.2 %collective-permute-start.6 = (bf16[128,1024]{1,0:T(8,128)(2,1)S(1)}, bf16[128,1024]{1,0:T(8,128)(2,1)S(1)}, u32[]{:S(2)}, u32[]{:S(2)}) collective-permute-start(bf16[128,1024]{1,0:T(8,128)(2,1)S(1)} %get-tuple-element.14), channel_id=1, source_target_pairs={{0,8},{4,12},{8,16},{12,20},{16,24},{20,28},{24,32},{28,36},{32,40... | collective-permute-start | bytes 786440 | tf_op jit(solution)/shard_map/ppermute | solution.py:34
  87.0 10.7 %collective-permute-start.7 = (bf16[128,1024]{1,0:T(8,128)(2,1)S(1)}, bf16[128,1024]{1,0:T(8,128)(2,1)S(1)}, u32[]{:S(2)}, u32[]{:S(2)}) collective-permute-start(bf16[128,1024]{1,0:T(8,128)(2,1)S(1)} %get-tuple-element.15), channel_id=1, source_target_pairs={{0,504},{4,508},{8,0},{12,4},{16,8},{20,12},{24,16},{28,20},{32,24... | collective-permute-start | bytes 786440 | tf_op jit(solution)/shard_map/ppermute | solution.py:34
  98.7 11.0 %all-to-all-start.2 = ((bf16[4,128,256]{2,1,0:T(8,128)(2,1)}), bf16[4,128,256]{2,1,0:T(8,128)(2,1)S(1)}, u32[]{:S(2)}, u32[]{:S(2)}) async-start(bf16[4,128,256]{2,1,0:T(8,128)(2,1)} %bitcast.29), calls=%async_computation.2 | async-start | bytes 524288 | tf_op jit(solution)/shard_map/all_to_all | solution.py:205
  109.7 27.7 %all-to-all-start.4 = ((bf16[16,8,1024]{2,1,0:T(8,128)(2,1)}), bf16[16,8,1024]{2,1,0:T(8,128)(2,1)S(1)}, u32[]{:S(2)}, u32[]{:S(2)}) async-start(bf16[16,8,1024]{2,1,0:T(8,128)(2,1)} %bitcast.12), calls=%async_computation.4 | async-start | bytes 524288 | tf_op jit(solution)/shard_map/all_to_all | solution.py:194

commit v2 on v1

v2 whole, which is shorter than its diff:
```python
import jax
import jax.numpy as jnp
from jax import lax
from jax.experimental import pallas as pl
from jax.experimental.pallas import tpu as pltpu
from jax.sharding import Mesh
from jax.sharding import PartitionSpec as P

HD = 128
SPAN = 64
NROWS = 128
NBR = 2
NY = 4
NZ = 16
NC = 2
NX = 4
DP = ("y", "z", "c")
ENC = 896
OWN = 7
PAD = 8
COLS = 1024
HALF = NY * NZ * PAD
NT = (((1,), (1,)), ((), ()))
TN = (((0,), (0,)), ((), ()))
SLOT_OWN, SLOT_RIGHT, SLOT_LEFT, SLOT_SWAP, SLOT_CROSS = range(5)


def after(value, *earlier):
    return lax.optimization_barrier((value,) + earlier)[0]


def swap_cores(value):
    return lax.ppermute(value, "c", [(0, 1), (1, 0)])


def shifted(value, steps):
    count = NY * NZ * NC
    return lax.ppermute(value, DP, [(i, (i + steps) % count) for i in range(count)])


def crossed(value):
    count = NY * NZ * NC
    return lax.ppermute(
        value, DP, [(i, (i + (1 if i % 2 else -1)) % count) for i in range(count)]
    )


def natural_column(place, core):
    row = place % PAD
    z = place // PAD % NZ
    y = place // (PAD * NZ) % NY
    c = (place // HALF + core) % NC
    return jnp.where(row < OWN, ((y * NZ + z) * NC + c) * OWN + row, -1)


def select_kernel(
    sel_ref, core_ref, own_ref, right_ref, left_ref, other_ref, x_ref, xt_ref, chosen_ref
):
    f32, b16 = jnp.float32, jnp.bfloat16
    sources = (own_ref, right_ref, left_ref, other_ref, other_ref)
    for pair in range(2 * NBR):
        for slot, source in enumerate(sources):
            first = NROWS if slot == SLOT_CROSS else 0

            @pl.when(sel_ref[pair] == slot)
            def _():
                chosen_ref[pair * NROWS : (pair + 1) * NROWS, :] = source[
                    first : first + NROWS, :
                ]

    place = lax.broadcasted_iota(jnp.int32, (1, NC * HALF), 1)
    column = natural_column(place, core_ref[0])
    pick = lax.broadcasted_iota(jnp.int32, (ENC, NC * HALF), 0) == column
    pick = jnp.where(pick, 1.0, 0.0).astype(b16)
    x = jnp.dot(chosen_ref[...], pick, preferred_element_type=f32)
    x_ref[...] = x.astype(b16)
    xt_ref[...] = x.T.astype(b16)


def select(sel, core, own, right, left, other):
    b16 = jnp.bfloat16
    vmem = pl.BlockSpec(memory_space=pltpu.VMEM)
    smem = pl.BlockSpec(memory_space=pltpu.SMEM)
    return pl.pallas_call(
        select_kernel,
        out_shape=(
            jax.ShapeDtypeStruct((4 * NROWS, COLS), b16),
            jax.ShapeDtypeStruct((COLS, 4 * NROWS), b16),
        ),
        in_specs=[smem, smem] + [vmem] * 4,
        out_specs=(vmem,) * 2,
        scratch_shapes=[pltpu.VMEM((4 * NROWS, ENC), b16)],
        compiler_params=pltpu.CompilerParams(vmem_limit_bytes=16 * 2**20),
        cost_estimate=pl.CostEstimate(
            flops=1_000_000_000, bytes_accessed=3_000_000, transcendentals=0
        ),
    )(sel, core, own, right, left, other)


def attention_kernel(
    x_ref, xt_ref, wa_ref, wb_ref, q_ref, g_ref, att_ref, qg_ref, cb_ref, send_ref, kv_ref
):
    f32, b16 = jnp.float32, jnp.bfloat16
    factor = 1.0 / HD**0.5
    kv = jnp.dot(x_ref[:, :HALF], wa_ref[...], preferred_element_type=f32)
    kv = kv + jnp.dot(x_ref[:, HALF:], wb_ref[...], preferred_element_type=f32)
    kv_ref[...] = kv.astype(b16)
    heads = COLS // 2 // HD
    units = [(span, head) for span in range(2) for head in range(heads)]
    rows = [slice(span * SPAN, (span + 1) * SPAN) for span, _ in units]
    span_rows = NBR * NROWS
    krows = [slice(span * span_rows, (span + 1) * span_rows) for span, _ in units]
    kcols = [slice(head * HD, (head + 1) * HD) for _, head in units]
    vcols = [slice((heads + head) * HD, (heads + head + 1) * HD) for _, head in units]
    q = [q_ref[r, c] for r, c in zip(rows, kcols)]
    g = [g_ref[r, c] for r, c in zip(rows, kcols)]
    k = [kv_ref[r, c] for r, c in zip(krows, kcols)]
    v = [kv_ref[r, c] for r, c in zip(krows, vcols)]
    scores = [
        lax.dot_general(a, b, NT, preferred_element_type=f32) * factor for a, b in zip(q, k)
    ]
    dprobs = [lax.dot_general(a, b, NT, preferred_element_type=f32) for a, b in zip(g, v)]
    raised = [jnp.exp(a - jnp.max(a, axis=-1, keepdims=True)) for a in scores]
    probs = [a / jnp.sum(a, axis=-1, keepdims=True) for a in raised]
    probs_b = [a.astype(b16) for a in probs]
    delta = [jnp.sum(a * b, axis=-1, keepdims=True) for a, b in zip(probs, dprobs)]
    dscores = [
        (a * (b - c) * factor).astype(b16) for a, b, c in zip(probs, dprobs, delta)
    ]
    for i in range(len(units)):
        out = jnp.dot(probs_b[i], v[i], preferred_element_type=f32)
        att_ref[rows[i], kcols[i]] = out.astype(b16)
    for i in range(len(units)):
        vgrad = lax.dot_general(probs_b[i], g[i], TN, preferred_element_type=f32)
        cb_ref[krows[i], vcols[i]] = vgrad.astype(b16)
    for i in range(len(units)):
        out = jnp.dot(dscores[i], k[i], preferred_element_type=f32)
        qg_ref[rows[i], kcols[i]] = out.astype(b16)
    for i in range(len(units)):
        kgrad = lax.dot_general(dscores[i], q[i], TN, preferred_element_type=f32)
        cb_ref[krows[i], kcols[i]] = kgrad.astype(b16)
    send_ref[...] = jnp.dot(
        xt_ref[HALF:, :], cb_ref[...], preferred_element_type=f32
    ).astype(b16)


def attend(x, xt, wa, wb, q, g):
    b16 = jnp.bfloat16
    vmem = pl.BlockSpec(memory_space=pltpu.VMEM)
    pairs = jax.ShapeDtypeStruct((4 * NROWS, COLS), b16)
    return pl.pallas_call(
        attention_kernel,
        out_shape=(
            jax.ShapeDtypeStruct(q.shape, b16),
            jax.ShapeDtypeStruct(q.shape, b16),
            pairs,
            jax.ShapeDtypeStruct((HALF, COLS), b16),
        ),
        in_specs=[vmem] * 6,
        out_specs=(vmem,) * 4,
        scratch_shapes=[pltpu.VMEM(pairs.shape, b16)],
        compiler_params=pltpu.CompilerParams(vmem_limit_bytes=20 * 2**20),
        cost_estimate=pl.CostEstimate(
            flops=2_500_000_000, bytes_accessed=6_000_000, transcendentals=131072
        ),
    )(x, xt, wa, wb, q, g)


def share_kernel(
    sel_ref, core_ref, xt_ref, wa_ref, wb_ref, cb_ref, keep_ref, ekeep_ref, esend_ref, acc_ref
):
    f32, b16 = jnp.float32, jnp.bfloat16
    keep_ref[...] = jnp.dot(
        xt_ref[:HALF, :], cb_ref[...], preferred_element_type=f32
    ).astype(b16)
    acc_ref[...] = jnp.zeros_like(acc_ref)
    core = core_ref[0]
    for half, w_ref in ((0, wa_ref), (1, wb_ref)):
        part = lax.dot_general(cb_ref[...], w_ref[...], NT, preferred_element_type=f32)
        c = (core + half) % NC
        for pair in range(2 * NBR):
            for y in range(NY):
                lanes = pl.ds(pl.multiple_of(y * 256 + c * 128, 128), 128)
                acc_ref[sel_ref[pair], :, lanes] += part[
                    pair * NROWS : (pair + 1) * NROWS, y * 128 : (y + 1) * 128
                ]
    for place in range(3):
        ekeep_ref[place * NROWS : (place + 1) * NROWS, :] = acc_ref[place].astype(b16)
    for place in range(2):
        esend_ref[place * NROWS : (place + 1) * NROWS, :] = acc_ref[3 + place].astype(b16)


def share(sel, core, xt, wa, wb, contributions):
    b16 = jnp.bfloat16
    vmem = pl.BlockSpec(memory_space=pltpu.VMEM)
    smem = pl.BlockSpec(memory_space=pltpu.SMEM)
    return pl.pallas_call(
        share_kernel,
        out_shape=(
            jax.ShapeDtypeStruct((HALF, COLS), b16),
            jax.ShapeDtypeStruct((3 * NROWS, COLS), b16),
            jax.ShapeDtypeStruct((2 * NROWS, COLS), b16),
        ),
        in_specs=[smem, smem] + [vmem] * 4,
        out_specs=(vmem,) * 3,
        scratch_shapes=[pltpu.VMEM((5, NROWS, COLS), jnp.float32)],
        compiler_params=pltpu.CompilerParams(vmem_limit_bytes=16 * 2**20),
        cost_estimate=pl.CostEstimate(
            flops=1_600_000_000, bytes_accessed=6_000_000, transcendentals=0
        ),
    )(sel, core, xt, wa, wb, contributions)


def merge_kernel(core_ref, x_ref, keep_ref, got_ref, *out_refs):
    f32 = jnp.float32
    from_cross = (None, core_ref[0] == 0, core_ref[0] == 1)
    for step, out_ref in enumerate(out_refs):
        part = (x_ref[0] + step) % NX
        lanes = pl.ds(pl.multiple_of(part * out_ref.shape[1], 128), out_ref.shape[1])
        swap = got_ref[:NROWS, lanes].astype(f32)
        cross = got_ref[NROWS:, lanes].astype(f32)
        for slot in (SLOT_OWN, SLOT_RIGHT, SLOT_LEFT):
            rows = slice(slot * NROWS, (slot + 1) * NROWS)
            total = keep_ref[rows, lanes].astype(f32)
            if slot == SLOT_OWN:
                total = total + swap
            else:
                total = total + jnp.where(from_cross[slot], cross, 0.0)
            out_ref[rows, :] = total.astype(out_ref.dtype)


def small_call(kernel, scalars, arrays, outs):
    vmem = pl.BlockSpec(memory_space=pltpu.VMEM)
    smem = pl.BlockSpec(memory_space=pltpu.SMEM)
    return pl.pallas_call(
        kernel,
        out_shape=outs,
        in_specs=[smem] * len(scalars) + [vmem] * len(arrays),
        out_specs=(vmem,) * len(outs),
        compiler_params=pltpu.CompilerParams(vmem_limit_bytes=8 * 2**20),
        cost_estimate=pl.CostEstimate(flops=1000, bytes_accessed=1000, transcendentals=0),
    )(*scalars, *arrays)


def summed(refs, rows):
    total = refs[0][rows, :].astype(jnp.float32)
    for ref in refs[1:]:
        total = total + ref[rows, :].astype(jnp.float32)
    return total


def groups_kernel(a_ref, b_ref, c_ref, d_ref, *out_refs):
    for slot, out_ref in enumerate(out_refs):
        rows = slice(slot * NROWS, (slot + 1) * NROWS)
        out_ref[...] = summed((a_ref, b_ref, c_ref, d_ref), rows).astype(out_ref.dtype)


def spread_kernel(w_ref, out_ref):
    f32 = jnp.float32
    half = COLS // 2
    left = [w_ref[r][:1, :].astype(f32) for r in range(OWN)]
    right = [w_ref[r][1:, :].astype(f32) for r in range(OWN)]
    blank = [jnp.zeros((PAD - OWN, half), f32)]
    rows = [jnp.concatenate(side + blank, axis=0) for side in (left, right)]
    rows = jnp.concatenate(rows, axis=1).astype(out_ref.dtype)
    for copy in range(out_ref.shape[0]):
        out_ref[copy] = rows


def reduced_kernel(parts_ref, out_ref):
    total = parts_ref[0].astype(jnp.float32)
    for i in range(1, parts_ref.shape[0]):
        total = total + parts_ref[i].astype(jnp.float32)
    out_ref[...] = total.astype(out_ref.dtype)


def reduced(parts):
    out = jax.ShapeDtypeStruct(parts.shape[1:], parts.dtype)
    return small_call(reduced_kernel, (), (parts,), (out,))[0]


def finish_kernel(own_ref, left_ref, right_ref, out_ref):
    b16 = jnp.bfloat16
    total = summed((own_ref, left_ref, right_ref), slice(None)).astype(b16)
    width, size = out_ref.shape[0], total.shape[1]
    place = lax.broadcasted_iota(jnp.int32, (1, size), 1)
    row, z, c = place % PAD, place // PAD % NZ, place // (PAD * NZ)
    column = jnp.where(row < OWN, (z * NC + c) * OWN + row, -1)
    pick = lax.broadcasted_iota(jnp.int32, (width, size), 0) == column
    pick = jnp.where(pick, 1.0, 0.0).astype(b16)
    out_ref[...] = lax.dot_general(
        pick, total, NT, preferred_element_type=jnp.float32
    ).astype(b16)


def per_device(queries, encodings, kv_weight, pair_list, cotangent):
    f32, b16 = jnp.float32, jnp.bfloat16
    core = lax.axis_index("c")
    me = (lax.axis_index("y") * NZ + lax.axis_index("z")) * NC + core
    count = NY * NZ * NC

    right = shifted(encodings, -2)
    left = shifted(encodings, 2)
    copies = jax.ShapeDtypeStruct((NZ, PAD, COLS), b16)
    (copies,) = small_call(spread_kernel, (), (kv_weight,), (copies,))
    w = lax.all_to_all(copies, "z", 0, 0).reshape(NZ * PAD, COLS)
    copies = jnp.broadcast_to(w[None], (NY,) + w.shape)
    here = after(encodings, copies)
    w = lax.all_to_all(copies, "y", 0, 0).reshape(HALF, COLS)
    other = swap_cores(jnp.concatenate([here, jnp.where(core == 0, right, left)]))

    offset = (pair_list.reshape(-1) - me + count) % count
    near = jnp.where(core == 0, 1, count - 1)
    sel = jnp.where(
        offset == 0,
        SLOT_OWN,
        jnp.where(
            offset == 2,
            SLOT_RIGHT,
            jnp.where(
                offset == count - 2,
                SLOT_LEFT,
                jnp.where(offset == near, SLOT_SWAP, SLOT_CROSS),
            ),
        ),
    ).astype(jnp.int32)
    w, other = lax.optimization_barrier((w, other))
    w_other = swap_cores(w)
    core_id = core.reshape(1)
    x, xt = select(sel, core_id, encodings, right, left, other)

    attended, query_grad, contributions, send = attend(
        x, xt, w, w_other, queries, cotangent
    )
    got = swap_cores(send)
    keep, ekeep, esend = share(sel, core_id, xt, w, w_other, contributions)
    total = (keep.astype(f32) + got.astype(f32)).astype(b16)
    esend = after(esend, total)
    parts = lax.all_to_all(total.reshape(NY, NZ * PAD, COLS), "y", 0, 0)
    got = swap_cores(esend)

    part = jax.ShapeDtypeStruct((3 * NROWS, COLS // NX), b16)
    slot = jax.ShapeDtypeStruct((NROWS, COLS // NX), b16)
    x_id = lax.axis_index("x").reshape(1)
    groups = list(small_call(merge_kernel, (core_id, x_id), (ekeep, got), (part,) * NX))
    for step in range(1, NX):
        groups[step] = lax.ppermute(
            groups[step], "x", [(i, (i + step) % NX) for i in range(NX)]
        )
    total = reduced(after(parts, groups[1], groups[2]))
    groups[0] = after(groups[0], total)
    parts = lax.all_to_all(total.reshape(NZ, PAD, COLS), "z", 0, 0)
    weight_grad = jnp.sum(parts.astype(f32), axis=0)[:OWN].reshape(OWN, 2, COLS // 2)
    own, right, left = small_call(groups_kernel, (), groups, (slot,) * 3)
    from_left = shifted(right, 2)
    from_right = shifted(left, -2)
    flipped = jax.ShapeDtypeStruct((ENC // NX, NROWS), b16)
    (flipped,) = small_call(finish_kernel, (), (own, from_left, from_right), (flipped,))
    encoding_grad = flipped.T
    return attended, query_grad, encoding_grad, weight_grad


def solution(mesh):
    mesh = Mesh(mesh.devices.reshape(NY, NZ, NC, NX), ("y", "z", "c", "x"))
    return jax.shard_map(
        per_device,
        mesh=mesh,
        in_specs=(P(DP, "x"), P(DP, None), P(DP, None, "x"), P(DP, None), P(DP, "x")),
        out_specs=(P(DP, "x"), P(DP, "x"), P(DP, "x"), P(DP, None, "x")),
        check_vma=False,
    )
```

time: 139 us -> 122 us (0.88)
  the two profiles are of different devices: /device:TPU:56 before, /device:TPU:6 now
where the time goes in v2:
time: 122 us; the launch traced here: 120 us
  starting transfers between devices  67.9 us (56%)
  waiting for transfers between devices  35.8 us (29%)
  Pallas kernels  11 us (9%)
  local copies, waits for them, and re-layouts  2.59 us (2%)
  other arithmetic  1.56 us (1%)
    ppermute x4, starting transfers between devices, shifted(): lax.ppermute(value, DP, [(i, (i + steps) % count) for i in range(count)])  18.6 us
    all_to_all x1, starting transfers between devices, per_device(): w = lax.all_to_all(copies, 'z', 0, 0).reshape(NZ * PAD, COLS)  15.2 us
    ppermute x3, waiting for transfers between devices, per_device(): lax.ppermute(groups[step], 'x', [(i, (i + step) % NX) for i in range(NX)])  12 us
    all_to_all x1, waiting for transfers between devices, per_device(): w = lax.all_to_all(copies, 'z', 0, 0).reshape(NZ * PAD, COLS)  11.1 us
    ppermute x3, starting transfers between devices, per_device(): lax.ppermute(groups[step], 'x', [(i, (i + step) % NX) for i in range(NX)])  10.2 us
    ppermute x4, starting transfers between devices, swap_cores(): return lax.ppermute(value, 'c', [(0, 1), (1, 0)])  8.14 us
    all_to_all x1, starting transfers between devices, per_device(): parts = lax.all_to_all(total.reshape(NZ, PAD, COLS), 'z', 0, 0)  7.7 us
    all_to_all x1, waiting for transfers between devices, per_device(): w = lax.all_to_all(copies, 'y', 0, 0).reshape(HALF, COLS)  7.08 us
  transfers between devices with their start and end apart: 15, of which 10 were waited for; matrix products, arithmetic and copies ran while one was open for 1% of the time, Pallas kernels for 5%

profile of v2, /device:TPU:6, one launch (start us, length us, event | category | flops | bytes accessed | tf_op | source)
XLA Modules:
  0.0 119.7 jit_solution(15694148912847612185)
XLA Ops:
  2.1 15.2 %all-to-all-start = ((bf16[16,8,1024]{2,1,0:T(8,128)(2,1)}), bf16[16,8,1024]{2,1,0:T(8,128)(2,1)S(1)}, u32[]{:S(2)}, u32[]{:S(2)}) async-start(bf16[16,8,1024]{2,1,0:T(8,128)(2,1)} %shard_map.84), calls=%async_computation | async-start | bytes 524288 | tf_op jit(solution)/shard_map/all_to_all | solution.py:306
  17.3 3.8 %collective-permute-start.1 = (bf16[128,896]{1,0:T(8,128)(2,1)}, bf16[128,896]{1,0:T(8,128)(2,1)S(1)}, u32[]{:S(2)}, u32[]{:S(2)}) collective-permute-start(bf16[128,896]{1,0:T(8,128)(2,1)} %own_ref.1), channel_id=1, source_target_pairs={{0,8},{4,12},{8,16},{12,20},{16,24},{20,28},{24,32},{28,36},{32,40... | collective-permute-start | bytes 688136 | tf_op jit(solution)/shard_map/ppermute | solution.py:38
  21.1 5.6 %collective-permute-start = (bf16[128,896]{1,0:T(8,128)(2,1)}, bf16[128,896]{1,0:T(8,128)(2,1)S(1)}, u32[]{:S(2)}, u32[]{:S(2)}) collective-permute-start(bf16[128,896]{1,0:T(8,128)(2,1)} %own_ref.1), channel_id=1, source_target_pairs={{0,504},{4,508},{8,0},{12,4},{16,8},{20,12},{24,16},{28,20},{32,24... | collective-permute-start | bytes 688136 | tf_op jit(solution)/shard_map/ppermute | solution.py:38
  26.7 11.1 %all-to-all-done = bf16[16,8,1024]{2,1,0:T(8,128)(2,1)S(1)} async-done(((bf16[16,8,1024]{2,1,0:T(8,128)(2,1)}), bf16[16,8,1024]{2,1,0:T(8,128)(2,1)S(1)}, u32[]{:S(2)}, u32[]{:S(2)}) %all-to-all-start) | async-done | bytes 262176 | tf_op jit(solution)/shard_map/all_to_all | solution.py:306
  39.0 4.6 %all-to-all-start.1 = ((bf16[4,128,1024]{2,1,0:T(8,128)(2,1)}), bf16[4,128,1024]{2,1,0:T(8,128)(2,1)S(1)}, u32[]{:S(2)}, u32[]{:S(2)}) async-start(bf16[4,128,1024]{2,1,0:T(8,128)(2,1)} %broadcast_in_dim.25), calls=%async_computation.1 | async-start | bytes 2097152 | tf_op jit(solution)/shard_map/all_to_all | solution.py:309
  43.7 1.9 %collective-permute-start.2 = (bf16[256,896]{1,0:T(8,128)(2,1)S(1)}, bf16[256,896]{1,0:T(8,128)(2,1)S(1)}, u32[]{:S(2)}, u32[]{:S(2)}) collective-permute-start(bf16[256,896]{1,0:T(8,128)(2,1)S(1)} %pad_maximum_fusion), channel_id=1, source_target_pairs={{0,4},{4,0},{1,5},{5,1},{2,6},{6,2},{3,7},{7,3},{8,12},{12,8},{9,1... | collective-permute-start | bytes 1376264 | tf_op jit(solution)/shard_map/ppermute | solution.py:33
  45.6 1.8 %collective-permute-done.2.other_ref = bf16[256,896]{1,0:T(8,128)(2,1)S(1)} collective-permute-done((bf16[256,896]{1,0:T(8,128)(2,1)S(1)}, bf16[256,896]{1,0:T(8,128)(2,1)S(1)}, u32[]{:S(2)}, u32[]{:S(2)}) %collective-permute-start.2) | collective-permute-done | bytes 458784 | tf_op jit(solution)/shard_map/ppermute | solution.py:33
  47.4 7.1 %all-to-all-done.1 = bf16[4,128,1024]{2,1,0:T(8,128)(2,1)S(1)} async-done(((bf16[4,128,1024]{2,1,0:T(8,128)(2,1)}), bf16[4,128,1024]{2,1,0:T(8,128)(2,1)S(1)}, u32[]{:S(2)}, u32[]{:S(2)}) %all-to-all-start.1) | async-done | bytes 1048608 | tf_op jit(solution)/shard_map/all_to_all | solution.py:309
  54.5 1.9 %collective-permute-start.3 = (bf16[512,1024]{1,0:T(8,128)(2,1)S(1)}, bf16[512,1024]{1,0:T(8,128)(2,1)S(1)}, u32[]{:S(2)}, u32[]{:S(2)}) collective-permute-start(bf16[512,1024]{1,0:T(8,128)(2,1)S(1)} %bitcast.8), channel_id=1, source_target_pairs={{0,4},{4,0},{1,5},{5,1},{2,6},{6,2},{3,7},{7,3},{8,12},{12,8},{9,1... | collective-permute-start | bytes 3145736 | tf_op jit(solution)/shard_map/ppermute | solution.py:33
  56.6 2.1 %shard_map.85 = (bf16[512,1024]{1,0:T(8,128)(2,1)S(1)}, bf16[1024,512]{1,0:T(8,128)(2,1)S(1)}) custom-call(s32[4]{0:T(128)S(1)} %compare_select_fusion.5.sel_ref, s32[1]{0:T(128)} %bitcast.core_ref, bf16[128,896]{1,0:T(8,128)(2,1)S(1)} %copy-done, bf16[128,896]{1,0:T(8,128)(2,1)S(1)} %collective-permute-done.right_ref, ...), custom_call_target="tpu_custom_call" | custom-call | flops 1000000000 | bytes 3000000 | tf_op jit(solution)/shard_map/pallas_call | solution.py:84
  59.1 3.4 %shard_map.86 = (bf16[128,512]{1,0:T(8,128)(2,1)}, bf16[128,512]{1,0:T(8,128)(2,1)}, bf16[512,1024]{1,0:T(8,128)(2,1)S(1)}, bf16[512,1024]{1,0:T(8,128)(2,1)S(1)}) custom-call(bf16[512,1024]{1,0:T(8,128)(2,1)S(1)} %get-tuple-element.28.x_ref, bf16[1024,512]{1,0:T(8,128)(2,1)S(1)} %get-tuple-element.29.xt_ref, bf16[512,1024]{1,0:T(8,128)(2,1)S(1)} %bitcast.9, ...), custom_call_target="tpu_custom_call" | custom-call | flops 2500000000 | bytes 6000000 | tf_op jit(solution)/shard_map/pallas_call | solution.py:151
  62.5 2.1 %collective-permute-start.4 = (bf16[512,1024]{1,0:T(8,128)(2,1)S(1)}, bf16[512,1024]{1,0:T(8,128)(2,1)S(1)}, u32[]{:S(2)}, u32[]{:S(2)}) collective-permute-start(bf16[512,1024]{1,0:T(8,128)(2,1)S(1)} %get-tuple-element.37), channel_id=1, source_target_pairs={{0,4},{4,0},{1,5},{5,1},{2,6},{6,2},{3,7},{7,3},{8,12},{12,8},{9,1... | collective-permute-start | bytes 3145736 | tf_op jit(solution)/shard_map/ppermute | solution.py:33
  64.5 2.8 %shard_map.87 = (bf16[512,1024]{1,0:T(8,128)(2,1)S(1)}, bf16[384,1024]{1,0:T(8,128)(2,1)S(1)}, bf16[256,1024]{1,0:T(8,128)(2,1)S(1)}) custom-call(s32[4]{0:T(128)S(1)} %compare_select_fusion.5.sel_ref, s32[1]{0:T(128)} %bitcast.core_ref, bf16[1024,512]{1,0:T(8,128)(2,1)S(1)} %get-tuple-element.29.xt_ref, bf16[512,1024]{1,0:T(8,128)(2,1)S(1)} %bitcast.10, ...), custom_call_target="tpu_custom_call" | custom-call | flops 1600000000 | bytes 6000000 | tf_op jit(solution)/shard_map/pallas_call | solution.py:197
  68.8 3.5 %all-to-all-start.2 = ((bf16[4,128,1024]{2,1,0:T(8,128)(2,1)}), bf16[4,128,1024]{2,1,0:T(8,128)(2,1)S(1)}, u32[]{:S(2)}, u32[]{:S(2)}) async-start(bf16[4,128,1024]{2,1,0:T(8,128)(2,1)} %bitcast.4), calls=%async_computation.2 | async-start | bytes 2097152 | tf_op jit(solution)/shard_map/all_to_all | solution.py:339
  72.3 2.3 %collective-permute-start.5 = (bf16[256,1024]{1,0:T(8,128)(2,1)S(1)}, bf16[256,1024]{1,0:T(8,128)(2,1)S(1)}, u32[]{:S(2)}, u32[]{:S(2)}) collective-permute-start(bf16[256,1024]{1,0:T(8,128)(2,1)S(1)} %get-tuple-element.38), channel_id=1, source_target_pairs={{0,4},{4,0},{1,5},{5,1},{2,6},{6,2},{3,7},{7,3},{8,12},{12,8},{9,1... | collective-permute-start | bytes 1572872 | tf_op jit(solution)/shard_map/ppermute | solution.py:33
  76.3 2.4 %collective-permute-start.6 = (bf16[384,256]{1,0:T(8,128)(2,1)S(1)}, bf16[384,256]{1,0:T(8,128)(2,1)S(1)}, u32[]{:S(2)}, u32[]{:S(2)}) collective-permute-start(bf16[384,256]{1,0:T(8,128)(2,1)S(1)} %get-tuple-element.40), channel_id=1, source_target_pairs={{0,1},{1,2},{2,3},{3,0},{4,5},{5,6},{6,7},{7,4},{8,9},{9,10},{10,1... | collective-permute-start | bytes 589832 | tf_op jit(solution)/shard_map/ppermute | solution.py:347
  78.7 4.3 %collective-permute-start.7 = (bf16[384,256]{1,0:T(8,128)(2,1)S(1)}, bf16[384,256]{1,0:T(8,128)(2,1)S(1)}, u32[]{:S(2)}, u32[]{:S(2)}) collective-permute-start(bf16[384,256]{1,0:T(8,128)(2,1)S(1)} %get-tuple-element.41), channel_id=1, source_target_pairs={{0,2},{1,3},{2,0},{3,1},{4,6},{5,7},{6,4},{7,5},{8,10},{9,11},{10,... | collective-permute-start | bytes 589832 | tf_op jit(solution)/shard_map/ppermute | solution.py:347
  83.1 2.9 %collective-permute-done.6.b_ref = bf16[384,256]{1,0:T(8,128)(2,1)S(1)} collective-permute-done((bf16[384,256]{1,0:T(8,128)(2,1)S(1)}, bf16[384,256]{1,0:T(8,128)(2,1)S(1)}, u32[]{:S(2)}, u32[]{:S(2)}) %collective-permute-start.6) | collective-permute-done | bytes 196640 | tf_op jit(solution)/shard_map/ppermute | solution.py:347
  85.9 3.1 %collective-permute-done.7.c_ref = bf16[384,256]{1,0:T(8,128)(2,1)S(1)} collective-permute-done((bf16[384,256]{1,0:T(8,128)(2,1)S(1)}, bf16[384,256]{1,0:T(8,128)(2,1)S(1)}, u32[]{:S(2)}, u32[]{:S(2)}) %collective-permute-start.7) | collective-permute-done | bytes 196640 | tf_op jit(solution)/shard_map/ppermute | solution.py:347
  89.8 7.7 %all-to-all-start.3 = ((bf16[16,8,1024]{2,1,0:T(8,128)(2,1)}), bf16[16,8,1024]{2,1,0:T(8,128)(2,1)S(1)}, u32[]{:S(2)}, u32[]{:S(2)}) async-start(bf16[16,8,1024]{2,1,0:T(8,128)(2,1)} %bitcast.6), calls=%async_computation.3 | async-start | bytes 524288 | tf_op jit(solution)/shard_map/all_to_all | solution.py:352
  97.5 3.5 %collective-permute-start.8 = (bf16[384,256]{1,0:T(8,128)(2,1)S(1)}, bf16[384,256]{1,0:T(8,128)(2,1)S(1)}, u32[]{:S(2)}, u32[]{:S(2)}) collective-permute-start(bf16[384,256]{1,0:T(8,128)(2,1)S(1)} %get-tuple-element.44), channel_id=1, source_target_pairs={{0,3},{1,0},{2,1},{3,2},{4,7},{5,4},{6,5},{7,6},{8,11},{9,8},{10,9... | collective-permute-start | bytes 589832 | tf_op jit(solution)/shard_map/ppermute | solution.py:347
  101.0 6.0 %collective-permute-done.8.d_ref = bf16[384,256]{1,0:T(8,128)(2,1)S(1)} collective-permute-done((bf16[384,256]{1,0:T(8,128)(2,1)S(1)}, bf16[384,256]{1,0:T(8,128)(2,1)S(1)}, u32[]{:S(2)}, u32[]{:S(2)}) %collective-permute-start.8) | collective-permute-done | bytes 196640 | tf_op jit(solution)/shard_map/ppermute | solution.py:347
  107.2 3.5 %collective-permute-start.9 = (bf16[128,256]{1,0:T(8,128)(2,1)S(1)}, bf16[128,256]{1,0:T(8,128)(2,1)S(1)}, u32[]{:S(2)}, u32[]{:S(2)}) collective-permute-start(bf16[128,256]{1,0:T(8,128)(2,1)S(1)} %get-tuple-element.46), channel_id=1, source_target_pairs={{0,8},{4,12},{8,16},{12,20},{16,24},{20,28},{24,32},{28,36},{32,40... | collective-permute-start | bytes 196616 | tf_op jit(solution)/shard_map/ppermute | solution.py:38
  110.7 5.6 %collective-permute-start.10 = (bf16[128,256]{1,0:T(8,128)(2,1)S(1)}, bf16[128,256]{1,0:T(8,128)(2,1)S(1)}, u32[]{:S(2)}, u32[]{:S(2)}) collective-permute-start(bf16[128,256]{1,0:T(8,128)(2,1)S(1)} %get-tuple-element.47), channel_id=1, source_target_pairs={{0,504},{4,508},{8,0},{12,4},{16,8},{20,12},{24,16},{28,20},{32,24... | collective-permute-start | bytes 196616 | tf_op jit(solution)/shard_map/ppermute | solution.py:38
  (33 shorter events, 10.6 us)
Async XLA Ops:
  0.6 0.7 copy-start.1
  2.1 35.8 %all-to-all-start = ((bf16[16,8,1024]{2,1,0:T(8,128)(2,1)}), bf16[16,8,1024]{2,1,0:T(8,128)(2,1)S(1)}, u32[]{:S(2)}, u32[]{:S(2)}) async-start(bf16[16,8,1024]{2,1,0:T(8,128)(2,1)} %shard_map.84), calls=%async_computation | async-start | bytes 524288 | tf_op jit(solution)/shard_map/all_to_all | solution.py:306
  17.3 26.3 %collective-permute-start.1 = (bf16[128,896]{1,0:T(8,128)(2,1)}, bf16[128,896]{1,0:T(8,128)(2,1)S(1)}, u32[]{:S(2)}, u32[]{:S(2)}) collective-permute-start(bf16[128,896]{1,0:T(8,128)(2,1)} %own_ref.1), channel_id=1, source_target_pairs={{0,8},{4,12},{8,16},{12,20},{16,24},{20,28},{24,32},{28,36},{32,40... | collective-permute-start | bytes 688136 | tf_op jit(solution)/shard_map/ppermute | solution.py:38
  21.1 22.5 %collective-permute-start = (bf16[128,896]{1,0:T(8,128)(2,1)}, bf16[128,896]{1,0:T(8,128)(2,1)S(1)}, u32[]{:S(2)}, u32[]{:S(2)}) collective-permute-start(bf16[128,896]{1,0:T(8,128)(2,1)} %own_ref.1), channel_id=1, source_target_pairs={{0,504},{4,508},{8,0},{12,4},{16,8},{20,12},{24,16},{28,20},{32,24... | collective-permute-start | bytes 688136 | tf_op jit(solution)/shard_map/ppermute | solution.py:38
  39.0 4.6 %copy-start = (bf16[128,896]{1,0:T(8,128)(2,1)S(1)}, bf16[128,896]{1,0:T(8,128)(2,1)}, u32[]{:S(2)}) copy-start(bf16[128,896]{1,0:T(8,128)(2,1)} %own_ref.1) | copy-start | bytes 688132
  39.0 15.5 %all-to-all-start.1 = ((bf16[4,128,1024]{2,1,0:T(8,128)(2,1)}), bf16[4,128,1024]{2,1,0:T(8,128)(2,1)S(1)}, u32[]{:S(2)}, u32[]{:S(2)}) async-start(bf16[4,128,1024]{2,1,0:T(8,128)(2,1)} %broadcast_in_dim.25), calls=%async_computation.1 | async-start | bytes 2097152 | tf_op jit(solution)/shard_map/all_to_all | solution.py:309
  43.6 12.8 %copy-start.4 = (s32[2,2]{1,0:T(2,128)S(1)}, s32[2,2]{1,0:T(2,128)}, u32[]{:S(2)}) copy-start(s32[2,2]{1,0:T(2,128)} %param.8) | copy-start | bytes 52
  43.7 3.7 %collective-permute-start.2 = (bf16[256,896]{1,0:T(8,128)(2,1)S(1)}, bf16[256,896]{1,0:T(8,128)(2,1)S(1)}, u32[]{:S(2)}, u32[]{:S(2)}) collective-permute-start(bf16[256,896]{1,0:T(8,128)(2,1)S(1)} %pad_maximum_fusion), channel_id=1, source_target_pairs={{0,4},{4,0},{1,5},{5,1},{2,6},{6,2},{3,7},{7,3},{8,12},{12,8},{9,1... | collective-permute-start | bytes 1376264 | tf_op jit(solution)/shard_map/ppermute | solution.py:33
  54.5 4.5 %collective-permute-start.3 = (bf16[512,1024]{1,0:T(8,128)(2,1)S(1)}, bf16[512,1024]{1,0:T(8,128)(2,1)S(1)}, u32[]{:S(2)}, u32[]{:S(2)}) collective-permute-start(bf16[512,1024]{1,0:T(8,128)(2,1)S(1)} %bitcast.8), channel_id=1, source_target_pairs={{0,4},{4,0},{1,5},{5,1},{2,6},{6,2},{3,7},{7,3},{8,12},{12,8},{9,1... | collective-permute-start | bytes 3145736 | tf_op jit(solution)/shard_map/ppermute | solution.py:33
  56.6 2.5 %copy-start.2 = (bf16[128,512]{1,0:T(8,128)(2,1)S(1)}, bf16[128,512]{1,0:T(8,128)(2,1)}, u32[]{:S(2)}) copy-start(bf16[128,512]{1,0:T(8,128)(2,1)} %q_ref.1) | copy-start | bytes 393220
  56.6 2.5 %copy-start.3 = (bf16[128,512]{1,0:T(8,128)(2,1)S(1)}, bf16[128,512]{1,0:T(8,128)(2,1)}, u32[]{:S(2)}) copy-start(bf16[128,512]{1,0:T(8,128)(2,1)} %g_ref.1) | copy-start | bytes 393220
  62.5 4.9 %collective-permute-start.4 = (bf16[512,1024]{1,0:T(8,128)(2,1)S(1)}, bf16[512,1024]{1,0:T(8,128)(2,1)S(1)}, u32[]{:S(2)}, u32[]{:S(2)}) collective-permute-start(bf16[512,1024]{1,0:T(8,128)(2,1)S(1)} %get-tuple-element.37), channel_id=1, source_target_pairs={{0,4},{4,0},{1,5},{5,1},{2,6},{6,2},{3,7},{7,3},{8,12},{12,8},{9,1... | collective-permute-start | bytes 3145736 | tf_op jit(solution)/shard_map/ppermute | solution.py:33
  68.8 20.2 %all-to-all-start.2 = ((bf16[4,128,1024]{2,1,0:T(8,128)(2,1)}), bf16[4,128,1024]{2,1,0:T(8,128)(2,1)S(1)}, u32[]{:S(2)}, u32[]{:S(2)}) async-start(bf16[4,128,1024]{2,1,0:T(8,128)(2,1)} %bitcast.4), calls=%async_computation.2 | async-start | bytes 2097152 | tf_op jit(solution)/shard_map/all_to_all | solution.py:339
  72.3 3.8 %collective-permute-start.5 = (bf16[256,1024]{1,0:T(8,128)(2,1)S(1)}, bf16[256,1024]{1,0:T(8,128)(2,1)S(1)}, u32[]{:S(2)}, u32[]{:S(2)}) collective-permute-start(bf16[256,1024]{1,0:T(8,128)(2,1)S(1)} %get-tuple-element.38), channel_id=1, source_target_pairs={{0,4},{4,0},{1,5},{5,1},{2,6},{6,2},{3,7},{7,3},{8,12},{12,8},{9,1... | collective-permute-start | bytes 1572872 | tf_op jit(solution)/shard_map/ppermute | solution.py:33
  76.3 9.6 %collective-permute-start.6 = (bf16[384,256]{1,0:T(8,128)(2,1)S(1)}, bf16[384,256]{1,0:T(8,128)(2,1)S(1)}, u32[]{:S(2)}, u32[]{:S(2)}) collective-permute-start(bf16[384,256]{1,0:T(8,128)(2,1)S(1)} %get-tuple-element.40), channel_id=1, source_target_pairs={{0,1},{1,2},{2,3},{3,0},{4,5},{5,6},{6,7},{7,4},{8,9},{9,10},{10,1... | collective-permute-start | bytes 589832 | tf_op jit(solution)/shard_map/ppermute | solution.py:347
  78.7 10.3 %collective-permute-start.7 = (bf16[384,256]{1,0:T(8,128)(2,1)S(1)}, bf16[384,256]{1,0:T(8,128)(2,1)S(1)}, u32[]{:S(2)}, u32[]{:S(2)}) collective-permute-start(bf16[384,256]{1,0:T(8,128)(2,1)S(1)} %get-tuple-element.41), channel_id=1, source_target_pairs={{0,2},{1,3},{2,0},{3,1},{4,6},{5,7},{6,4},{7,5},{8,10},{9,11},{10,... | collective-permute-start | bytes 589832 | tf_op jit(solution)/shard_map/ppermute | solution.py:347
  89.8 29.2 %all-to-all-start.3 = ((bf16[16,8,1024]{2,1,0:T(8,128)(2,1)}), bf16[16,8,1024]{2,1,0:T(8,128)(2,1)S(1)}, u32[]{:S(2)}, u32[]{:S(2)}) async-start(bf16[16,8,1024]{2,1,0:T(8,128)(2,1)} %bitcast.6), calls=%async_computation.3 | async-start | bytes 524288 | tf_op jit(solution)/shard_map/all_to_all | solution.py:352
  97.5 9.5 %collective-permute-start.8 = (bf16[384,256]{1,0:T(8,128)(2,1)S(1)}, bf16[384,256]{1,0:T(8,128)(2,1)S(1)}, u32[]{:S(2)}, u32[]{:S(2)}) collective-permute-start(bf16[384,256]{1,0:T(8,128)(2,1)S(1)} %get-tuple-element.44), channel_id=1, source_target_pairs={{0,3},{1,0},{2,1},{3,2},{4,7},{5,4},{6,5},{7,6},{8,11},{9,8},{10,9... | collective-permute-start | bytes 589832 | tf_op jit(solution)/shard_map/ppermute | solution.py:347
  107.2 9.8 %collective-permute-start.9 = (bf16[128,256]{1,0:T(8,128)(2,1)S(1)}, bf16[128,256]{1,0:T(8,128)(2,1)S(1)}, u32[]{:S(2)}, u32[]{:S(2)}) collective-permute-start(bf16[128,256]{1,0:T(8,128)(2,1)S(1)} %get-tuple-element.46), channel_id=1, source_target_pairs={{0,8},{4,12},{8,16},{12,20},{16,24},{20,28},{24,32},{28,36},{32,40... | collective-permute-start | bytes 196616 | tf_op jit(solution)/shard_map/ppermute | solution.py:38
  110.7 7.5 %collective-permute-start.10 = (bf16[128,256]{1,0:T(8,128)(2,1)S(1)}, bf16[128,256]{1,0:T(8,128)(2,1)S(1)}, u32[]{:S(2)}, u32[]{:S(2)}) collective-permute-start(bf16[128,256]{1,0:T(8,128)(2,1)S(1)} %get-tuple-element.47), channel_id=1, source_target_pairs={{0,504},{4,508},{8,0},{12,4},{16,8},{20,12},{24,16},{28,20},{32,24... | collective-permute-start | bytes 196616 | tf_op jit(solution)/shard_map/ppermute | solution.py:38

commit v3 on v2

--- a/solution.py
+++ b/solution.py
@@ -97,13 +97,16 @@
     )(sel, core, own, right, left, other)
 
 
+def project_kernel(x_ref, w_ref, kv_ref):
+    kv_ref[...] = jnp.dot(x_ref[:, :HALF], w_ref[...], preferred_element_type=jnp.float32)
+
+
 def attention_kernel(
-    x_ref, xt_ref, wa_ref, wb_ref, q_ref, g_ref, att_ref, qg_ref, cb_ref, send_ref, kv_ref
+    x_ref, xt_ref, part_ref, wb_ref, q_ref, g_ref, att_ref, qg_ref, cb_ref, send_ref, kv_ref
 ):
     f32, b16 = jnp.float32, jnp.bfloat16
     factor = 1.0 / HD**0.5
-    kv = jnp.dot(x_ref[:, :HALF], wa_ref[...], preferred_element_type=f32)
-    kv = kv + jnp.dot(x_ref[:, HALF:], wb_ref[...], preferred_element_type=f32)
+    kv = part_ref[...] + jnp.dot(x_ref[:, HALF:], wb_ref[...], preferred_element_type=f32)
     kv_ref[...] = kv.astype(b16)
     heads = COLS // 2 // HD
     units = [(span, head) for span in range(2) for head in range(heads)]
@@ -144,7 +147,7 @@
     ).astype(b16)
 
 
-def attend(x, xt, wa, wb, q, g):
+def attend(x, xt, part, wb, q, g):
     b16 = jnp.bfloat16
     vmem = pl.BlockSpec(memory_space=pltpu.VMEM)
     pairs = jax.ShapeDtypeStruct((4 * NROWS, COLS), b16)
@@ -163,7 +166,7 @@
         cost_estimate=pl.CostEstimate(
             flops=2_500_000_000, bytes_accessed=6_000_000, transcendentals=131072
         ),
-    )(x, xt, wa, wb, q, g)
+    )(x, xt, part, wb, q, g)
 
 
 def share_kernel(
@@ -279,6 +282,43 @@
     return small_call(reduced_kernel, (), (parts,), (out,))[0]
 
 
+def add_kernel(keep_ref, got_ref, out_ref, sum_ref, sems):
+    copies = []
+    for part in range(NY):
+        size = sum_ref.shape[1]
+        rows = slice(part * size, (part + 1) * size)
+        total = keep_ref[rows, :].astype(jnp.float32) + got_ref[rows, :].astype(jnp.float32)
+        sum_ref[part] = total.astype(sum_ref.dtype)
+        copies.append(pltpu.make_async_copy(sum_ref.at[part], out_ref.at[part], sems.at[part]))
+        copies[-1].start()
+    for copy in copies:
+        copy.wait()
+
+
+def copies_kernel(block_ref, out_ref, sems):
+    copies = [
+        pltpu.make_async_copy(block_ref, out_ref.at[i], sems.at[i])
+        for i in range(out_ref.shape[0])
+    ]
+    for copy in copies:
+        copy.start()
+    for copy in copies:
+        copy.wait()
+
+
+def streamed(kernel, arrays, out, *scratch):
+    vmem = pl.BlockSpec(memory_space=pltpu.VMEM)
+    return pl.pallas_call(
+        kernel,
+        out_shape=out,
+        in_specs=[vmem] * len(arrays),
+        out_specs=pl.BlockSpec(memory_space=pl.ANY),
+        scratch_shapes=list(scratch) + [pltpu.SemaphoreType.DMA((out.shape[0],))],
+        compiler_params=pltpu.CompilerParams(vmem_limit_bytes=8 * 2**20),
+        cost_estimate=pl.CostEstimate(flops=1000, bytes_accessed=1000, transcendentals=0),
+    )(*arrays)
+
+
 def finish_kernel(own_ref, left_ref, right_ref, out_ref):
     b16 = jnp.bfloat16
     total = summed((own_ref, left_ref, right_ref), slice(None)).astype(b16)
@@ -304,7 +344,8 @@
     copies = jax.ShapeDtypeStruct((NZ, PAD, COLS), b16)
     (copies,) = small_call(spread_kernel, (), (kv_weight,), (copies,))
     w = lax.all_to_all(copies, "z", 0, 0).reshape(NZ * PAD, COLS)
-    copies = jnp.broadcast_to(w[None], (NY,) + w.shape)
+    copies = jax.ShapeDtypeStruct((NY,) + w.shape, b16)
+    copies = streamed(copies_kernel, (w,), copies)
     here = after(encodings, copies)
     w = lax.all_to_all(copies, "y", 0, 0).reshape(HALF, COLS)
     other = swap_cores(jnp.concatenate([here, jnp.where(core == 0, right, left)]))
@@ -324,30 +365,32 @@
             ),
         ),
     ).astype(jnp.int32)
-    w, other = lax.optimization_barrier((w, other))
-    w_other = swap_cores(w)
     core_id = core.reshape(1)
     x, xt = select(sel, core_id, encodings, right, left, other)
+    w_other = swap_cores(after(w, x))
+    part = jax.ShapeDtypeStruct((4 * NROWS, COLS), f32)
+    (part,) = small_call(project_kernel, (), (x, w), (part,))
 
     attended, query_grad, contributions, send = attend(
-        x, xt, w, w_other, queries, cotangent
+        x, xt, part, w_other, queries, cotangent
     )
     got = swap_cores(send)
     keep, ekeep, esend = share(sel, core_id, xt, w, w_other, contributions)
-    total = (keep.astype(f32) + got.astype(f32)).astype(b16)
+    total = jax.ShapeDtypeStruct((NY, HALF // NY, COLS), b16)
+    total = streamed(add_kernel, (keep, got), total, pltpu.VMEM(total.shape, b16))
     esend = after(esend, total)
-    parts = lax.all_to_all(total.reshape(NY, NZ * PAD, COLS), "y", 0, 0)
+    parts = lax.all_to_all(total, "y", 0, 0)
     got = swap_cores(esend)
 
     part = jax.ShapeDtypeStruct((3 * NROWS, COLS // NX), b16)
     slot = jax.ShapeDtypeStruct((NROWS, COLS // NX), b16)
     x_id = lax.axis_index("x").reshape(1)
     groups = list(small_call(merge_kernel, (core_id, x_id), (ekeep, got), (part,) * NX))
-    for step in range(1, NX):
+    for step in (2, 1, 3):
         groups[step] = lax.ppermute(
             groups[step], "x", [(i, (i + step) % NX) for i in range(NX)]
         )
-    total = reduced(after(parts, groups[1], groups[2]))
+    total = reduced(after(parts, groups[1], groups[3]))
     groups[0] = after(groups[0], total)
     parts = lax.all_to_all(total.reshape(NZ, PAD, COLS), "z", 0, 0)
     weight_grad = jnp.sum(parts.astype(f32), axis=0)[:OWN].reshape(OWN, 2, COLS // 2)

time: 122 us -> 119 us (0.975); the launches traced: 120 us -> 118 us
  Pallas kernels: 11 us -> 13.3 us
  other arithmetic: 1.56 us -> 0.13 us
  waiting for transfers between devices: 35.8 us -> 34.5 us
    all_to_all x1, waiting for transfers between devices: 7.08 us -> 3.97 us  [per_device(): w = lax.all_to_all(copies, 'y', 0, 0).reshape(HALF, COLS)]
    pallas_call x0 -> x2, Pallas kernels: none -> 2.1 us  [streamed(): pl.pallas_call(kernel, out_shape=out, in_specs=[vmem] * len(arrays), out_...]
    convert_element_type x1 -> x0, other arithmetic: 1.43 us -> none  [per_device(): total = (keep.astype(f32) + got.astype(f32)).astype(b16)]
    ppermute x4, waiting for transfers between devices: 3.69 us -> 5.09 us  [swap_cores(): return lax.ppermute(value, 'c', [(0, 1), (1, 0)])]
    pallas_call x5 -> x6, Pallas kernels: 2.69 us -> 3.42 us  [small_call(): pl.pallas_call(kernel, out_shape=outs, in_specs=[smem] * len(scalars) + [...]
  transfers between devices with their start and end apart: 15 -> 15, of which waited for: 10 -> 10; matrix products, arithmetic and copies ran while one was open for 1% -> 0% of each run, Pallas kernels for 5% -> 7%
where the time goes in v3:
time: 119 us; the launch traced here: 118 us
  starting transfers between devices  66.9 us (56%)
  waiting for transfers between devices  34.5 us (29%)
  Pallas kernels  13.3 us (11%)
  local copies, waits for them, and re-layouts  2.45 us (2%)
    ppermute x4, starting transfers between devices, shifted(): lax.ppermute(value, DP, [(i, (i + steps) % count) for i in range(count)])  18.8 us
    all_to_all x1, starting transfers between devices, per_device(): w = lax.all_to_all(copies, 'z', 0, 0).reshape(NZ * PAD, COLS)  15.2 us
    ppermute x3, waiting for transfers between devices, per_device(): lax.ppermute(groups[step], 'x', [(i, (i + step) % NX) for i in range(NX)])  12.5 us
    all_to_all x1, waiting for transfers between devices, per_device(): w = lax.all_to_all(copies, 'z', 0, 0).reshape(NZ * PAD, COLS)  11 us
    ppermute x3, starting transfers between devices, per_device(): lax.ppermute(groups[step], 'x', [(i, (i + step) % NX) for i in range(NX)])  8.98 us
    ppermute x4, starting transfers between devices, swap_cores(): return lax.ppermute(value, 'c', [(0, 1), (1, 0)])  8.26 us
    all_to_all x1, starting transfers between devices, per_device(): parts = lax.all_to_all(total.reshape(NZ, PAD, COLS), 'z', 0, 0)  7.69 us
    ppermute x4, waiting for transfers between devices, swap_cores(): return lax.ppermute(value, 'c', [(0, 1), (1, 0)])  5.09 us
  transfers between devices with their start and end apart: 15, of which 10 were waited for; matrix products, arithmetic and copies ran while one was open for 0% of the time, Pallas kernels for 7%

profile of v3, /device:TPU:6, one launch (start us, length us, event | category | flops | bytes accessed | tf_op | source)
XLA Modules:
  0.0 118.2 jit_solution(2874112593243899173)
XLA Ops:
  2.1 15.2 %all-to-all-start = ((bf16[16,8,1024]{2,1,0:T(8,128)(2,1)}), bf16[16,8,1024]{2,1,0:T(8,128)(2,1)S(1)}, u32[]{:S(2)}, u32[]{:S(2)}) async-start(bf16[16,8,1024]{2,1,0:T(8,128)(2,1)} %shard_map.84), calls=%async_computation | async-start | bytes 524288 | tf_op jit(solution)/shard_map/all_to_all | solution.py:346
  17.3 4.0 %collective-permute-start.1 = (bf16[128,896]{1,0:T(8,128)(2,1)}, bf16[128,896]{1,0:T(8,128)(2,1)S(1)}, u32[]{:S(2)}, u32[]{:S(2)}) collective-permute-start(bf16[128,896]{1,0:T(8,128)(2,1)} %own_ref.1), channel_id=1, source_target_pairs={{0,8},{4,12},{8,16},{12,20},{16,24},{20,28},{24,32},{28,36},{32,40... | collective-permute-start | bytes 688136 | tf_op jit(solution)/shard_map/ppermute | solution.py:38
  21.3 5.6 %collective-permute-start = (bf16[128,896]{1,0:T(8,128)(2,1)}, bf16[128,896]{1,0:T(8,128)(2,1)S(1)}, u32[]{:S(2)}, u32[]{:S(2)}) collective-permute-start(bf16[128,896]{1,0:T(8,128)(2,1)} %own_ref.1), channel_id=1, source_target_pairs={{0,504},{4,508},{8,0},{12,4},{16,8},{20,12},{24,16},{28,20},{32,24... | collective-permute-start | bytes 688136 | tf_op jit(solution)/shard_map/ppermute | solution.py:38
  26.9 11.0 %all-to-all-done = bf16[16,8,1024]{2,1,0:T(8,128)(2,1)S(1)} async-done(((bf16[16,8,1024]{2,1,0:T(8,128)(2,1)}), bf16[16,8,1024]{2,1,0:T(8,128)(2,1)S(1)}, u32[]{:S(2)}, u32[]{:S(2)}) %all-to-all-start) | async-done | bytes 262176 | tf_op jit(solution)/shard_map/all_to_all | solution.py:346
  38.9 4.5 %all-to-all-start.1 = ((bf16[4,128,1024]{2,1,0:T(8,128)(2,1)}), bf16[4,128,1024]{2,1,0:T(8,128)(2,1)S(1)}, u32[]{:S(2)}, u32[]{:S(2)}) async-start(bf16[4,128,1024]{2,1,0:T(8,128)(2,1)} %shard_map.85), calls=%async_computation.1 | async-start | bytes 2097152 | tf_op jit(solution)/shard_map/all_to_all | solution.py:350
  43.5 1.9 %collective-permute-start.2 = (bf16[256,896]{1,0:T(8,128)(2,1)S(1)}, bf16[256,896]{1,0:T(8,128)(2,1)S(1)}, u32[]{:S(2)}, u32[]{:S(2)}) collective-permute-start(bf16[256,896]{1,0:T(8,128)(2,1)S(1)} %pad_maximum_fusion), channel_id=1, source_target_pairs={{0,4},{4,0},{1,5},{5,1},{2,6},{6,2},{3,7},{7,3},{8,12},{12,8},{9,1... | collective-permute-start | bytes 1376264 | tf_op jit(solution)/shard_map/ppermute | solution.py:33
  47.2 2.1 %shard_map.86 = (bf16[512,1024]{1,0:T(8,128)(2,1)S(1)}, bf16[1024,512]{1,0:T(8,128)(2,1)S(1)}) custom-call(s32[4]{0:T(128)S(1)} %compare_select_fusion.5.sel_ref, s32[1]{0:T(128)} %bitcast.core_ref, bf16[128,896]{1,0:T(8,128)(2,1)S(1)} %copy-done, bf16[128,896]{1,0:T(8,128)(2,1)S(1)} %collective-permute-done.right_ref, ...), custom_call_target="tpu_custom_call" | custom-call | flops 1000000000 | bytes 3000000 | tf_op jit(solution)/shard_map/pallas_call | solution.py:84
  50.3 4.0 %all-to-all-done.1 = bf16[4,128,1024]{2,1,0:T(8,128)(2,1)S(1)} async-done(((bf16[4,128,1024]{2,1,0:T(8,128)(2,1)}), bf16[4,128,1024]{2,1,0:T(8,128)(2,1)S(1)}, u32[]{:S(2)}, u32[]{:S(2)}) %all-to-all-start.1) | async-done | bytes 1048608 | tf_op jit(solution)/shard_map/all_to_all | solution.py:350
  54.3 2.0 %collective-permute-start.3 = (bf16[512,1024]{1,0:T(8,128)(2,1)S(1)}, bf16[512,1024]{1,0:T(8,128)(2,1)S(1)}, u32[]{:S(2)}, u32[]{:S(2)}) collective-permute-start(bf16[512,1024]{1,0:T(8,128)(2,1)S(1)} %bitcast.7), channel_id=1, source_target_pairs={{0,4},{4,0},{1,5},{5,1},{2,6},{6,2},{3,7},{7,3},{8,12},{12,8},{9,1... | collective-permute-start | bytes 3145736 | tf_op jit(solution)/shard_map/ppermute | solution.py:33
  57.0 1.9 %collective-permute-done.3.wb_ref = bf16[512,1024]{1,0:T(8,128)(2,1)S(1)} collective-permute-done((bf16[512,1024]{1,0:T(8,128)(2,1)S(1)}, bf16[512,1024]{1,0:T(8,128)(2,1)S(1)}, u32[]{:S(2)}, u32[]{:S(2)}) %collective-permute-start.3) | collective-permute-done | bytes 1048608 | tf_op jit(solution)/shard_map/ppermute | solution.py:33
  59.0 2.9 %shard_map.88 = (bf16[128,512]{1,0:T(8,128)(2,1)}, bf16[128,512]{1,0:T(8,128)(2,1)}, bf16[512,1024]{1,0:T(8,128)(2,1)S(1)}, bf16[512,1024]{1,0:T(8,128)(2,1)S(1)}) custom-call(bf16[512,1024]{1,0:T(8,128)(2,1)S(1)} %get-tuple-element.26.x_ref, bf16[1024,512]{1,0:T(8,128)(2,1)S(1)} %copy-done.5, f32[512,1024]{1,0:T(8,128)S(1)} %shard_map.87.part_ref, ...), custom_call_target="tpu_custom_call" | custom-call | flops 2500000000 | bytes 6000000 | tf_op jit(solution)/shard_map/pallas_call | solution.py:154
  61.8 2.0 %collective-permute-start.4 = (bf16[512,1024]{1,0:T(8,128)(2,1)S(1)}, bf16[512,1024]{1,0:T(8,128)(2,1)S(1)}, u32[]{:S(2)}, u32[]{:S(2)}) collective-permute-start(bf16[512,1024]{1,0:T(8,128)(2,1)S(1)} %get-tuple-element.35), channel_id=1, source_target_pairs={{0,4},{4,0},{1,5},{5,1},{2,6},{6,2},{3,7},{7,3},{8,12},{12,8},{9,1... | collective-permute-start | bytes 3145736 | tf_op jit(solution)/shard_map/ppermute | solution.py:33
  63.9 2.8 %shard_map.89 = (bf16[512,1024]{1,0:T(8,128)(2,1)S(1)}, bf16[384,1024]{1,0:T(8,128)(2,1)S(1)}, bf16[256,1024]{1,0:T(8,128)(2,1)S(1)}) custom-call(s32[4]{0:T(128)S(1)} %compare_select_fusion.5.sel_ref, s32[1]{0:T(128)} %bitcast.core_ref, bf16[1024,512]{1,0:T(8,128)(2,1)S(1)} %copy-done.5, bf16[512,1024]{1,0:T(8,128)(2,1)S(1)} %bitcast.9, ...), custom_call_target="tpu_custom_call" | custom-call | flops 1600000000 | bytes 6000000 | tf_op jit(solution)/shard_map/pallas_call | solution.py:200
  67.8 3.5 %all-to-all-start.2 = ((bf16[4,128,1024]{2,1,0:T(8,128)(2,1)}), bf16[4,128,1024]{2,1,0:T(8,128)(2,1)S(1)}, u32[]{:S(2)}, u32[]{:S(2)}) async-start(bf16[4,128,1024]{2,1,0:T(8,128)(2,1)} %shard_map.90), calls=%async_computation.2 | async-start | bytes 2097152 | tf_op jit(solution)/shard_map/all_to_all | solution.py:382
  71.3 2.3 %collective-permute-start.5 = (bf16[256,1024]{1,0:T(8,128)(2,1)S(1)}, bf16[256,1024]{1,0:T(8,128)(2,1)S(1)}, u32[]{:S(2)}, u32[]{:S(2)}) collective-permute-start(bf16[256,1024]{1,0:T(8,128)(2,1)S(1)} %get-tuple-element.36), channel_id=1, source_target_pairs={{0,4},{4,0},{1,5},{5,1},{2,6},{6,2},{3,7},{7,3},{8,12},{12,8},{9,1... | collective-permute-start | bytes 1572872 | tf_op jit(solution)/shard_map/ppermute | solution.py:33
  75.3 2.4 %collective-permute-start.6 = (bf16[384,256]{1,0:T(8,128)(2,1)S(1)}, bf16[384,256]{1,0:T(8,128)(2,1)S(1)}, u32[]{:S(2)}, u32[]{:S(2)}) collective-permute-start(bf16[384,256]{1,0:T(8,128)(2,1)S(1)} %get-tuple-element.38), channel_id=1, source_target_pairs={{0,1},{1,2},{2,3},{3,0},{4,5},{5,6},{6,7},{7,4},{8,9},{9,10},{10,1... | collective-permute-start | bytes 589832 | tf_op jit(solution)/shard_map/ppermute | solution.py:390
  77.7 3.5 %collective-permute-start.7 = (bf16[384,256]{1,0:T(8,128)(2,1)S(1)}, bf16[384,256]{1,0:T(8,128)(2,1)S(1)}, u32[]{:S(2)}, u32[]{:S(2)}) collective-permute-start(bf16[384,256]{1,0:T(8,128)(2,1)S(1)} %get-tuple-element.39), channel_id=1, source_target_pairs={{0,3},{1,0},{2,1},{3,2},{4,7},{5,4},{6,5},{7,6},{8,11},{9,8},{10,9... | collective-permute-start | bytes 589832 | tf_op jit(solution)/shard_map/ppermute | solution.py:390
  81.2 3.2 %collective-permute-done.6.b_ref = bf16[384,256]{1,0:T(8,128)(2,1)S(1)} collective-permute-done((bf16[384,256]{1,0:T(8,128)(2,1)S(1)}, bf16[384,256]{1,0:T(8,128)(2,1)S(1)}, u32[]{:S(2)}, u32[]{:S(2)}) %collective-permute-start.6) | collective-permute-done | bytes 196640 | tf_op jit(solution)/shard_map/ppermute | solution.py:390
  84.4 3.3 %collective-permute-done.7.d_ref = bf16[384,256]{1,0:T(8,128)(2,1)S(1)} collective-permute-done((bf16[384,256]{1,0:T(8,128)(2,1)S(1)}, bf16[384,256]{1,0:T(8,128)(2,1)S(1)}, u32[]{:S(2)}, u32[]{:S(2)}) %collective-permute-start.7) | collective-permute-done | bytes 196640 | tf_op jit(solution)/shard_map/ppermute | solution.py:390
  88.6 7.7 %all-to-all-start.3 = ((bf16[16,8,1024]{2,1,0:T(8,128)(2,1)}), bf16[16,8,1024]{2,1,0:T(8,128)(2,1)S(1)}, u32[]{:S(2)}, u32[]{:S(2)}) async-start(bf16[16,8,1024]{2,1,0:T(8,128)(2,1)} %bitcast.5), calls=%async_computation.3 | async-start | bytes 524288 | tf_op jit(solution)/shard_map/all_to_all | solution.py:395
  96.3 3.1 %collective-permute-start.8 = (bf16[384,256]{1,0:T(8,128)(2,1)S(1)}, bf16[384,256]{1,0:T(8,128)(2,1)S(1)}, u32[]{:S(2)}, u32[]{:S(2)}) collective-permute-start(bf16[384,256]{1,0:T(8,128)(2,1)S(1)} %get-tuple-element.42), channel_id=1, source_target_pairs={{0,2},{1,3},{2,0},{3,1},{4,6},{5,7},{6,4},{7,5},{8,10},{9,11},{10,... | collective-permute-start | bytes 589832 | tf_op jit(solution)/shard_map/ppermute | solution.py:390
  99.4 6.0 %collective-permute-done.8.c_ref = bf16[384,256]{1,0:T(8,128)(2,1)S(1)} collective-permute-done((bf16[384,256]{1,0:T(8,128)(2,1)S(1)}, bf16[384,256]{1,0:T(8,128)(2,1)S(1)}, u32[]{:S(2)}, u32[]{:S(2)}) %collective-permute-start.8) | collective-permute-done | bytes 196640 | tf_op jit(solution)/shard_map/ppermute | solution.py:390
  105.5 3.7 %collective-permute-start.9 = (bf16[128,256]{1,0:T(8,128)(2,1)S(1)}, bf16[128,256]{1,0:T(8,128)(2,1)S(1)}, u32[]{:S(2)}, u32[]{:S(2)}) collective-permute-start(bf16[128,256]{1,0:T(8,128)(2,1)S(1)} %get-tuple-element.44), channel_id=1, source_target_pairs={{0,8},{4,12},{8,16},{12,20},{16,24},{20,28},{24,32},{28,36},{32,40... | collective-permute-start | bytes 196616 | tf_op jit(solution)/shard_map/ppermute | solution.py:38
  109.3 5.5 %collective-permute-start.10 = (bf16[128,256]{1,0:T(8,128)(2,1)S(1)}, bf16[128,256]{1,0:T(8,128)(2,1)S(1)}, u32[]{:S(2)}, u32[]{:S(2)}) collective-permute-start(bf16[128,256]{1,0:T(8,128)(2,1)S(1)} %get-tuple-element.45), channel_id=1, source_target_pairs={{0,504},{4,508},{8,0},{12,4},{16,8},{20,12},{24,16},{28,20},{32,24... | collective-permute-start | bytes 196616 | tf_op jit(solution)/shard_map/ppermute | solution.py:38
  (38 shorter events, 13.2 us)
Async XLA Ops:
  0.6 0.7 copy-start.1
  2.1 35.8 %all-to-all-start = ((bf16[16,8,1024]{2,1,0:T(8,128)(2,1)}), bf16[16,8,1024]{2,1,0:T(8,128)(2,1)S(1)}, u32[]{:S(2)}, u32[]{:S(2)}) async-start(bf16[16,8,1024]{2,1,0:T(8,128)(2,1)} %shard_map.84), calls=%async_computation | async-start | bytes 524288 | tf_op jit(solution)/shard_map/all_to_all | solution.py:346
  17.3 26.1 %copy-start = (bf16[128,896]{1,0:T(8,128)(2,1)S(1)}, bf16[128,896]{1,0:T(8,128)(2,1)}, u32[]{:S(2)}) copy-start(bf16[128,896]{1,0:T(8,128)(2,1)} %own_ref.1) | copy-start | bytes 688132
  17.3 26.1 %collective-permute-start.1 = (bf16[128,896]{1,0:T(8,128)(2,1)}, bf16[128,896]{1,0:T(8,128)(2,1)S(1)}, u32[]{:S(2)}, u32[]{:S(2)}) collective-permute-start(bf16[128,896]{1,0:T(8,128)(2,1)} %own_ref.1), channel_id=1, source_target_pairs={{0,8},{4,12},{8,16},{12,20},{16,24},{20,28},{24,32},{28,36},{32,40... | collective-permute-start | bytes 688136 | tf_op jit(solution)/shard_map/ppermute | solution.py:38
  21.3 22.1 %collective-permute-start = (bf16[128,896]{1,0:T(8,128)(2,1)}, bf16[128,896]{1,0:T(8,128)(2,1)S(1)}, u32[]{:S(2)}, u32[]{:S(2)}) collective-permute-start(bf16[128,896]{1,0:T(8,128)(2,1)} %own_ref.1), channel_id=1, source_target_pairs={{0,504},{4,508},{8,0},{12,4},{16,8},{20,12},{24,16},{28,20},{32,24... | collective-permute-start | bytes 688136 | tf_op jit(solution)/shard_map/ppermute | solution.py:38
  38.9 6.5 %copy-start.6 = (s32[2,2]{1,0:T(2,128)S(1)}, s32[2,2]{1,0:T(2,128)}, u32[]{:S(2)}) copy-start(s32[2,2]{1,0:T(2,128)} %param.8) | copy-start | bytes 52
  38.9 15.4 %all-to-all-start.1 = ((bf16[4,128,1024]{2,1,0:T(8,128)(2,1)}), bf16[4,128,1024]{2,1,0:T(8,128)(2,1)S(1)}, u32[]{:S(2)}, u32[]{:S(2)}) async-start(bf16[4,128,1024]{2,1,0:T(8,128)(2,1)} %shard_map.85), calls=%async_computation.1 | async-start | bytes 2097152 | tf_op jit(solution)/shard_map/all_to_all | solution.py:350
  43.5 3.7 %collective-permute-start.2 = (bf16[256,896]{1,0:T(8,128)(2,1)S(1)}, bf16[256,896]{1,0:T(8,128)(2,1)S(1)}, u32[]{:S(2)}, u32[]{:S(2)}) collective-permute-start(bf16[256,896]{1,0:T(8,128)(2,1)S(1)} %pad_maximum_fusion), channel_id=1, source_target_pairs={{0,4},{4,0},{1,5},{5,1},{2,6},{6,2},{3,7},{7,3},{8,12},{12,8},{9,1... | collective-permute-start | bytes 1376264 | tf_op jit(solution)/shard_map/ppermute | solution.py:33
  49.3 1.0 copy-start.4
  54.3 4.7 %copy-start.2 = (bf16[128,512]{1,0:T(8,128)(2,1)S(1)}, bf16[128,512]{1,0:T(8,128)(2,1)}, u32[]{:S(2)}) copy-start(bf16[128,512]{1,0:T(8,128)(2,1)} %q_ref.1) | copy-start | bytes 393220
  54.3 4.7 %copy-start.3 = (bf16[128,512]{1,0:T(8,128)(2,1)S(1)}, bf16[128,512]{1,0:T(8,128)(2,1)}, u32[]{:S(2)}) copy-start(bf16[128,512]{1,0:T(8,128)(2,1)} %g_ref.1) | copy-start | bytes 393220
  54.3 4.7 %copy-start.5 = (bf16[1024,512]{1,0:T(8,128)(2,1)S(1)}, bf16[1024,512]{1,0:T(8,128)(2,1)}, u32[]{:S(2)}) copy-start(bf16[1024,512]{1,0:T(8,128)(2,1)} %copy-done.4) | copy-start | bytes 3145732
  54.3 4.7 %collective-permute-start.3 = (bf16[512,1024]{1,0:T(8,128)(2,1)S(1)}, bf16[512,1024]{1,0:T(8,128)(2,1)S(1)}, u32[]{:S(2)}, u32[]{:S(2)}) collective-permute-start(bf16[512,1024]{1,0:T(8,128)(2,1)S(1)} %bitcast.7), channel_id=1, source_target_pairs={{0,4},{4,0},{1,5},{5,1},{2,6},{6,2},{3,7},{7,3},{8,12},{12,8},{9,1... | collective-permute-start | bytes 3145736 | tf_op jit(solution)/shard_map/ppermute | solution.py:33
  61.8 4.8 %collective-permute-start.4 = (bf16[512,1024]{1,0:T(8,128)(2,1)S(1)}, bf16[512,1024]{1,0:T(8,128)(2,1)S(1)}, u32[]{:S(2)}, u32[]{:S(2)}) collective-permute-start(bf16[512,1024]{1,0:T(8,128)(2,1)S(1)} %get-tuple-element.35), channel_id=1, source_target_pairs={{0,4},{4,0},{1,5},{5,1},{2,6},{6,2},{3,7},{7,3},{8,12},{12,8},{9,1... | collective-permute-start | bytes 3145736 | tf_op jit(solution)/shard_map/ppermute | solution.py:33
  67.8 19.9 %all-to-all-start.2 = ((bf16[4,128,1024]{2,1,0:T(8,128)(2,1)}), bf16[4,128,1024]{2,1,0:T(8,128)(2,1)S(1)}, u32[]{:S(2)}, u32[]{:S(2)}) async-start(bf16[4,128,1024]{2,1,0:T(8,128)(2,1)} %shard_map.90), calls=%async_computation.2 | async-start | bytes 2097152 | tf_op jit(solution)/shard_map/all_to_all | solution.py:382
  71.3 3.8 %collective-permute-start.5 = (bf16[256,1024]{1,0:T(8,128)(2,1)S(1)}, bf16[256,1024]{1,0:T(8,128)(2,1)S(1)}, u32[]{:S(2)}, u32[]{:S(2)}) collective-permute-start(bf16[256,1024]{1,0:T(8,128)(2,1)S(1)} %get-tuple-element.36), channel_id=1, source_target_pairs={{0,4},{4,0},{1,5},{5,1},{2,6},{6,2},{3,7},{7,3},{8,12},{12,8},{9,1... | collective-permute-start | bytes 1572872 | tf_op jit(solution)/shard_map/ppermute | solution.py:33
  75.3 9.1 %collective-permute-start.6 = (bf16[384,256]{1,0:T(8,128)(2,1)S(1)}, bf16[384,256]{1,0:T(8,128)(2,1)S(1)}, u32[]{:S(2)}, u32[]{:S(2)}) collective-permute-start(bf16[384,256]{1,0:T(8,128)(2,1)S(1)} %get-tuple-element.38), channel_id=1, source_target_pairs={{0,1},{1,2},{2,3},{3,0},{4,5},{5,6},{6,7},{7,4},{8,9},{9,10},{10,1... | collective-permute-start | bytes 589832 | tf_op jit(solution)/shard_map/ppermute | solution.py:390
  77.7 10.0 %collective-permute-start.7 = (bf16[384,256]{1,0:T(8,128)(2,1)S(1)}, bf16[384,256]{1,0:T(8,128)(2,1)S(1)}, u32[]{:S(2)}, u32[]{:S(2)}) collective-permute-start(bf16[384,256]{1,0:T(8,128)(2,1)S(1)} %get-tuple-element.39), channel_id=1, source_target_pairs={{0,3},{1,0},{2,1},{3,2},{4,7},{5,4},{6,5},{7,6},{8,11},{9,8},{10,9... | collective-permute-start | bytes 589832 | tf_op jit(solution)/shard_map/ppermute | solution.py:390
  88.6 29.0 %all-to-all-start.3 = ((bf16[16,8,1024]{2,1,0:T(8,128)(2,1)}), bf16[16,8,1024]{2,1,0:T(8,128)(2,1)S(1)}, u32[]{:S(2)}, u32[]{:S(2)}) async-start(bf16[16,8,1024]{2,1,0:T(8,128)(2,1)} %bitcast.5), calls=%async_computation.3 | async-start | bytes 524288 | tf_op jit(solution)/shard_map/all_to_all | solution.py:395
  96.3 9.2 %collective-permute-start.8 = (bf16[384,256]{1,0:T(8,128)(2,1)S(1)}, bf16[384,256]{1,0:T(8,128)(2,1)S(1)}, u32[]{:S(2)}, u32[]{:S(2)}) collective-permute-start(bf16[384,256]{1,0:T(8,128)(2,1)S(1)} %get-tuple-element.42), channel_id=1, source_target_pairs={{0,2},{1,3},{2,0},{3,1},{4,6},{5,7},{6,4},{7,5},{8,10},{9,11},{10,... | collective-permute-start | bytes 589832 | tf_op jit(solution)/shard_map/ppermute | solution.py:390
  105.5 9.8 %collective-permute-start.9 = (bf16[128,256]{1,0:T(8,128)(2,1)S(1)}, bf16[128,256]{1,0:T(8,128)(2,1)S(1)}, u32[]{:S(2)}, u32[]{:S(2)}) collective-permute-start(bf16[128,256]{1,0:T(8,128)(2,1)S(1)} %get-tuple-element.44), channel_id=1, source_target_pairs={{0,8},{4,12},{8,16},{12,20},{16,24},{20,28},{24,32},{28,36},{32,40... | collective-permute-start | bytes 196616 | tf_op jit(solution)/shard_map/ppermute | solution.py:38
  109.3 7.4 %collective-permute-start.10 = (bf16[128,256]{1,0:T(8,128)(2,1)S(1)}, bf16[128,256]{1,0:T(8,128)(2,1)S(1)}, u32[]{:S(2)}, u32[]{:S(2)}) collective-permute-start(bf16[128,256]{1,0:T(8,128)(2,1)S(1)} %get-tuple-element.45), channel_id=1, source_target_pairs={{0,504},{4,508},{8,0},{12,4},{16,8},{20,12},{24,16},{28,20},{32,24... | collective-permute-start | bytes 196616 | tf_op jit(solution)/shard_map/ppermute | solution.py:38

commit v4 on v0

v4 whole, which is shorter than its diff:
```python
import jax
import jax.numpy as jnp
from jax import lax
from jax.experimental import pallas as pl
from jax.experimental.pallas import tpu as pltpu
from jax.sharding import Mesh
from jax.sharding import PartitionSpec as P

HD = 128
SPAN = 64
NROWS = 128
NBR = 2
NY = 4
NZ = 16
NC = 2
NX = 4
DP = ("y", "z", "c")
ENC = 896
OWN = 7
PAD = 8
COLS = 1024
SIDE = COLS // NC
PART = COLS // (2 * NC)
ROWS = NY * NZ * NC * PAD
NEAR = 6
NT = (((1,), (1,)), ((), ()))
TN = (((0,), (0,)), ((), ()))
OWN_BLOCK, RIGHT, LEFT = range(3)


def after(value, *earlier):
    return lax.optimization_barrier((value,) + earlier)[0]


def swap_cores(value):
    return lax.ppermute(value, "c", [(0, 1), (1, 0)])


def shifted(value, steps):
    count = NY * NZ * NC
    return lax.ppermute(value, DP, [(i, (i + steps) % count) for i in range(count)])


def natural_column(place):
    row = place % PAD
    return jnp.where(row < OWN, place // PAD * OWN + row, -1)


def small_call(kernel, scalars, arrays, outs, scratch=(), limit=8, specs=None):
    vmem = pl.BlockSpec(memory_space=pltpu.VMEM)
    smem = pl.BlockSpec(memory_space=pltpu.SMEM)
    return pl.pallas_call(
        kernel,
        out_shape=outs,
        in_specs=[smem] * len(scalars) + [vmem] * len(arrays),
        out_specs=specs or (vmem,) * len(outs),
        scratch_shapes=list(scratch),
        compiler_params=pltpu.CompilerParams(vmem_limit_bytes=limit * 2**20),
        cost_estimate=pl.CostEstimate(flops=1000, bytes_accessed=1000, transcendentals=0),
    )(*scalars, *arrays)


def shape(*size, dtype=jnp.bfloat16):
    return jax.ShapeDtypeStruct(size, dtype)


def spread_kernel(core_ref, w_ref, out_ref):
    f32 = jnp.float32
    lanes = pl.ds(pl.multiple_of(core_ref[0] * PART, PART), PART)
    sides = []
    for t in range(2):
        rows = []
        for core in range(NC):
            rows += [w_ref[core, r, :, lanes].astype(f32)[t : t + 1, :] for r in range(OWN)]
            rows.append(jnp.zeros((PAD - OWN, PART), f32))
        sides.append(jnp.concatenate(rows, axis=0))
    rows = jnp.concatenate(sides, axis=1).astype(out_ref.dtype)
    for copy in range(out_ref.shape[0]):
        out_ref[copy] = rows


def copies_kernel(block_ref, out_ref, sems):
    copies = [
        pltpu.make_async_copy(block_ref, out_ref.at[i], sems.at[i])
        for i in range(out_ref.shape[0])
    ]
    for copy in copies:
        copy.start()
    for copy in copies:
        copy.wait()


def pack_kernel(core_ref, q_ref, g_ref, near_ref, far_ref):
    for out_ref, side in ((near_ref, core_ref[0]), (far_ref, 1 - core_ref[0])):
        lanes = pl.ds(pl.multiple_of(side * PART, PART), PART)
        out_ref[:, :PART] = q_ref[:, lanes]
        out_ref[:, PART:] = g_ref[:, lanes]


def unpack_kernel(core_ref, mine_ref, got_ref, att_ref, qg_ref):
    core = core_ref[0]
    here = pl.ds(pl.multiple_of(core * PART, PART), PART)
    there = pl.ds(pl.multiple_of((1 - core) * PART, PART), PART)
    for out_ref, first in ((att_ref, 0), (qg_ref, PART)):
        out_ref[:, here] = mine_ref[:, first : first + PART]
        out_ref[:, there] = got_ref[:, first : first + PART]


def layout_kernel(own_ref, right_ref, left_ref, other_ref, x_ref):
    f32, b16 = jnp.float32, jnp.bfloat16
    place = lax.broadcasted_iota(jnp.int32, (1, ROWS), 1)
    pick = lax.broadcasted_iota(jnp.int32, (ENC, ROWS), 0) == natural_column(place)
    pick = jnp.where(pick, 1.0, 0.0).astype(b16)
    parts = [own_ref[...], right_ref[...], left_ref[...]]
    parts += [other_ref[i * NROWS : (i + 1) * NROWS, :] for i in range(3)]
    for i, part in enumerate(parts):
        x = jnp.dot(part, pick, preferred_element_type=f32)
        x_ref[i * NROWS : (i + 1) * NROWS, :] = x.astype(b16)


def attention_kernel(
    sel_ref, x_ref, w_ref, near_ref, far_ref,
    mine_ref, back_ref, cb_ref, share_ref, kv_ref, acc_ref, out_ref, sems,
):
    f32, b16 = jnp.float32, jnp.bfloat16
    factor = 1.0 / HD**0.5
    acc_ref[...] = jnp.zeros_like(acc_ref)
    kv_ref[...] = jnp.dot(x_ref[...], w_ref[...], preferred_element_type=f32).astype(b16)
    heads = PART // HD
    units = [(span, head) for span in range(4) for head in range(heads)]
    kcols = [slice(head * HD, (head + 1) * HD) for _, head in units]
    vcols = [slice(PART + head * HD, PART + (head + 1) * HD) for _, head in units]
    rows = [slice(span % 2 * SPAN, (span % 2 + 1) * SPAN) for span, _ in units]
    blocks = [
        [
            pl.ds(pl.multiple_of(sel_ref[span * NBR + j] * NROWS, NROWS), NROWS)
            for j in range(NBR)
        ]
        for span, _ in units
    ]
    q, g = [], []
    for (span, _), r, kc, vc in zip(units, rows, kcols, vcols):
        from_ref = near_ref if span < 2 else far_ref
        q.append(from_ref[r, kc])
        g.append(from_ref[r, vc])
    k = [jnp.concatenate([kv_ref[b, c] for b in two], axis=0) for two, c in zip(blocks, kcols)]
    v = [jnp.concatenate([kv_ref[b, c] for b in two], axis=0) for two, c in zip(blocks, vcols)]
    scores = [
        lax.dot_general(a, b, NT, preferred_element_type=f32) * factor for a, b in zip(q, k)
    ]
    dprobs = [lax.dot_general(a, b, NT, preferred_element_type=f32) for a, b in zip(g, v)]
    raised = [jnp.exp(a - jnp.max(a, axis=-1, keepdims=True)) for a in scores]
    probs = [a / jnp.sum(a, axis=-1, keepdims=True) for a in raised]
    probs_b = [a.astype(b16) for a in probs]
    delta = [jnp.sum(a * b, axis=-1, keepdims=True) for a, b in zip(probs, dprobs)]
    dscores = [
        (a * (b - c) * factor).astype(b16) for a, b, c in zip(probs, dprobs, delta)
    ]
    for i, (span, _) in enumerate(units):
        to_ref = mine_ref if span < 2 else back_ref
        out = jnp.dot(probs_b[i], v[i], preferred_element_type=f32)
        to_ref[rows[i], kcols[i]] = out.astype(b16)
        out = jnp.dot(dscores[i], k[i], preferred_element_type=f32)
        to_ref[rows[i], vcols[i]] = out.astype(b16)
    vgrad = [lax.dot_general(a, b, TN, preferred_element_type=f32) for a, b in zip(probs_b, g)]
    kgrad = [lax.dot_general(a, b, TN, preferred_element_type=f32) for a, b in zip(dscores, q)]
    for i in range(len(units)):
        for j, block in enumerate(blocks[i]):
            part = slice(j * NROWS, (j + 1) * NROWS)
            acc_ref[block, kcols[i]] += kgrad[i][part, :]
            acc_ref[block, vcols[i]] += vgrad[i][part, :]
    cb_ref[...] = acc_ref[...].astype(b16)
    copies = []
    for part in range(NY):
        size = out_ref.shape[1]
        rows = slice(part * size, (part + 1) * size)
        product = lax.dot_general(x_ref[:, rows], cb_ref[...], TN, preferred_element_type=f32)
        out_ref[part] = product.astype(b16)
        copies.append(pltpu.make_async_copy(out_ref.at[part], share_ref.at[part], sems.at[part]))
        copies[-1].start()
    for copy in copies:
        copy.wait()


def encoding_kernel(w_ref, cb_ref, keep_ref, send_ref):
    half = keep_ref.shape[0]
    for out_ref, first in ((keep_ref, 0), (send_ref, half)):
        out_ref[...] = lax.dot_general(
            cb_ref[first : first + half, :], w_ref[...], NT, preferred_element_type=jnp.float32
        ).astype(out_ref.dtype)


def merge_kernel(x_ref, keep_ref, got_ref, *out_refs):
    for step, out_ref in enumerate(out_refs):
        width = out_ref.shape[1]
        lanes = pl.ds(pl.multiple_of((x_ref[0] + step) % NX * width, width), width)
        total = keep_ref[:, lanes].astype(jnp.float32) + got_ref[:, lanes].astype(jnp.float32)
        out_ref[...] = total.astype(out_ref.dtype)


def summed(refs, rows):
    total = refs[0][rows, :].astype(jnp.float32)
    for ref in refs[1:]:
        total = total + ref[rows, :].astype(jnp.float32)
    return total


def groups_kernel(a_ref, b_ref, c_ref, d_ref, *out_refs):
    for slot, out_ref in enumerate(out_refs):
        rows = slice(slot * NROWS, (slot + 1) * NROWS)
        out_ref[...] = summed((a_ref, b_ref, c_ref, d_ref), rows).astype(out_ref.dtype)


def reduced_kernel(parts_ref, out_ref):
    total = parts_ref[0].astype(jnp.float32)
    for i in range(1, parts_ref.shape[0]):
        total = total + parts_ref[i].astype(jnp.float32)
    out_ref[...] = total.astype(out_ref.dtype)


def finish_kernel(own_ref, left_ref, right_ref, out_ref):
    b16 = jnp.bfloat16
    total = summed((own_ref, left_ref, right_ref), slice(None)).astype(b16)
    width, size = out_ref.shape[0], total.shape[1]
    column = natural_column(lax.broadcasted_iota(jnp.int32, (1, size), 1))
    pick = lax.broadcasted_iota(jnp.int32, (width, size), 0) == column
    pick = jnp.where(pick, 1.0, 0.0).astype(b16)
    out_ref[...] = lax.dot_general(
        pick, total, NT, preferred_element_type=jnp.float32
    ).astype(b16)


def per_device(queries, encodings, kv_weight, pair_list, cotangent):
    f32, b16 = jnp.float32, jnp.bfloat16
    core = lax.axis_index("c")
    core_id = core.reshape(1)
    chip = lax.axis_index("y") * NZ + lax.axis_index("z")
    hbm = pl.BlockSpec(memory_space=pltpu.HBM)
    vmem = pl.BlockSpec(memory_space=pltpu.VMEM)

    both = lax.all_gather(kv_weight, "c")
    (copies,) = small_call(spread_kernel, (core_id,), (both,), (shape(NZ, NC * PAD, SIDE),))
    w = lax.all_to_all(copies, "z", 0, 0).reshape(NZ * NC * PAD, SIDE)
    right = shifted(encodings, -2)
    left = shifted(encodings, 2)
    near, far = small_call(
        pack_kernel, (core_id,), (queries, cotangent), (shape(NROWS, SIDE),) * 2
    )
    far = swap_cores(far)
    pairs_far = swap_cores(pair_list)
    w = after(w, pairs_far)
    (copies,) = small_call(
        copies_kernel, (), (w,), (shape(NY, *w.shape),),
        [pltpu.SemaphoreType.DMA((NY,))], specs=(hbm,),
    )
    w = lax.all_to_all(copies, "y", 0, 0).reshape(ROWS, SIDE)
    here = after(encodings, copies)
    other = swap_cores(jnp.concatenate([here, right, left]))
    (x,) = small_call(
        layout_kernel, (), (encodings, right, left, other),
        (shape(NEAR * NROWS, ROWS),), limit=16,
    )

    pairs = jnp.concatenate([pair_list.reshape(-1), pairs_far.reshape(-1)])
    step = (pairs // NC - chip + NY * NZ) % (NY * NZ)
    place = jnp.where(step == 0, OWN_BLOCK, jnp.where(step == 1, RIGHT, LEFT))
    sel = (place + jnp.where(pairs % NC == core, 0, 3)).astype(jnp.int32)

    grads = shape(NEAR * NROWS, SIDE)
    chunk = shape(NY, ROWS // NY, SIDE)
    mine, back, contributions, share = small_call(
        attention_kernel, (sel,), (x, w, near, far),
        (shape(NROWS, SIDE), shape(NROWS, SIDE), grads, chunk),
        [
            pltpu.VMEM(grads.shape, b16),
            pltpu.VMEM(grads.shape, f32),
            pltpu.VMEM(chunk.shape, b16),
            pltpu.SemaphoreType.DMA((NY,)),
        ],
        limit=20, specs=(vmem, vmem, vmem, hbm),
    )
    parts = lax.all_to_all(share, "y", 0, 0)
    ekeep, esend = small_call(
        encoding_kernel, (), (w, after(contributions, share)), (shape(3 * NROWS, ROWS),) * 2,
        limit=16,
    )
    got = swap_cores(esend)
    x_id = lax.axis_index("x").reshape(1)
    groups = list(
        small_call(merge_kernel, (x_id,), (ekeep, got), (shape(3 * NROWS, ROWS // NX),) * NX)
    )
    for step in (1, 3, 2):
        groups[step] = lax.ppermute(
            groups[step], "x", [(i, (i + step) % NX) for i in range(NX)]
        )
    returned = swap_cores(back)
    parts = after(parts, groups[1], groups[3])
    (total,) = small_call(reduced_kernel, (), (parts,), (shape(ROWS // NY, SIDE),))
    parts = lax.all_to_all(total.reshape(NZ, NC * PAD, SIDE), "z", 0, 0)
    sums = lax.all_gather(jnp.sum(parts.astype(f32), axis=0), "c")
    sums = lax.dynamic_slice_in_dim(sums, core * PAD, OWN, 1).reshape(NC, OWN, 2, PART)
    weight_grad = sums.transpose(1, 2, 0, 3).reshape(OWN, 2, COLS // 2)

    groups[0] = after(groups[0], total)
    own, right, left = small_call(
        groups_kernel, (), groups, (shape(NROWS, ROWS // NX),) * 3
    )
    from_left = shifted(right, 2)
    from_right = shifted(left, -2)
    attended, query_grad = small_call(
        unpack_kernel, (core_id,), (mine, returned), (shape(NROWS, SIDE),) * 2
    )
    own = after(own, weight_grad)
    (flipped,) = small_call(
        finish_kernel, (), (own, from_left, from_right), (shape(ENC // NX, NROWS),)
    )
    return attended, query_grad, flipped.T, weight_grad


def solution(mesh):
    mesh = Mesh(mesh.devices.reshape(NY, NZ, NC, NX), ("y", "z", "c", "x"))
    return jax.shard_map(
        per_device,
        mesh=mesh,
        in_specs=(P(DP, "x"), P(DP, None), P(DP, None, "x"), P(DP, None), P(DP, "x")),
        out_specs=(P(DP, "x"), P(DP, "x"), P(DP, "x"), P(DP, None, "x")),
        check_vma=False,
    )
```

time: 645 us -> 117 us (0.18)
  waiting for transfers between devices: 530 us -> 22.8 us
  starting transfers between devices: 30 us -> 70.1 us
  local copies, waits for them, and re-layouts: 38.3 us -> 2.8 us
  matrix products: 24.6 us -> 0 us
  Pallas kernels: 0 us -> 13.9 us
  between operations: 14.7 us -> 0.93 us
    unnamed x4 -> x0, waiting for transfers between devices: 339 us -> none
    all_gather x1 -> x0, waiting for transfers between devices: 146 us -> none  [per_device(): weights = lax.all_gather(kv_weight, 'dp', axis=0, tiled=True)]
    all_to_all x0 -> x4, starting transfers between devices: none -> 32.2 us  [the longest x1 15.2 us: per_device(): w = lax.all_to_all(copies, 'z', 0, 0).reshape(NZ * NC * PAD, SIDE)]
    reduce_scatter x1 -> x0, waiting for transfers between devices: 26.7 us -> none  [per_device(): lax.psum_scatter(partial_sum.astype(jnp.bfloat16), 'mp', scatter_dimensio...]
    dot_general x10 -> x0, matrix products: 24.6 us -> none  [the longest x1 5.67 us: per_device(): jnp.einsum('chqk,cqhd->ckhd', dscores, query_rows, preferred_element_type...]
    all_to_all x0 -> x4, waiting for transfers between devices: none -> 17.8 us  [the longest x1 9.53 us: per_device(): parts = lax.all_to_all(share, 'y', 0, 0)]
    pallas_call x0 -> x11, Pallas kernels: none -> 13.9 us  [small_call(): pl.pallas_call(kernel, out_shape=outs, in_specs=[smem] * len(scalars) + [...]
    ppermute x8 -> x12, waiting for transfers between devices: 18.8 us -> 4.99 us  [the longest x5 2.64 us: swap_cores(): return lax.ppermute(value, 'c', [(0, 1), (1, 0)])]
  transfers between devices with their start and end apart: 11 -> 16, of which waited for: 10 -> 6; matrix products, arithmetic and copies ran while one was open for 3% -> 2% of each run, Pallas kernels for 0% -> 4%
where the time goes in v4:
time: 117 us; the launch traced here: 115 us
  starting transfers between devices  70.1 us (60%)
  waiting for transfers between devices  22.8 us (19%)
  Pallas kernels  13.9 us (12%)
  blocking collectives  3.89 us (3%)
  local copies, waits for them, and re-layouts  2.8 us (2%)
    ppermute x4, starting transfers between devices, shifted(): lax.ppermute(value, DP, [(i, (i + steps) % count) for i in range(count)])  18.6 us
    all_to_all x1, starting transfers between devices, per_device(): w = lax.all_to_all(copies, 'z', 0, 0).reshape(NZ * NC * PAD, SIDE)  15.2 us
    pallas_call x11, Pallas kernels, small_call(): pl.pallas_call(kernel, out_shape=outs, in_specs=[smem] * len(scalars) + [...  13.9 us
    ppermute x5, starting transfers between devices, swap_cores(): return lax.ppermute(value, 'c', [(0, 1), (1, 0)])  10.1 us
    all_to_all x1, waiting for transfers between devices, per_device(): parts = lax.all_to_all(share, 'y', 0, 0)  9.53 us
    ppermute x3, starting transfers between devices, per_device(): lax.ppermute(groups[step], 'x', [(i, (i + step) % NX) for i in range(NX)])  9.3 us
    all_to_all x1, starting transfers between devices, per_device(): parts = lax.all_to_all(total.reshape(NZ, NC * PAD, SIDE), 'z', 0, 0)  8.34 us
    all_to_all x1, waiting for transfers between devices, per_device(): w = lax.all_to_all(copies, 'z', 0, 0).reshape(NZ * NC * PAD, SIDE)  7.49 us
  transfers between devices with their start and end apart: 16, of which 6 were waited for; matrix products, arithmetic and copies ran while one was open for 2% of the time, Pallas kernels for 4%

profile of v4, /device:TPU:6, one launch (start us, length us, event | category | flops | bytes accessed | tf_op | source)
XLA Modules:
  0.0 115.5 jit_solution(15974474493708739456)
XLA Ops:
  0.6 2.0 %all-gather = bf16[14,2,512]{2,1,0:T(2,128)(2,1)S(1)} all-gather(bf16[7,2,512]{2,1,0:T(2,128)(2,1)} %param.7), channel_id=2, replica_groups=mesh['y'=4,'z'=16,'c'=2,'x'=4] {'c'}, dimensions={0}, use_global_device_ids=true | all-gather | bytes 43008 | tf_op jit(solution)/shard_map/all_gather | solution.py:241
  3.4 15.2 %all-to-all-start = ((bf16[16,16,512]{2,1,0:T(8,128)(2,1)}), bf16[16,16,512]{2,1,0:T(8,128)(2,1)S(1)}, u32[]{:S(2)}, u32[]{:S(2)}) async-start(bf16[16,16,512]{2,1,0:T(8,128)(2,1)} %shard_map.84), calls=%async_computation | async-start | bytes 524288 | tf_op jit(solution)/shard_map/all_to_all | solution.py:243
  18.6 7.5 %collective-permute-start.1 = (bf16[128,896]{1,0:T(8,128)(2,1)}, bf16[128,896]{1,0:T(8,128)(2,1)S(1)}, u32[]{:S(2)}, u32[]{:S(2)}) collective-permute-start(bf16[128,896]{1,0:T(8,128)(2,1)} %own_ref.1), channel_id=1, source_target_pairs={{0,504},{4,508},{8,0},{12,4},{16,8},{20,12},{24,16},{28,20},{32,24... | collective-permute-start | bytes 688136 | tf_op jit(solution)/shard_map/ppermute | solution.py:41
  26.1 1.9 %collective-permute-start.2 = (bf16[128,896]{1,0:T(8,128)(2,1)}, bf16[128,896]{1,0:T(8,128)(2,1)S(1)}, u32[]{:S(2)}, u32[]{:S(2)}) collective-permute-start(bf16[128,896]{1,0:T(8,128)(2,1)} %own_ref.1), channel_id=1, source_target_pairs={{0,8},{4,12},{8,16},{12,20},{16,24},{20,28},{24,32},{28,36},{32,40... | collective-permute-start | bytes 688136 | tf_op jit(solution)/shard_map/ppermute | solution.py:41
  28.0 1.9 %collective-permute-start = (s32[2,2]{1,0:T(2,128)}, s32[2,2]{1,0:T(2,128)S(1)}, u32[]{:S(2)}, u32[]{:S(2)}) collective-permute-start(s32[2,2]{1,0:T(2,128)} %param.8), channel_id=1, source_target_pairs={{0,4},{4,0},{1,5},{5,1},{2,6},{6,2},{3,7},{7,3},{8,12},{12,8},{9,1... | collective-permute-start | bytes 56 | tf_op jit(solution)/shard_map/ppermute | solution.py:36
  31.3 7.5 %all-to-all-done = bf16[16,16,512]{2,1,0:T(8,128)(2,1)S(1)} async-done(((bf16[16,16,512]{2,1,0:T(8,128)(2,1)}), bf16[16,16,512]{2,1,0:T(8,128)(2,1)S(1)}, u32[]{:S(2)}, u32[]{:S(2)}) %all-to-all-start) | async-done | bytes 262176 | tf_op jit(solution)/shard_map/all_to_all | solution.py:243
  39.8 4.6 %all-to-all-start.1 = ((bf16[4,256,512]{2,1,0:T(8,128)(2,1)}), bf16[4,256,512]{2,1,0:T(8,128)(2,1)S(1)}, u32[]{:S(2)}, u32[]{:S(2)}) async-start(bf16[4,256,512]{2,1,0:T(8,128)(2,1)} %shard_map.85), calls=%async_computation.1 | async-start | bytes 2097152 | tf_op jit(solution)/shard_map/all_to_all | solution.py:256
  45.4 1.9 %collective-permute-start.3 = (bf16[384,896]{1,0:T(8,128)(2,1)}, bf16[384,896]{1,0:T(8,128)(2,1)S(1)}, u32[]{:S(2)}, u32[]{:S(2)}) collective-permute-start(bf16[384,896]{1,0:T(8,128)(2,1)} %pad_maximum_fusion), channel_id=1, source_target_pairs={{0,4},{4,0},{1,5},{5,1},{2,6},{6,2},{3,7},{7,3},{8,12},{12,8},{9,1... | collective-permute-start | bytes 2064392 | tf_op jit(solution)/shard_map/ppermute | solution.py:36
  48.0 2.4 %collective-permute-start.4 = (bf16[128,512]{1,0:T(8,128)(2,1)}, bf16[128,512]{1,0:T(8,128)(2,1)}, u32[]{:S(2)}, u32[]{:S(2)}) collective-permute-start(bf16[128,512]{1,0:T(8,128)(2,1)} %get-tuple-element.30), channel_id=1, source_target_pairs={{0,4},{4,0},{1,5},{5,1},{2,6},{6,2},{3,7},{7,3},{8,12},{12,8},{9,1... | collective-permute-start | bytes 393224 | tf_op jit(solution)/shard_map/ppermute | solution.py:36
  52.6 1.9 %shard_map.86.x_ref = bf16[768,1024]{1,0:T(8,128)(2,1)S(1)} custom-call(bf16[128,896]{1,0:T(8,128)(2,1)S(1)} %copy-done.1, bf16[128,896]{1,0:T(8,128)(2,1)S(1)} %collective-permute-done.1.right_ref, bf16[128,896]{1,0:T(8,128)(2,1)S(1)} %collective-permute-done.2.left_ref, bf16[384,896]{1,0:T(8,128)(2,1)S(1)} %copy-done.3), custom_call_target="tpu_custom_call" | custom-call | flops 1000 | bytes 1000 | tf_op jit(solution)/shard_map/pallas_call | solution.py:52
  55.3 5.0 %shard_map.88 = (bf16[128,512]{1,0:T(8,128)(2,1)S(1)}, bf16[128,512]{1,0:T(8,128)(2,1)S(1)}, bf16[768,512]{1,0:T(8,128)(2,1)S(1)}, bf16[4,256,512]{2,1,0:T(8,128)(2,1)S(1)}) custom-call(s32[8]{0:T(128)S(1)} %fusion.sel_ref, bf16[768,1024]{1,0:T(8,128)(2,1)S(1)} %shard_map.86.x_ref, bf16[1024,512]{1,0:T(8,128)(2,1)S(1)} %bitcast.11, ...), custom_call_target="tpu_custom_call" | custom-call | flops 1000 | bytes 1000 | tf_op jit(solution)/shard_map/pallas_call | solution.py:52
  60.4 1.9 %shard_map.90 = (bf16[384,1024]{1,0:T(8,128)(2,1)S(1)}, bf16[384,1024]{1,0:T(8,128)(2,1)}) custom-call(bf16[1024,512]{1,0:T(8,128)(2,1)S(1)} %bitcast.12, bf16[768,512]{1,0:T(8,128)(2,1)S(1)} %get-tuple-element.37.cb_ref), custom_call_target="tpu_custom_call" | custom-call | flops 1000 | bytes 1000 | tf_op jit(solution)/shard_map/pallas_call | solution.py:52
  62.3 1.9 %collective-permute-start.6 = (bf16[384,1024]{1,0:T(8,128)(2,1)}, bf16[384,1024]{1,0:T(8,128)(2,1)S(1)}, u32[]{:S(2)}, u32[]{:S(2)}) collective-permute-start(bf16[384,1024]{1,0:T(8,128)(2,1)} %get-tuple-element.39), channel_id=1, source_target_pairs={{0,4},{4,0},{1,5},{5,1},{2,6},{6,2},{3,7},{7,3},{8,12},{12,8},{9,1... | collective-permute-start | bytes 2359304 | tf_op jit(solution)/shard_map/ppermute | solution.py:36
  64.2 4.0 %all-to-all-start.2 = ((bf16[4,256,512]{2,1,0:T(8,128)(2,1)}), bf16[4,256,512]{2,1,0:T(8,128)(2,1)S(1)}, u32[]{:S(2)}, u32[]{:S(2)}) async-start(bf16[4,256,512]{2,1,0:T(8,128)(2,1)} %copy-done), calls=%async_computation.2 | async-start | bytes 2097152 | tf_op jit(solution)/shard_map/all_to_all | solution.py:282
  68.5 2.5 %collective-permute-start.7 = (bf16[384,256]{1,0:T(8,128)(2,1)S(1)}, bf16[384,256]{1,0:T(8,128)(2,1)S(1)}, u32[]{:S(2)}, u32[]{:S(2)}) collective-permute-start(bf16[384,256]{1,0:T(8,128)(2,1)S(1)} %get-tuple-element.41), channel_id=1, source_target_pairs={{0,1},{1,2},{2,3},{3,0},{4,5},{5,6},{6,7},{7,4},{8,9},{9,10},{10,1... | collective-permute-start | bytes 589832 | tf_op jit(solution)/shard_map/ppermute | solution.py:293
  71.0 3.5 %collective-permute-start.8 = (bf16[384,256]{1,0:T(8,128)(2,1)S(1)}, bf16[384,256]{1,0:T(8,128)(2,1)S(1)}, u32[]{:S(2)}, u32[]{:S(2)}) collective-permute-start(bf16[384,256]{1,0:T(8,128)(2,1)S(1)} %get-tuple-element.42), channel_id=1, source_target_pairs={{0,3},{1,0},{2,1},{3,2},{4,7},{5,4},{6,5},{7,6},{8,11},{9,8},{10,9... | collective-permute-start | bytes 589832 | tf_op jit(solution)/shard_map/ppermute | solution.py:293
  74.5 9.5 %all-to-all-done.2.parts_ref = bf16[4,256,512]{2,1,0:T(8,128)(2,1)S(1)} async-done(((bf16[4,256,512]{2,1,0:T(8,128)(2,1)}), bf16[4,256,512]{2,1,0:T(8,128)(2,1)S(1)}, u32[]{:S(2)}, u32[]{:S(2)}) %all-to-all-start.2) | async-done | bytes 1048608 | tf_op jit(solution)/shard_map/all_to_all | solution.py:282
  84.8 8.3 %all-to-all-start.3 = ((bf16[16,16,512]{2,1,0:T(8,128)(2,1)}), bf16[16,16,512]{2,1,0:T(8,128)(2,1)S(1)}, u32[]{:S(2)}, u32[]{:S(2)}) async-start(bf16[16,16,512]{2,1,0:T(8,128)(2,1)} %bitcast.5), calls=%async_computation.3 | async-start | bytes 524288 | tf_op jit(solution)/shard_map/all_to_all | solution.py:299
  93.2 3.3 %collective-permute-start.9 = (bf16[384,256]{1,0:T(8,128)(2,1)S(1)}, bf16[384,256]{1,0:T(8,128)(2,1)S(1)}, u32[]{:S(2)}, u32[]{:S(2)}) collective-permute-start(bf16[384,256]{1,0:T(8,128)(2,1)S(1)} %get-tuple-element.45), channel_id=1, source_target_pairs={{0,2},{1,3},{2,0},{3,1},{4,6},{5,7},{6,4},{7,5},{8,10},{9,11},{10,... | collective-permute-start | bytes 589832 | tf_op jit(solution)/shard_map/ppermute | solution.py:293
  96.5 1.9 %collective-permute-start.5 = (bf16[128,512]{1,0:T(8,128)(2,1)S(1)}, bf16[128,512]{1,0:T(8,128)(2,1)S(1)}, u32[]{:S(2)}, u32[]{:S(2)}) collective-permute-start(bf16[128,512]{1,0:T(8,128)(2,1)S(1)} %copy-done.7), channel_id=1, source_target_pairs={{0,4},{4,0},{1,5},{5,1},{2,6},{6,2},{3,7},{7,3},{8,12},{12,8},{9,1... | collective-permute-start | bytes 393224 | tf_op jit(solution)/shard_map/ppermute | solution.py:36
  100.5 2.3 %collective-permute-done.9.c_ref = bf16[384,256]{1,0:T(8,128)(2,1)S(1)} collective-permute-done((bf16[384,256]{1,0:T(8,128)(2,1)S(1)}, bf16[384,256]{1,0:T(8,128)(2,1)S(1)}, u32[]{:S(2)}, u32[]{:S(2)}) %collective-permute-start.9) | collective-permute-done | bytes 196640 | tf_op jit(solution)/shard_map/ppermute | solution.py:293
  102.9 3.5 %collective-permute-start.10 = (bf16[128,256]{1,0:T(8,128)(2,1)S(1)}, bf16[128,256]{1,0:T(8,128)(2,1)S(1)}, u32[]{:S(2)}, u32[]{:S(2)}) collective-permute-start(bf16[128,256]{1,0:T(8,128)(2,1)S(1)} %get-tuple-element.48), channel_id=1, source_target_pairs={{0,8},{4,12},{8,16},{12,20},{16,24},{20,28},{24,32},{28,36},{32,40... | collective-permute-start | bytes 196616 | tf_op jit(solution)/shard_map/ppermute | solution.py:41
  106.5 5.6 %collective-permute-start.11 = (bf16[128,256]{1,0:T(8,128)(2,1)S(1)}, bf16[128,256]{1,0:T(8,128)(2,1)S(1)}, u32[]{:S(2)}, u32[]{:S(2)}) collective-permute-start(bf16[128,256]{1,0:T(8,128)(2,1)S(1)} %get-tuple-element.49), channel_id=1, source_target_pairs={{0,504},{4,508},{8,0},{12,4},{16,8},{20,12},{24,16},{28,20},{32,24... | collective-permute-start | bytes 196616 | tf_op jit(solution)/shard_map/ppermute | solution.py:41
  112.2 1.9 %all-gather.1 = f32[32,512]{1,0:T(8,128)S(1)} all-gather(f32[16,512]{1,0:T(8,128)S(1)} %convert_reduce_fusion), channel_id=3, replica_groups=mesh['y'=4,'z'=16,'c'=2,'x'=4] {'c'}, dimensions={0}, use_global_device_ids=true | all-gather | bytes 98304 | tf_op jit(solution)/shard_map/all_gather | solution.py:300
  (47 shorter events, 12.4 us)
Async XLA Ops:
  3.4 35.4 %all-to-all-start = ((bf16[16,16,512]{2,1,0:T(8,128)(2,1)}), bf16[16,16,512]{2,1,0:T(8,128)(2,1)S(1)}, u32[]{:S(2)}, u32[]{:S(2)}) async-start(bf16[16,16,512]{2,1,0:T(8,128)(2,1)} %shard_map.84), calls=%async_computation | async-start | bytes 524288 | tf_op jit(solution)/shard_map/all_to_all | solution.py:243
  18.6 25.8 %collective-permute-start.1 = (bf16[128,896]{1,0:T(8,128)(2,1)}, bf16[128,896]{1,0:T(8,128)(2,1)S(1)}, u32[]{:S(2)}, u32[]{:S(2)}) collective-permute-start(bf16[128,896]{1,0:T(8,128)(2,1)} %own_ref.1), channel_id=1, source_target_pairs={{0,504},{4,508},{8,0},{12,4},{16,8},{20,12},{24,16},{28,20},{32,24... | collective-permute-start | bytes 688136 | tf_op jit(solution)/shard_map/ppermute | solution.py:41
  26.1 18.4 %collective-permute-start.2 = (bf16[128,896]{1,0:T(8,128)(2,1)}, bf16[128,896]{1,0:T(8,128)(2,1)S(1)}, u32[]{:S(2)}, u32[]{:S(2)}) collective-permute-start(bf16[128,896]{1,0:T(8,128)(2,1)} %own_ref.1), channel_id=1, source_target_pairs={{0,8},{4,12},{8,16},{12,20},{16,24},{20,28},{24,32},{28,36},{32,40... | collective-permute-start | bytes 688136 | tf_op jit(solution)/shard_map/ppermute | solution.py:41
  28.0 3.2 %collective-permute-start = (s32[2,2]{1,0:T(2,128)}, s32[2,2]{1,0:T(2,128)S(1)}, u32[]{:S(2)}, u32[]{:S(2)}) collective-permute-start(s32[2,2]{1,0:T(2,128)} %param.8), channel_id=1, source_target_pairs={{0,4},{4,0},{1,5},{5,1},{2,6},{6,2},{3,7},{7,3},{8,12},{12,8},{9,1... | collective-permute-start | bytes 56 | tf_op jit(solution)/shard_map/ppermute | solution.py:36
  39.8 4.7 %copy-start.1 = (bf16[128,896]{1,0:T(8,128)(2,1)S(1)}, bf16[128,896]{1,0:T(8,128)(2,1)}, u32[]{:S(2)}) copy-start(bf16[128,896]{1,0:T(8,128)(2,1)} %own_ref.1) | copy-start | bytes 688132
  39.8 7.5 %copy-start.4 = (bf16[128,512]{1,0:T(8,128)(2,1)S(1)}, bf16[128,512]{1,0:T(8,128)(2,1)}, u32[]{:S(2)}) copy-start(bf16[128,512]{1,0:T(8,128)(2,1)} %q_ref.1) | copy-start | bytes 393220
  39.8 7.5 %copy-start.5 = (bf16[128,512]{1,0:T(8,128)(2,1)S(1)}, bf16[128,512]{1,0:T(8,128)(2,1)}, u32[]{:S(2)}) copy-start(bf16[128,512]{1,0:T(8,128)(2,1)} %g_ref.1) | copy-start | bytes 393220
  39.8 10.6 %copy-start.8 = (s32[2,2]{1,0:T(2,128)S(1)}, s32[2,2]{1,0:T(2,128)}, u32[]{:S(2)}) copy-start(s32[2,2]{1,0:T(2,128)} %param.8) | copy-start | bytes 52
  39.8 15.5 %all-to-all-start.1 = ((bf16[4,256,512]{2,1,0:T(8,128)(2,1)}), bf16[4,256,512]{2,1,0:T(8,128)(2,1)S(1)}, u32[]{:S(2)}, u32[]{:S(2)}) async-start(bf16[4,256,512]{2,1,0:T(8,128)(2,1)} %shard_map.85), calls=%async_computation.1 | async-start | bytes 2097152 | tf_op jit(solution)/shard_map/all_to_all | solution.py:256
  45.4 5.3 %collective-permute-start.3 = (bf16[384,896]{1,0:T(8,128)(2,1)}, bf16[384,896]{1,0:T(8,128)(2,1)S(1)}, u32[]{:S(2)}, u32[]{:S(2)}) collective-permute-start(bf16[384,896]{1,0:T(8,128)(2,1)} %pad_maximum_fusion), channel_id=1, source_target_pairs={{0,4},{4,0},{1,5},{5,1},{2,6},{6,2},{3,7},{7,3},{8,12},{12,8},{9,1... | collective-permute-start | bytes 2064392 | tf_op jit(solution)/shard_map/ppermute | solution.py:36
  48.0 6.6 %collective-permute-start.4 = (bf16[128,512]{1,0:T(8,128)(2,1)}, bf16[128,512]{1,0:T(8,128)(2,1)}, u32[]{:S(2)}, u32[]{:S(2)}) collective-permute-start(bf16[128,512]{1,0:T(8,128)(2,1)} %get-tuple-element.30), channel_id=1, source_target_pairs={{0,4},{4,0},{1,5},{5,1},{2,6},{6,2},{3,7},{7,3},{8,12},{12,8},{9,1... | collective-permute-start | bytes 393224 | tf_op jit(solution)/shard_map/ppermute | solution.py:36
  51.5 1.1 copy-start.3
  60.3 1.9 %copy-start.6 = (bf16[128,512]{1,0:T(8,128)(2,1)}, bf16[128,512]{1,0:T(8,128)(2,1)S(1)}, u32[]{:S(2)}) copy-start(bf16[128,512]{1,0:T(8,128)(2,1)S(1)} %get-tuple-element.32) | copy-start | bytes 393220
  60.4 1.9 %copy-start = (bf16[4,256,512]{2,1,0:T(8,128)(2,1)}, bf16[4,256,512]{2,1,0:T(8,128)(2,1)S(1)}, u32[]{:S(2)}) copy-start(bf16[4,256,512]{2,1,0:T(8,128)(2,1)S(1)} %get-tuple-element.36) | copy-start | bytes 3145732
  62.3 6.0 %collective-permute-start.6 = (bf16[384,1024]{1,0:T(8,128)(2,1)}, bf16[384,1024]{1,0:T(8,128)(2,1)S(1)}, u32[]{:S(2)}, u32[]{:S(2)}) collective-permute-start(bf16[384,1024]{1,0:T(8,128)(2,1)} %get-tuple-element.39), channel_id=1, source_target_pairs={{0,4},{4,0},{1,5},{5,1},{2,6},{6,2},{3,7},{7,3},{8,12},{12,8},{9,1... | collective-permute-start | bytes 2359304 | tf_op jit(solution)/shard_map/ppermute | solution.py:36
  64.2 19.8 %all-to-all-start.2 = ((bf16[4,256,512]{2,1,0:T(8,128)(2,1)}), bf16[4,256,512]{2,1,0:T(8,128)(2,1)S(1)}, u32[]{:S(2)}, u32[]{:S(2)}) async-start(bf16[4,256,512]{2,1,0:T(8,128)(2,1)} %copy-done), calls=%async_computation.2 | async-start | bytes 2097152 | tf_op jit(solution)/shard_map/all_to_all | solution.py:282
  68.5 28.1 %copy-start.7 = (bf16[128,512]{1,0:T(8,128)(2,1)S(1)}, bf16[128,512]{1,0:T(8,128)(2,1)}, u32[]{:S(2)}) copy-start(bf16[128,512]{1,0:T(8,128)(2,1)} %copy-done.6) | copy-start | bytes 393220
  68.5 15.5 %collective-permute-start.7 = (bf16[384,256]{1,0:T(8,128)(2,1)S(1)}, bf16[384,256]{1,0:T(8,128)(2,1)S(1)}, u32[]{:S(2)}, u32[]{:S(2)}) collective-permute-start(bf16[384,256]{1,0:T(8,128)(2,1)S(1)} %get-tuple-element.41), channel_id=1, source_target_pairs={{0,1},{1,2},{2,3},{3,0},{4,5},{5,6},{6,7},{7,4},{8,9},{9,10},{10,1... | collective-permute-start | bytes 589832 | tf_op jit(solution)/shard_map/ppermute | solution.py:293
  71.0 13.0 %collective-permute-start.8 = (bf16[384,256]{1,0:T(8,128)(2,1)S(1)}, bf16[384,256]{1,0:T(8,128)(2,1)S(1)}, u32[]{:S(2)}, u32[]{:S(2)}) collective-permute-start(bf16[384,256]{1,0:T(8,128)(2,1)S(1)} %get-tuple-element.42), channel_id=1, source_target_pairs={{0,3},{1,0},{2,1},{3,2},{4,7},{5,4},{6,5},{7,6},{8,11},{9,8},{10,9... | collective-permute-start | bytes 589832 | tf_op jit(solution)/shard_map/ppermute | solution.py:293
  84.8 27.3 %all-to-all-start.3 = ((bf16[16,16,512]{2,1,0:T(8,128)(2,1)}), bf16[16,16,512]{2,1,0:T(8,128)(2,1)S(1)}, u32[]{:S(2)}, u32[]{:S(2)}) async-start(bf16[16,16,512]{2,1,0:T(8,128)(2,1)} %bitcast.5), calls=%async_computation.3 | async-start | bytes 524288 | tf_op jit(solution)/shard_map/all_to_all | solution.py:299
  93.2 9.6 %collective-permute-start.9 = (bf16[384,256]{1,0:T(8,128)(2,1)S(1)}, bf16[384,256]{1,0:T(8,128)(2,1)S(1)}, u32[]{:S(2)}, u32[]{:S(2)}) collective-permute-start(bf16[384,256]{1,0:T(8,128)(2,1)S(1)} %get-tuple-element.45), channel_id=1, source_target_pairs={{0,2},{1,3},{2,0},{3,1},{4,6},{5,7},{6,4},{7,5},{8,10},{9,11},{10,... | collective-permute-start | bytes 589832 | tf_op jit(solution)/shard_map/ppermute | solution.py:293
  96.5 3.2 %collective-permute-start.5 = (bf16[128,512]{1,0:T(8,128)(2,1)S(1)}, bf16[128,512]{1,0:T(8,128)(2,1)S(1)}, u32[]{:S(2)}, u32[]{:S(2)}) collective-permute-start(bf16[128,512]{1,0:T(8,128)(2,1)S(1)} %copy-done.7), channel_id=1, source_target_pairs={{0,4},{4,0},{1,5},{5,1},{2,6},{6,2},{3,7},{7,3},{8,12},{12,8},{9,1... | collective-permute-start | bytes 393224 | tf_op jit(solution)/shard_map/ppermute | solution.py:36
  102.9 11.7 %collective-permute-start.10 = (bf16[128,256]{1,0:T(8,128)(2,1)S(1)}, bf16[128,256]{1,0:T(8,128)(2,1)S(1)}, u32[]{:S(2)}, u32[]{:S(2)}) collective-permute-start(bf16[128,256]{1,0:T(8,128)(2,1)S(1)} %get-tuple-element.48), channel_id=1, source_target_pairs={{0,8},{4,12},{8,16},{12,20},{16,24},{20,28},{24,32},{28,36},{32,40... | collective-permute-start | bytes 196616 | tf_op jit(solution)/shard_map/ppermute | solution.py:41
  106.5 8.2 %collective-permute-start.11 = (bf16[128,256]{1,0:T(8,128)(2,1)S(1)}, bf16[128,256]{1,0:T(8,128)(2,1)S(1)}, u32[]{:S(2)}, u32[]{:S(2)}) collective-permute-start(bf16[128,256]{1,0:T(8,128)(2,1)S(1)} %get-tuple-element.49), channel_id=1, source_target_pairs={{0,504},{4,508},{8,0},{12,4},{16,8},{20,12},{24,16},{28,20},{32,24... | collective-permute-start | bytes 196616 | tf_op jit(solution)/shard_map/ppermute | solution.py:41
  (1 other events, 0.9 us)

commit v5 on v4

--- a/solution.py
+++ b/solution.py
@@ -173,9 +173,13 @@
     copies = []
     for part in range(NY):
         size = out_ref.shape[1]
-        rows = slice(part * size, (part + 1) * size)
-        product = lax.dot_general(x_ref[:, rows], cb_ref[...], TN, preferred_element_type=f32)
-        out_ref[part] = product.astype(b16)
+        if part % 2 == 0:
+            product = lax.dot_general(
+                x_ref[:, part * size : (part + 2) * size], cb_ref[...], TN,
+                preferred_element_type=f32,
+            )
+        first = part % 2 * size
+        out_ref[part] = product[first : first + size, :].astype(b16)
         copies.append(pltpu.make_async_copy(out_ref.at[part], share_ref.at[part], sems.at[part]))
         copies[-1].start()
     for copy in copies:
@@ -184,10 +188,9 @@
 
 def encoding_kernel(w_ref, cb_ref, keep_ref, send_ref):
     half = keep_ref.shape[0]
-    for out_ref, first in ((keep_ref, 0), (send_ref, half)):
-        out_ref[...] = lax.dot_general(
-            cb_ref[first : first + half, :], w_ref[...], NT, preferred_element_type=jnp.float32
-        ).astype(out_ref.dtype)
+    part = lax.dot_general(cb_ref[...], w_ref[...], NT, preferred_element_type=jnp.float32)
+    keep_ref[...] = part[:half, :].astype(keep_ref.dtype)
+    send_ref[...] = part[half:, :].astype(send_ref.dtype)
 
 
 def merge_kernel(x_ref, keep_ref, got_ref, *out_refs):
@@ -281,7 +284,8 @@
     )
     parts = lax.all_to_all(share, "y", 0, 0)
     ekeep, esend = small_call(
-        encoding_kernel, (), (w, after(contributions, share)), (shape(3 * NROWS, ROWS),) * 2,
+        encoding_kernel, (), (w, contributions),
+        (shape(3 * NROWS, ROWS),) * 2,
         limit=16,
     )
     got = swap_cores(esend)

time: 117 us -> 117 us (level)
  no operation moved by 1% of the time
where the time goes in v5:
time: 117 us; the launch traced here: 115 us
  starting transfers between devices  70.1 us (60%)
  waiting for transfers between devices  22.8 us (19%)
  Pallas kernels  13.6 us (12%)
  blocking collectives  3.89 us (3%)
  local copies, waits for them, and re-layouts  2.8 us (2%)
    ppermute x4, starting transfers between devices, shifted(): lax.ppermute(value, DP, [(i, (i + steps) % count) for i in range(count)])  18.6 us
    all_to_all x1, starting transfers between devices, per_device(): w = lax.all_to_all(copies, 'z', 0, 0).reshape(NZ * NC * PAD, SIDE)  15.2 us
    pallas_call x11, Pallas kernels, small_call(): pl.pallas_call(kernel, out_shape=outs, in_specs=[smem] * len(scalars) + [...  13.6 us
    ppermute x5, starting transfers between devices, swap_cores(): return lax.ppermute(value, 'c', [(0, 1), (1, 0)])  10.1 us
    all_to_all x1, waiting for transfers between devices, per_device(): parts = lax.all_to_all(share, 'y', 0, 0)  9.53 us
    ppermute x3, starting transfers between devices, per_device(): lax.ppermute(groups[step], 'x', [(i, (i + step) % NX) for i in range(NX)])  9.31 us
    all_to_all x1, starting transfers between devices, per_device(): parts = lax.all_to_all(total.reshape(NZ, NC * PAD, SIDE), 'z', 0, 0)  8.33 us
    all_to_all x1, waiting for transfers between devices, per_device(): w = lax.all_to_all(copies, 'z', 0, 0).reshape(NZ * NC * PAD, SIDE)  7.49 us
  transfers between devices with their start and end apart: 16, of which 6 were waited for; matrix products, arithmetic and copies ran while one was open for 2% of the time, Pallas kernels for 4%

profile of v5, /device:TPU:6, one launch (start us, length us, event | category | flops | bytes accessed | tf_op | source)
XLA Modules:
  0.0 115.1 jit_solution(16030166584663775835)
XLA Ops:
  0.6 2.0 %all-gather = bf16[14,2,512]{2,1,0:T(2,128)(2,1)S(1)} all-gather(bf16[7,2,512]{2,1,0:T(2,128)(2,1)} %param.7), channel_id=2, replica_groups=mesh['y'=4,'z'=16,'c'=2,'x'=4] {'c'}, dimensions={0}, use_global_device_ids=true | all-gather | bytes 43008 | tf_op jit(solution)/shard_map/all_gather | solution.py:244
  3.4 15.2 %all-to-all-start = ((bf16[16,16,512]{2,1,0:T(8,128)(2,1)}), bf16[16,16,512]{2,1,0:T(8,128)(2,1)S(1)}, u32[]{:S(2)}, u32[]{:S(2)}) async-start(bf16[16,16,512]{2,1,0:T(8,128)(2,1)} %shard_map.84), calls=%async_computation | async-start | bytes 524288 | tf_op jit(solution)/shard_map/all_to_all | solution.py:246
  18.6 7.5 %collective-permute-start.1 = (bf16[128,896]{1,0:T(8,128)(2,1)}, bf16[128,896]{1,0:T(8,128)(2,1)S(1)}, u32[]{:S(2)}, u32[]{:S(2)}) collective-permute-start(bf16[128,896]{1,0:T(8,128)(2,1)} %own_ref.1), channel_id=1, source_target_pairs={{0,504},{4,508},{8,0},{12,4},{16,8},{20,12},{24,16},{28,20},{32,24... | collective-permute-start | bytes 688136 | tf_op jit(solution)/shard_map/ppermute | solution.py:41
  26.1 1.9 %collective-permute-start.2 = (bf16[128,896]{1,0:T(8,128)(2,1)}, bf16[128,896]{1,0:T(8,128)(2,1)S(1)}, u32[]{:S(2)}, u32[]{:S(2)}) collective-permute-start(bf16[128,896]{1,0:T(8,128)(2,1)} %own_ref.1), channel_id=1, source_target_pairs={{0,8},{4,12},{8,16},{12,20},{16,24},{20,28},{24,32},{28,36},{32,40... | collective-permute-start | bytes 688136 | tf_op jit(solution)/shard_map/ppermute | solution.py:41
  28.0 1.9 %collective-permute-start = (s32[2,2]{1,0:T(2,128)}, s32[2,2]{1,0:T(2,128)S(1)}, u32[]{:S(2)}, u32[]{:S(2)}) collective-permute-start(s32[2,2]{1,0:T(2,128)} %param.8), channel_id=1, source_target_pairs={{0,4},{4,0},{1,5},{5,1},{2,6},{6,2},{3,7},{7,3},{8,12},{12,8},{9,1... | collective-permute-start | bytes 56 | tf_op jit(solution)/shard_map/ppermute | solution.py:36
  31.3 7.5 %all-to-all-done = bf16[16,16,512]{2,1,0:T(8,128)(2,1)S(1)} async-done(((bf16[16,16,512]{2,1,0:T(8,128)(2,1)}), bf16[16,16,512]{2,1,0:T(8,128)(2,1)S(1)}, u32[]{:S(2)}, u32[]{:S(2)}) %all-to-all-start) | async-done | bytes 262176 | tf_op jit(solution)/shard_map/all_to_all | solution.py:246
  39.8 4.6 %all-to-all-start.1 = ((bf16[4,256,512]{2,1,0:T(8,128)(2,1)}), bf16[4,256,512]{2,1,0:T(8,128)(2,1)S(1)}, u32[]{:S(2)}, u32[]{:S(2)}) async-start(bf16[4,256,512]{2,1,0:T(8,128)(2,1)} %shard_map.85), calls=%async_computation.1 | async-start | bytes 2097152 | tf_op jit(solution)/shard_map/all_to_all | solution.py:259
  45.4 1.9 %collective-permute-start.3 = (bf16[384,896]{1,0:T(8,128)(2,1)}, bf16[384,896]{1,0:T(8,128)(2,1)S(1)}, u32[]{:S(2)}, u32[]{:S(2)}) collective-permute-start(bf16[384,896]{1,0:T(8,128)(2,1)} %pad_maximum_fusion), channel_id=1, source_target_pairs={{0,4},{4,0},{1,5},{5,1},{2,6},{6,2},{3,7},{7,3},{8,12},{12,8},{9,1... | collective-permute-start | bytes 2064392 | tf_op jit(solution)/shard_map/ppermute | solution.py:36
  48.0 2.4 %collective-permute-start.4 = (bf16[128,512]{1,0:T(8,128)(2,1)}, bf16[128,512]{1,0:T(8,128)(2,1)}, u32[]{:S(2)}, u32[]{:S(2)}) collective-permute-start(bf16[128,512]{1,0:T(8,128)(2,1)} %get-tuple-element.29), channel_id=1, source_target_pairs={{0,4},{4,0},{1,5},{5,1},{2,6},{6,2},{3,7},{7,3},{8,12},{12,8},{9,1... | collective-permute-start | bytes 393224 | tf_op jit(solution)/shard_map/ppermute | solution.py:36
  52.6 1.9 %shard_map.86.x_ref = bf16[768,1024]{1,0:T(8,128)(2,1)S(1)} custom-call(bf16[128,896]{1,0:T(8,128)(2,1)S(1)} %copy-done.1, bf16[128,896]{1,0:T(8,128)(2,1)S(1)} %collective-permute-done.1.right_ref, bf16[128,896]{1,0:T(8,128)(2,1)S(1)} %collective-permute-done.2.left_ref, bf16[384,896]{1,0:T(8,128)(2,1)S(1)} %copy-done.3), custom_call_target="tpu_custom_call" | custom-call | flops 1000 | bytes 1000 | tf_op jit(solution)/shard_map/pallas_call | solution.py:52
  55.3 4.6 %shard_map.88 = (bf16[128,512]{1,0:T(8,128)(2,1)S(1)}, bf16[128,512]{1,0:T(8,128)(2,1)S(1)}, bf16[768,512]{1,0:T(8,128)(2,1)S(1)}, bf16[4,256,512]{2,1,0:T(8,128)(2,1)S(1)}) custom-call(s32[8]{0:T(128)S(1)} %fusion.sel_ref, bf16[768,1024]{1,0:T(8,128)(2,1)S(1)} %shard_map.86.x_ref, bf16[1024,512]{1,0:T(8,128)(2,1)S(1)} %bitcast.11, ...), custom_call_target="tpu_custom_call" | custom-call | flops 1000 | bytes 1000 | tf_op jit(solution)/shard_map/pallas_call | solution.py:52
  60.0 1.9 %shard_map.90 = (bf16[384,1024]{1,0:T(8,128)(2,1)S(1)}, bf16[384,1024]{1,0:T(8,128)(2,1)}) custom-call(bf16[1024,512]{1,0:T(8,128)(2,1)S(1)} %bitcast.12, bf16[768,512]{1,0:T(8,128)(2,1)S(1)} %get-tuple-element.34.cb_ref), custom_call_target="tpu_custom_call" | custom-call | flops 1000 | bytes 1000 | tf_op jit(solution)/shard_map/pallas_call | solution.py:52
  61.9 1.9 %collective-permute-start.6 = (bf16[384,1024]{1,0:T(8,128)(2,1)}, bf16[384,1024]{1,0:T(8,128)(2,1)S(1)}, u32[]{:S(2)}, u32[]{:S(2)}) collective-permute-start(bf16[384,1024]{1,0:T(8,128)(2,1)} %get-tuple-element.36), channel_id=1, source_target_pairs={{0,4},{4,0},{1,5},{5,1},{2,6},{6,2},{3,7},{7,3},{8,12},{12,8},{9,1... | collective-permute-start | bytes 2359304 | tf_op jit(solution)/shard_map/ppermute | solution.py:36
  63.9 4.0 %all-to-all-start.2 = ((bf16[4,256,512]{2,1,0:T(8,128)(2,1)}), bf16[4,256,512]{2,1,0:T(8,128)(2,1)S(1)}, u32[]{:S(2)}, u32[]{:S(2)}) async-start(bf16[4,256,512]{2,1,0:T(8,128)(2,1)} %copy-done), calls=%async_computation.2 | async-start | bytes 2097152 | tf_op jit(solution)/shard_map/all_to_all | solution.py:285
  68.1 2.5 %collective-permute-start.7 = (bf16[384,256]{1,0:T(8,128)(2,1)S(1)}, bf16[384,256]{1,0:T(8,128)(2,1)S(1)}, u32[]{:S(2)}, u32[]{:S(2)}) collective-permute-start(bf16[384,256]{1,0:T(8,128)(2,1)S(1)} %get-tuple-element.39), channel_id=1, source_target_pairs={{0,1},{1,2},{2,3},{3,0},{4,5},{5,6},{6,7},{7,4},{8,9},{9,10},{10,1... | collective-permute-start | bytes 589832 | tf_op jit(solution)/shard_map/ppermute | solution.py:297
  70.7 3.5 %collective-permute-start.8 = (bf16[384,256]{1,0:T(8,128)(2,1)S(1)}, bf16[384,256]{1,0:T(8,128)(2,1)S(1)}, u32[]{:S(2)}, u32[]{:S(2)}) collective-permute-start(bf16[384,256]{1,0:T(8,128)(2,1)S(1)} %get-tuple-element.40), channel_id=1, source_target_pairs={{0,3},{1,0},{2,1},{3,2},{4,7},{5,4},{6,5},{7,6},{8,11},{9,8},{10,9... | collective-permute-start | bytes 589832 | tf_op jit(solution)/shard_map/ppermute | solution.py:297
  74.1 9.5 %all-to-all-done.2.parts_ref = bf16[4,256,512]{2,1,0:T(8,128)(2,1)S(1)} async-done(((bf16[4,256,512]{2,1,0:T(8,128)(2,1)}), bf16[4,256,512]{2,1,0:T(8,128)(2,1)S(1)}, u32[]{:S(2)}, u32[]{:S(2)}) %all-to-all-start.2) | async-done | bytes 1048608 | tf_op jit(solution)/shard_map/all_to_all | solution.py:285
  84.5 8.3 %all-to-all-start.3 = ((bf16[16,16,512]{2,1,0:T(8,128)(2,1)}), bf16[16,16,512]{2,1,0:T(8,128)(2,1)S(1)}, u32[]{:S(2)}, u32[]{:S(2)}) async-start(bf16[16,16,512]{2,1,0:T(8,128)(2,1)} %bitcast.5), calls=%async_computation.3 | async-start | bytes 524288 | tf_op jit(solution)/shard_map/all_to_all | solution.py:303
  92.8 3.3 %collective-permute-start.9 = (bf16[384,256]{1,0:T(8,128)(2,1)S(1)}, bf16[384,256]{1,0:T(8,128)(2,1)S(1)}, u32[]{:S(2)}, u32[]{:S(2)}) collective-permute-start(bf16[384,256]{1,0:T(8,128)(2,1)S(1)} %get-tuple-element.43), channel_id=1, source_target_pairs={{0,2},{1,3},{2,0},{3,1},{4,6},{5,7},{6,4},{7,5},{8,10},{9,11},{10,... | collective-permute-start | bytes 589832 | tf_op jit(solution)/shard_map/ppermute | solution.py:297
  96.2 1.9 %collective-permute-start.5 = (bf16[128,512]{1,0:T(8,128)(2,1)S(1)}, bf16[128,512]{1,0:T(8,128)(2,1)S(1)}, u32[]{:S(2)}, u32[]{:S(2)}) collective-permute-start(bf16[128,512]{1,0:T(8,128)(2,1)S(1)} %copy-done.7), channel_id=1, source_target_pairs={{0,4},{4,0},{1,5},{5,1},{2,6},{6,2},{3,7},{7,3},{8,12},{12,8},{9,1... | collective-permute-start | bytes 393224 | tf_op jit(solution)/shard_map/ppermute | solution.py:36
  100.2 2.3 %collective-permute-done.9.c_ref = bf16[384,256]{1,0:T(8,128)(2,1)S(1)} collective-permute-done((bf16[384,256]{1,0:T(8,128)(2,1)S(1)}, bf16[384,256]{1,0:T(8,128)(2,1)S(1)}, u32[]{:S(2)}, u32[]{:S(2)}) %collective-permute-start.9) | collective-permute-done | bytes 196640 | tf_op jit(solution)/shard_map/ppermute | solution.py:297
  102.6 3.5 %collective-permute-start.10 = (bf16[128,256]{1,0:T(8,128)(2,1)S(1)}, bf16[128,256]{1,0:T(8,128)(2,1)S(1)}, u32[]{:S(2)}, u32[]{:S(2)}) collective-permute-start(bf16[128,256]{1,0:T(8,128)(2,1)S(1)} %get-tuple-element.46), channel_id=1, source_target_pairs={{0,8},{4,12},{8,16},{12,20},{16,24},{20,28},{24,32},{28,36},{32,40... | collective-permute-start | bytes 196616 | tf_op jit(solution)/shard_map/ppermute | solution.py:41
  106.1 5.6 %collective-permute-start.11 = (bf16[128,256]{1,0:T(8,128)(2,1)S(1)}, bf16[128,256]{1,0:T(8,128)(2,1)S(1)}, u32[]{:S(2)}, u32[]{:S(2)}) collective-permute-start(bf16[128,256]{1,0:T(8,128)(2,1)S(1)} %get-tuple-element.47), channel_id=1, source_target_pairs={{0,504},{4,508},{8,0},{12,4},{16,8},{20,12},{24,16},{28,20},{32,24... | collective-permute-start | bytes 196616 | tf_op jit(solution)/shard_map/ppermute | solution.py:41
  111.8 1.9 %all-gather.1 = f32[32,512]{1,0:T(8,128)S(1)} all-gather(f32[16,512]{1,0:T(8,128)S(1)} %convert_reduce_fusion), channel_id=3, replica_groups=mesh['y'=4,'z'=16,'c'=2,'x'=4] {'c'}, dimensions={0}, use_global_device_ids=true | all-gather | bytes 98304 | tf_op jit(solution)/shard_map/all_gather | solution.py:304
  (47 shorter events, 12.4 us)
Async XLA Ops:
  3.4 35.4 %all-to-all-start = ((bf16[16,16,512]{2,1,0:T(8,128)(2,1)}), bf16[16,16,512]{2,1,0:T(8,128)(2,1)S(1)}, u32[]{:S(2)}, u32[]{:S(2)}) async-start(bf16[16,16,512]{2,1,0:T(8,128)(2,1)} %shard_map.84), calls=%async_computation | async-start | bytes 524288 | tf_op jit(solution)/shard_map/all_to_all | solution.py:246
  18.6 25.8 %collective-permute-start.1 = (bf16[128,896]{1,0:T(8,128)(2,1)}, bf16[128,896]{1,0:T(8,128)(2,1)S(1)}, u32[]{:S(2)}, u32[]{:S(2)}) collective-permute-start(bf16[128,896]{1,0:T(8,128)(2,1)} %own_ref.1), channel_id=1, source_target_pairs={{0,504},{4,508},{8,0},{12,4},{16,8},{20,12},{24,16},{28,20},{32,24... | collective-permute-start | bytes 688136 | tf_op jit(solution)/shard_map/ppermute | solution.py:41
  26.1 18.4 %collective-permute-start.2 = (bf16[128,896]{1,0:T(8,128)(2,1)}, bf16[128,896]{1,0:T(8,128)(2,1)S(1)}, u32[]{:S(2)}, u32[]{:S(2)}) collective-permute-start(bf16[128,896]{1,0:T(8,128)(2,1)} %own_ref.1), channel_id=1, source_target_pairs={{0,8},{4,12},{8,16},{12,20},{16,24},{20,28},{24,32},{28,36},{32,40... | collective-permute-start | bytes 688136 | tf_op jit(solution)/shard_map/ppermute | solution.py:41
  28.0 3.2 %collective-permute-start = (s32[2,2]{1,0:T(2,128)}, s32[2,2]{1,0:T(2,128)S(1)}, u32[]{:S(2)}, u32[]{:S(2)}) collective-permute-start(s32[2,2]{1,0:T(2,128)} %param.8), channel_id=1, source_target_pairs={{0,4},{4,0},{1,5},{5,1},{2,6},{6,2},{3,7},{7,3},{8,12},{12,8},{9,1... | collective-permute-start | bytes 56 | tf_op jit(solution)/shard_map/ppermute | solution.py:36
  39.8 4.7 %copy-start.1 = (bf16[128,896]{1,0:T(8,128)(2,1)S(1)}, bf16[128,896]{1,0:T(8,128)(2,1)}, u32[]{:S(2)}) copy-start(bf16[128,896]{1,0:T(8,128)(2,1)} %own_ref.1) | copy-start | bytes 688132
  39.8 7.5 %copy-start.4 = (bf16[128,512]{1,0:T(8,128)(2,1)S(1)}, bf16[128,512]{1,0:T(8,128)(2,1)}, u32[]{:S(2)}) copy-start(bf16[128,512]{1,0:T(8,128)(2,1)} %q_ref.1) | copy-start | bytes 393220
  39.8 7.5 %copy-start.5 = (bf16[128,512]{1,0:T(8,128)(2,1)S(1)}, bf16[128,512]{1,0:T(8,128)(2,1)}, u32[]{:S(2)}) copy-start(bf16[128,512]{1,0:T(8,128)(2,1)} %g_ref.1) | copy-start | bytes 393220
  39.8 10.6 %copy-start.8 = (s32[2,2]{1,0:T(2,128)S(1)}, s32[2,2]{1,0:T(2,128)}, u32[]{:S(2)}) copy-start(s32[2,2]{1,0:T(2,128)} %param.8) | copy-start | bytes 52
  39.8 15.5 %all-to-all-start.1 = ((bf16[4,256,512]{2,1,0:T(8,128)(2,1)}), bf16[4,256,512]{2,1,0:T(8,128)(2,1)S(1)}, u32[]{:S(2)}, u32[]{:S(2)}) async-start(bf16[4,256,512]{2,1,0:T(8,128)(2,1)} %shard_map.85), calls=%async_computation.1 | async-start | bytes 2097152 | tf_op jit(solution)/shard_map/all_to_all | solution.py:259
  45.4 5.3 %collective-permute-start.3 = (bf16[384,896]{1,0:T(8,128)(2,1)}, bf16[384,896]{1,0:T(8,128)(2,1)S(1)}, u32[]{:S(2)}, u32[]{:S(2)}) collective-permute-start(bf16[384,896]{1,0:T(8,128)(2,1)} %pad_maximum_fusion), channel_id=1, source_target_pairs={{0,4},{4,0},{1,5},{5,1},{2,6},{6,2},{3,7},{7,3},{8,12},{12,8},{9,1... | collective-permute-start | bytes 2064392 | tf_op jit(solution)/shard_map/ppermute | solution.py:36
  48.0 6.6 %collective-permute-start.4 = (bf16[128,512]{1,0:T(8,128)(2,1)}, bf16[128,512]{1,0:T(8,128)(2,1)}, u32[]{:S(2)}, u32[]{:S(2)}) collective-permute-start(bf16[128,512]{1,0:T(8,128)(2,1)} %get-tuple-element.29), channel_id=1, source_target_pairs={{0,4},{4,0},{1,5},{5,1},{2,6},{6,2},{3,7},{7,3},{8,12},{12,8},{9,1... | collective-permute-start | bytes 393224 | tf_op jit(solution)/shard_map/ppermute | solution.py:36
  51.5 1.1 copy-start.3
  60.0 1.9 %copy-start.6 = (bf16[128,512]{1,0:T(8,128)(2,1)}, bf16[128,512]{1,0:T(8,128)(2,1)S(1)}, u32[]{:S(2)}) copy-start(bf16[128,512]{1,0:T(8,128)(2,1)S(1)} %get-tuple-element.31) | copy-start | bytes 393220
  60.0 3.8 %copy-start = (bf16[4,256,512]{2,1,0:T(8,128)(2,1)}, bf16[4,256,512]{2,1,0:T(8,128)(2,1)S(1)}, u32[]{:S(2)}) copy-start(bf16[4,256,512]{2,1,0:T(8,128)(2,1)S(1)} %get-tuple-element.38) | copy-start | bytes 3145732
  61.9 6.0 %collective-permute-start.6 = (bf16[384,1024]{1,0:T(8,128)(2,1)}, bf16[384,1024]{1,0:T(8,128)(2,1)S(1)}, u32[]{:S(2)}, u32[]{:S(2)}) collective-permute-start(bf16[384,1024]{1,0:T(8,128)(2,1)} %get-tuple-element.36), channel_id=1, source_target_pairs={{0,4},{4,0},{1,5},{5,1},{2,6},{6,2},{3,7},{7,3},{8,12},{12,8},{9,1... | collective-permute-start | bytes 2359304 | tf_op jit(solution)/shard_map/ppermute | solution.py:36
  63.9 19.8 %all-to-all-start.2 = ((bf16[4,256,512]{2,1,0:T(8,128)(2,1)}), bf16[4,256,512]{2,1,0:T(8,128)(2,1)S(1)}, u32[]{:S(2)}, u32[]{:S(2)}) async-start(bf16[4,256,512]{2,1,0:T(8,128)(2,1)} %copy-done), calls=%async_computation.2 | async-start | bytes 2097152 | tf_op jit(solution)/shard_map/all_to_all | solution.py:285
  68.1 28.1 %copy-start.7 = (bf16[128,512]{1,0:T(8,128)(2,1)S(1)}, bf16[128,512]{1,0:T(8,128)(2,1)}, u32[]{:S(2)}) copy-start(bf16[128,512]{1,0:T(8,128)(2,1)} %copy-done.6) | copy-start | bytes 393220
  68.1 15.5 %collective-permute-start.7 = (bf16[384,256]{1,0:T(8,128)(2,1)S(1)}, bf16[384,256]{1,0:T(8,128)(2,1)S(1)}, u32[]{:S(2)}, u32[]{:S(2)}) collective-permute-start(bf16[384,256]{1,0:T(8,128)(2,1)S(1)} %get-tuple-element.39), channel_id=1, source_target_pairs={{0,1},{1,2},{2,3},{3,0},{4,5},{5,6},{6,7},{7,4},{8,9},{9,10},{10,1... | collective-permute-start | bytes 589832 | tf_op jit(solution)/shard_map/ppermute | solution.py:297
  70.7 13.0 %collective-permute-start.8 = (bf16[384,256]{1,0:T(8,128)(2,1)S(1)}, bf16[384,256]{1,0:T(8,128)(2,1)S(1)}, u32[]{:S(2)}, u32[]{:S(2)}) collective-permute-start(bf16[384,256]{1,0:T(8,128)(2,1)S(1)} %get-tuple-element.40), channel_id=1, source_target_pairs={{0,3},{1,0},{2,1},{3,2},{4,7},{5,4},{6,5},{7,6},{8,11},{9,8},{10,9... | collective-permute-start | bytes 589832 | tf_op jit(solution)/shard_map/ppermute | solution.py:297
  84.5 27.3 %all-to-all-start.3 = ((bf16[16,16,512]{2,1,0:T(8,128)(2,1)}), bf16[16,16,512]{2,1,0:T(8,128)(2,1)S(1)}, u32[]{:S(2)}, u32[]{:S(2)}) async-start(bf16[16,16,512]{2,1,0:T(8,128)(2,1)} %bitcast.5), calls=%async_computation.3 | async-start | bytes 524288 | tf_op jit(solution)/shard_map/all_to_all | solution.py:303
  92.8 9.6 %collective-permute-start.9 = (bf16[384,256]{1,0:T(8,128)(2,1)S(1)}, bf16[384,256]{1,0:T(8,128)(2,1)S(1)}, u32[]{:S(2)}, u32[]{:S(2)}) collective-permute-start(bf16[384,256]{1,0:T(8,128)(2,1)S(1)} %get-tuple-element.43), channel_id=1, source_target_pairs={{0,2},{1,3},{2,0},{3,1},{4,6},{5,7},{6,4},{7,5},{8,10},{9,11},{10,... | collective-permute-start | bytes 589832 | tf_op jit(solution)/shard_map/ppermute | solution.py:297
  96.2 3.2 %collective-permute-start.5 = (bf16[128,512]{1,0:T(8,128)(2,1)S(1)}, bf16[128,512]{1,0:T(8,128)(2,1)S(1)}, u32[]{:S(2)}, u32[]{:S(2)}) collective-permute-start(bf16[128,512]{1,0:T(8,128)(2,1)S(1)} %copy-done.7), channel_id=1, source_target_pairs={{0,4},{4,0},{1,5},{5,1},{2,6},{6,2},{3,7},{7,3},{8,12},{12,8},{9,1... | collective-permute-start | bytes 393224 | tf_op jit(solution)/shard_map/ppermute | solution.py:36
  102.6 11.7 %collective-permute-start.10 = (bf16[128,256]{1,0:T(8,128)(2,1)S(1)}, bf16[128,256]{1,0:T(8,128)(2,1)S(1)}, u32[]{:S(2)}, u32[]{:S(2)}) collective-permute-start(bf16[128,256]{1,0:T(8,128)(2,1)S(1)} %get-tuple-element.46), channel_id=1, source_target_pairs={{0,8},{4,12},{8,16},{12,20},{16,24},{20,28},{24,32},{28,36},{32,40... | collective-permute-start | bytes 196616 | tf_op jit(solution)/shard_map/ppermute | solution.py:41
  106.1 8.2 %collective-permute-start.11 = (bf16[128,256]{1,0:T(8,128)(2,1)S(1)}, bf16[128,256]{1,0:T(8,128)(2,1)S(1)}, u32[]{:S(2)}, u32[]{:S(2)}) collective-permute-start(bf16[128,256]{1,0:T(8,128)(2,1)S(1)} %get-tuple-element.47), channel_id=1, source_target_pairs={{0,504},{4,508},{8,0},{12,4},{16,8},{20,12},{24,16},{28,20},{32,24... | collective-permute-start | bytes 196616 | tf_op jit(solution)/shard_map/ppermute | solution.py:41
  (1 other events, 0.9 us)

commit v6 on v5

--- a/solution.py
+++ b/solution.py
@@ -156,12 +156,6 @@
     dscores = [
         (a * (b - c) * factor).astype(b16) for a, b, c in zip(probs, dprobs, delta)
     ]
-    for i, (span, _) in enumerate(units):
-        to_ref = mine_ref if span < 2 else back_ref
-        out = jnp.dot(probs_b[i], v[i], preferred_element_type=f32)
-        to_ref[rows[i], kcols[i]] = out.astype(b16)
-        out = jnp.dot(dscores[i], k[i], preferred_element_type=f32)
-        to_ref[rows[i], vcols[i]] = out.astype(b16)
     vgrad = [lax.dot_general(a, b, TN, preferred_element_type=f32) for a, b in zip(probs_b, g)]
     kgrad = [lax.dot_general(a, b, TN, preferred_element_type=f32) for a, b in zip(dscores, q)]
     for i in range(len(units)):
@@ -182,6 +176,12 @@
         out_ref[part] = product[first : first + size, :].astype(b16)
         copies.append(pltpu.make_async_copy(out_ref.at[part], share_ref.at[part], sems.at[part]))
         copies[-1].start()
+    for i, (span, _) in enumerate(units):
+        to_ref = mine_ref if span < 2 else back_ref
+        out = jnp.dot(probs_b[i], v[i], preferred_element_type=f32)
+        to_ref[rows[i], kcols[i]] = out.astype(b16)
+        out = jnp.dot(dscores[i], k[i], preferred_element_type=f32)
+        to_ref[rows[i], vcols[i]] = out.astype(b16)
     for copy in copies:
         copy.wait()
 

time: 117 us -> 117 us (level)
  no operation moved by 1% of the time
where the time goes in v6:
time: 117 us; the launch traced here: 115 us
  starting transfers between devices  70.1 us (60%)
  waiting for transfers between devices  22.8 us (19%)
  Pallas kernels  13.8 us (12%)
  blocking collectives  3.89 us (3%)
  local copies, waits for them, and re-layouts  2.8 us (2%)
    ppermute x4, starting transfers between devices, shifted(): lax.ppermute(value, DP, [(i, (i + steps) % count) for i in range(count)])  18.6 us
    all_to_all x1, starting transfers between devices, per_device(): w = lax.all_to_all(copies, 'z', 0, 0).reshape(NZ * NC * PAD, SIDE)  15.2 us
    pallas_call x11, Pallas kernels, small_call(): pl.pallas_call(kernel, out_shape=outs, in_specs=[smem] * len(scalars) + [...  13.8 us
    ppermute x5, starting transfers between devices, swap_cores(): return lax.ppermute(value, 'c', [(0, 1), (1, 0)])  10.1 us
    all_to_all x1, waiting for transfers between devices, per_device(): parts = lax.all_to_all(share, 'y', 0, 0)  9.54 us
    ppermute x3, starting transfers between devices, per_device(): lax.ppermute(groups[step], 'x', [(i, (i + step) % NX) for i in range(NX)])  9.31 us
    all_to_all x1, starting transfers between devices, per_device(): parts = lax.all_to_all(total.reshape(NZ, NC * PAD, SIDE), 'z', 0, 0)  8.33 us
    all_to_all x1, waiting for transfers between devices, per_device(): w = lax.all_to_all(copies, 'z', 0, 0).reshape(NZ * NC * PAD, SIDE)  7.49 us
  transfers between devices with their start and end apart: 16, of which 6 were waited for; matrix products, arithmetic and copies ran while one was open for 2% of the time, Pallas kernels for 4%

profile of v6, /device:TPU:6, one launch (start us, length us, event | category | flops | bytes accessed | tf_op | source)
XLA Modules:
  0.0 115.4 jit_solution(639096905133403852)
XLA Ops:
  0.6 2.0 %all-gather = bf16[14,2,512]{2,1,0:T(2,128)(2,1)S(1)} all-gather(bf16[7,2,512]{2,1,0:T(2,128)(2,1)} %param.7), channel_id=2, replica_groups=mesh['y'=4,'z'=16,'c'=2,'x'=4] {'c'}, dimensions={0}, use_global_device_ids=true | all-gather | bytes 43008 | tf_op jit(solution)/shard_map/all_gather | solution.py:244
  3.4 15.2 %all-to-all-start = ((bf16[16,16,512]{2,1,0:T(8,128)(2,1)}), bf16[16,16,512]{2,1,0:T(8,128)(2,1)S(1)}, u32[]{:S(2)}, u32[]{:S(2)}) async-start(bf16[16,16,512]{2,1,0:T(8,128)(2,1)} %shard_map.84), calls=%async_computation | async-start | bytes 524288 | tf_op jit(solution)/shard_map/all_to_all | solution.py:246
  18.6 7.5 %collective-permute-start.1 = (bf16[128,896]{1,0:T(8,128)(2,1)}, bf16[128,896]{1,0:T(8,128)(2,1)S(1)}, u32[]{:S(2)}, u32[]{:S(2)}) collective-permute-start(bf16[128,896]{1,0:T(8,128)(2,1)} %own_ref.1), channel_id=1, source_target_pairs={{0,504},{4,508},{8,0},{12,4},{16,8},{20,12},{24,16},{28,20},{32,24... | collective-permute-start | bytes 688136 | tf_op jit(solution)/shard_map/ppermute | solution.py:41
  26.1 1.9 %collective-permute-start.2 = (bf16[128,896]{1,0:T(8,128)(2,1)}, bf16[128,896]{1,0:T(8,128)(2,1)S(1)}, u32[]{:S(2)}, u32[]{:S(2)}) collective-permute-start(bf16[128,896]{1,0:T(8,128)(2,1)} %own_ref.1), channel_id=1, source_target_pairs={{0,8},{4,12},{8,16},{12,20},{16,24},{20,28},{24,32},{28,36},{32,40... | collective-permute-start | bytes 688136 | tf_op jit(solution)/shard_map/ppermute | solution.py:41
  28.0 1.9 %collective-permute-start = (s32[2,2]{1,0:T(2,128)}, s32[2,2]{1,0:T(2,128)S(1)}, u32[]{:S(2)}, u32[]{:S(2)}) collective-permute-start(s32[2,2]{1,0:T(2,128)} %param.8), channel_id=1, source_target_pairs={{0,4},{4,0},{1,5},{5,1},{2,6},{6,2},{3,7},{7,3},{8,12},{12,8},{9,1... | collective-permute-start | bytes 56 | tf_op jit(solution)/shard_map/ppermute | solution.py:36
  31.3 7.5 %all-to-all-done = bf16[16,16,512]{2,1,0:T(8,128)(2,1)S(1)} async-done(((bf16[16,16,512]{2,1,0:T(8,128)(2,1)}), bf16[16,16,512]{2,1,0:T(8,128)(2,1)S(1)}, u32[]{:S(2)}, u32[]{:S(2)}) %all-to-all-start) | async-done | bytes 262176 | tf_op jit(solution)/shard_map/all_to_all | solution.py:246
  39.8 4.6 %all-to-all-start.1 = ((bf16[4,256,512]{2,1,0:T(8,128)(2,1)}), bf16[4,256,512]{2,1,0:T(8,128)(2,1)S(1)}, u32[]{:S(2)}, u32[]{:S(2)}) async-start(bf16[4,256,512]{2,1,0:T(8,128)(2,1)} %shard_map.85), calls=%async_computation.1 | async-start | bytes 2097152 | tf_op jit(solution)/shard_map/all_to_all | solution.py:259
  45.4 1.9 %collective-permute-start.3 = (bf16[384,896]{1,0:T(8,128)(2,1)}, bf16[384,896]{1,0:T(8,128)(2,1)S(1)}, u32[]{:S(2)}, u32[]{:S(2)}) collective-permute-start(bf16[384,896]{1,0:T(8,128)(2,1)} %pad_maximum_fusion), channel_id=1, source_target_pairs={{0,4},{4,0},{1,5},{5,1},{2,6},{6,2},{3,7},{7,3},{8,12},{12,8},{9,1... | collective-permute-start | bytes 2064392 | tf_op jit(solution)/shard_map/ppermute | solution.py:36
  48.0 2.4 %collective-permute-start.4 = (bf16[128,512]{1,0:T(8,128)(2,1)}, bf16[128,512]{1,0:T(8,128)(2,1)}, u32[]{:S(2)}, u32[]{:S(2)}) collective-permute-start(bf16[128,512]{1,0:T(8,128)(2,1)} %get-tuple-element.29), channel_id=1, source_target_pairs={{0,4},{4,0},{1,5},{5,1},{2,6},{6,2},{3,7},{7,3},{8,12},{12,8},{9,1... | collective-permute-start | bytes 393224 | tf_op jit(solution)/shard_map/ppermute | solution.py:36
  52.6 1.9 %shard_map.86.x_ref = bf16[768,1024]{1,0:T(8,128)(2,1)S(1)} custom-call(bf16[128,896]{1,0:T(8,128)(2,1)S(1)} %copy-done.1, bf16[128,896]{1,0:T(8,128)(2,1)S(1)} %collective-permute-done.1.right_ref, bf16[128,896]{1,0:T(8,128)(2,1)S(1)} %collective-permute-done.2.left_ref, bf16[384,896]{1,0:T(8,128)(2,1)S(1)} %copy-done.3), custom_call_target="tpu_custom_call" | custom-call | flops 1000 | bytes 1000 | tf_op jit(solution)/shard_map/pallas_call | solution.py:52
  55.3 4.9 %shard_map.88 = (bf16[128,512]{1,0:T(8,128)(2,1)S(1)}, bf16[128,512]{1,0:T(8,128)(2,1)S(1)}, bf16[768,512]{1,0:T(8,128)(2,1)S(1)}, bf16[4,256,512]{2,1,0:T(8,128)(2,1)S(1)}) custom-call(s32[8]{0:T(128)S(1)} %fusion.sel_ref, bf16[768,1024]{1,0:T(8,128)(2,1)S(1)} %shard_map.86.x_ref, bf16[1024,512]{1,0:T(8,128)(2,1)S(1)} %bitcast.11, ...), custom_call_target="tpu_custom_call" | custom-call | flops 1000 | bytes 1000 | tf_op jit(solution)/shard_map/pallas_call | solution.py:52
  60.3 1.9 %shard_map.90 = (bf16[384,1024]{1,0:T(8,128)(2,1)S(1)}, bf16[384,1024]{1,0:T(8,128)(2,1)}) custom-call(bf16[1024,512]{1,0:T(8,128)(2,1)S(1)} %bitcast.12, bf16[768,512]{1,0:T(8,128)(2,1)S(1)} %get-tuple-element.34.cb_ref), custom_call_target="tpu_custom_call" | custom-call | flops 1000 | bytes 1000 | tf_op jit(solution)/shard_map/pallas_call | solution.py:52
  62.2 1.9 %collective-permute-start.6 = (bf16[384,1024]{1,0:T(8,128)(2,1)}, bf16[384,1024]{1,0:T(8,128)(2,1)S(1)}, u32[]{:S(2)}, u32[]{:S(2)}) collective-permute-start(bf16[384,1024]{1,0:T(8,128)(2,1)} %get-tuple-element.36), channel_id=1, source_target_pairs={{0,4},{4,0},{1,5},{5,1},{2,6},{6,2},{3,7},{7,3},{8,12},{12,8},{9,1... | collective-permute-start | bytes 2359304 | tf_op jit(solution)/shard_map/ppermute | solution.py:36
  64.1 4.0 %all-to-all-start.2 = ((bf16[4,256,512]{2,1,0:T(8,128)(2,1)}), bf16[4,256,512]{2,1,0:T(8,128)(2,1)S(1)}, u32[]{:S(2)}, u32[]{:S(2)}) async-start(bf16[4,256,512]{2,1,0:T(8,128)(2,1)} %copy-done), calls=%async_computation.2 | async-start | bytes 2097152 | tf_op jit(solution)/shard_map/all_to_all | solution.py:285
  68.4 2.5 %collective-permute-start.7 = (bf16[384,256]{1,0:T(8,128)(2,1)S(1)}, bf16[384,256]{1,0:T(8,128)(2,1)S(1)}, u32[]{:S(2)}, u32[]{:S(2)}) collective-permute-start(bf16[384,256]{1,0:T(8,128)(2,1)S(1)} %get-tuple-element.39), channel_id=1, source_target_pairs={{0,1},{1,2},{2,3},{3,0},{4,5},{5,6},{6,7},{7,4},{8,9},{9,10},{10,1... | collective-permute-start | bytes 589832 | tf_op jit(solution)/shard_map/ppermute | solution.py:297
  70.9 3.5 %collective-permute-start.8 = (bf16[384,256]{1,0:T(8,128)(2,1)S(1)}, bf16[384,256]{1,0:T(8,128)(2,1)S(1)}, u32[]{:S(2)}, u32[]{:S(2)}) collective-permute-start(bf16[384,256]{1,0:T(8,128)(2,1)S(1)} %get-tuple-element.40), channel_id=1, source_target_pairs={{0,3},{1,0},{2,1},{3,2},{4,7},{5,4},{6,5},{7,6},{8,11},{9,8},{10,9... | collective-permute-start | bytes 589832 | tf_op jit(solution)/shard_map/ppermute | solution.py:297
  74.4 9.5 %all-to-all-done.2.parts_ref = bf16[4,256,512]{2,1,0:T(8,128)(2,1)S(1)} async-done(((bf16[4,256,512]{2,1,0:T(8,128)(2,1)}), bf16[4,256,512]{2,1,0:T(8,128)(2,1)S(1)}, u32[]{:S(2)}, u32[]{:S(2)}) %all-to-all-start.2) | async-done | bytes 1048608 | tf_op jit(solution)/shard_map/all_to_all | solution.py:285
  84.8 8.3 %all-to-all-start.3 = ((bf16[16,16,512]{2,1,0:T(8,128)(2,1)}), bf16[16,16,512]{2,1,0:T(8,128)(2,1)S(1)}, u32[]{:S(2)}, u32[]{:S(2)}) async-start(bf16[16,16,512]{2,1,0:T(8,128)(2,1)} %bitcast.5), calls=%async_computation.3 | async-start | bytes 524288 | tf_op jit(solution)/shard_map/all_to_all | solution.py:303
  93.1 3.3 %collective-permute-start.9 = (bf16[384,256]{1,0:T(8,128)(2,1)S(1)}, bf16[384,256]{1,0:T(8,128)(2,1)S(1)}, u32[]{:S(2)}, u32[]{:S(2)}) collective-permute-start(bf16[384,256]{1,0:T(8,128)(2,1)S(1)} %get-tuple-element.43), channel_id=1, source_target_pairs={{0,2},{1,3},{2,0},{3,1},{4,6},{5,7},{6,4},{7,5},{8,10},{9,11},{10,... | collective-permute-start | bytes 589832 | tf_op jit(solution)/shard_map/ppermute | solution.py:297
  96.5 1.9 %collective-permute-start.5 = (bf16[128,512]{1,0:T(8,128)(2,1)S(1)}, bf16[128,512]{1,0:T(8,128)(2,1)S(1)}, u32[]{:S(2)}, u32[]{:S(2)}) collective-permute-start(bf16[128,512]{1,0:T(8,128)(2,1)S(1)} %copy-done.7), channel_id=1, source_target_pairs={{0,4},{4,0},{1,5},{5,1},{2,6},{6,2},{3,7},{7,3},{8,12},{12,8},{9,1... | collective-permute-start | bytes 393224 | tf_op jit(solution)/shard_map/ppermute | solution.py:36
  100.4 2.3 %collective-permute-done.9.c_ref = bf16[384,256]{1,0:T(8,128)(2,1)S(1)} collective-permute-done((bf16[384,256]{1,0:T(8,128)(2,1)S(1)}, bf16[384,256]{1,0:T(8,128)(2,1)S(1)}, u32[]{:S(2)}, u32[]{:S(2)}) %collective-permute-start.9) | collective-permute-done | bytes 196640 | tf_op jit(solution)/shard_map/ppermute | solution.py:297
  102.9 3.5 %collective-permute-start.10 = (bf16[128,256]{1,0:T(8,128)(2,1)S(1)}, bf16[128,256]{1,0:T(8,128)(2,1)S(1)}, u32[]{:S(2)}, u32[]{:S(2)}) collective-permute-start(bf16[128,256]{1,0:T(8,128)(2,1)S(1)} %get-tuple-element.46), channel_id=1, source_target_pairs={{0,8},{4,12},{8,16},{12,20},{16,24},{20,28},{24,32},{28,36},{32,40... | collective-permute-start | bytes 196616 | tf_op jit(solution)/shard_map/ppermute | solution.py:41
  106.4 5.6 %collective-permute-start.11 = (bf16[128,256]{1,0:T(8,128)(2,1)S(1)}, bf16[128,256]{1,0:T(8,128)(2,1)S(1)}, u32[]{:S(2)}, u32[]{:S(2)}) collective-permute-start(bf16[128,256]{1,0:T(8,128)(2,1)S(1)} %get-tuple-element.47), channel_id=1, source_target_pairs={{0,504},{4,508},{8,0},{12,4},{16,8},{20,12},{24,16},{28,20},{32,24... | collective-permute-start | bytes 196616 | tf_op jit(solution)/shard_map/ppermute | solution.py:41
  112.1 1.9 %all-gather.1 = f32[32,512]{1,0:T(8,128)S(1)} all-gather(f32[16,512]{1,0:T(8,128)S(1)} %convert_reduce_fusion), channel_id=3, replica_groups=mesh['y'=4,'z'=16,'c'=2,'x'=4] {'c'}, dimensions={0}, use_global_device_ids=true | all-gather | bytes 98304 | tf_op jit(solution)/shard_map/all_gather | solution.py:304
  (47 shorter events, 12.4 us)
Async XLA Ops:
  3.4 35.4 %all-to-all-start = ((bf16[16,16,512]{2,1,0:T(8,128)(2,1)}), bf16[16,16,512]{2,1,0:T(8,128)(2,1)S(1)}, u32[]{:S(2)}, u32[]{:S(2)}) async-start(bf16[16,16,512]{2,1,0:T(8,128)(2,1)} %shard_map.84), calls=%async_computation | async-start | bytes 524288 | tf_op jit(solution)/shard_map/all_to_all | solution.py:246
  18.6 25.8 %collective-permute-start.1 = (bf16[128,896]{1,0:T(8,128)(2,1)}, bf16[128,896]{1,0:T(8,128)(2,1)S(1)}, u32[]{:S(2)}, u32[]{:S(2)}) collective-permute-start(bf16[128,896]{1,0:T(8,128)(2,1)} %own_ref.1), channel_id=1, source_target_pairs={{0,504},{4,508},{8,0},{12,4},{16,8},{20,12},{24,16},{28,20},{32,24... | collective-permute-start | bytes 688136 | tf_op jit(solution)/shard_map/ppermute | solution.py:41
  26.1 18.4 %collective-permute-start.2 = (bf16[128,896]{1,0:T(8,128)(2,1)}, bf16[128,896]{1,0:T(8,128)(2,1)S(1)}, u32[]{:S(2)}, u32[]{:S(2)}) collective-permute-start(bf16[128,896]{1,0:T(8,128)(2,1)} %own_ref.1), channel_id=1, source_target_pairs={{0,8},{4,12},{8,16},{12,20},{16,24},{20,28},{24,32},{28,36},{32,40... | collective-permute-start | bytes 688136 | tf_op jit(solution)/shard_map/ppermute | solution.py:41
  28.0 3.2 %collective-permute-start = (s32[2,2]{1,0:T(2,128)}, s32[2,2]{1,0:T(2,128)S(1)}, u32[]{:S(2)}, u32[]{:S(2)}) collective-permute-start(s32[2,2]{1,0:T(2,128)} %param.8), channel_id=1, source_target_pairs={{0,4},{4,0},{1,5},{5,1},{2,6},{6,2},{3,7},{7,3},{8,12},{12,8},{9,1... | collective-permute-start | bytes 56 | tf_op jit(solution)/shard_map/ppermute | solution.py:36
  39.8 4.7 %copy-start.1 = (bf16[128,896]{1,0:T(8,128)(2,1)S(1)}, bf16[128,896]{1,0:T(8,128)(2,1)}, u32[]{:S(2)}) copy-start(bf16[128,896]{1,0:T(8,128)(2,1)} %own_ref.1) | copy-start | bytes 688132
  39.8 7.5 %copy-start.4 = (bf16[128,512]{1,0:T(8,128)(2,1)S(1)}, bf16[128,512]{1,0:T(8,128)(2,1)}, u32[]{:S(2)}) copy-start(bf16[128,512]{1,0:T(8,128)(2,1)} %q_ref.1) | copy-start | bytes 393220
  39.8 7.5 %copy-start.5 = (bf16[128,512]{1,0:T(8,128)(2,1)S(1)}, bf16[128,512]{1,0:T(8,128)(2,1)}, u32[]{:S(2)}) copy-start(bf16[128,512]{1,0:T(8,128)(2,1)} %g_ref.1) | copy-start | bytes 393220
  39.8 10.6 %copy-start.8 = (s32[2,2]{1,0:T(2,128)S(1)}, s32[2,2]{1,0:T(2,128)}, u32[]{:S(2)}) copy-start(s32[2,2]{1,0:T(2,128)} %param.8) | copy-start | bytes 52
  39.8 15.5 %all-to-all-start.1 = ((bf16[4,256,512]{2,1,0:T(8,128)(2,1)}), bf16[4,256,512]{2,1,0:T(8,128)(2,1)S(1)}, u32[]{:S(2)}, u32[]{:S(2)}) async-start(bf16[4,256,512]{2,1,0:T(8,128)(2,1)} %shard_map.85), calls=%async_computation.1 | async-start | bytes 2097152 | tf_op jit(solution)/shard_map/all_to_all | solution.py:259
  45.4 5.3 %collective-permute-start.3 = (bf16[384,896]{1,0:T(8,128)(2,1)}, bf16[384,896]{1,0:T(8,128)(2,1)S(1)}, u32[]{:S(2)}, u32[]{:S(2)}) collective-permute-start(bf16[384,896]{1,0:T(8,128)(2,1)} %pad_maximum_fusion), channel_id=1, source_target_pairs={{0,4},{4,0},{1,5},{5,1},{2,6},{6,2},{3,7},{7,3},{8,12},{12,8},{9,1... | collective-permute-start | bytes 2064392 | tf_op jit(solution)/shard_map/ppermute | solution.py:36
  48.0 6.6 %collective-permute-start.4 = (bf16[128,512]{1,0:T(8,128)(2,1)}, bf16[128,512]{1,0:T(8,128)(2,1)}, u32[]{:S(2)}, u32[]{:S(2)}) collective-permute-start(bf16[128,512]{1,0:T(8,128)(2,1)} %get-tuple-element.29), channel_id=1, source_target_pairs={{0,4},{4,0},{1,5},{5,1},{2,6},{6,2},{3,7},{7,3},{8,12},{12,8},{9,1... | collective-permute-start | bytes 393224 | tf_op jit(solution)/shard_map/ppermute | solution.py:36
  51.5 1.1 copy-start.3
  60.3 1.9 %copy-start.6 = (bf16[128,512]{1,0:T(8,128)(2,1)}, bf16[128,512]{1,0:T(8,128)(2,1)S(1)}, u32[]{:S(2)}) copy-start(bf16[128,512]{1,0:T(8,128)(2,1)S(1)} %get-tuple-element.31) | copy-start | bytes 393220
  60.3 3.9 %copy-start = (bf16[4,256,512]{2,1,0:T(8,128)(2,1)}, bf16[4,256,512]{2,1,0:T(8,128)(2,1)S(1)}, u32[]{:S(2)}) copy-start(bf16[4,256,512]{2,1,0:T(8,128)(2,1)S(1)} %get-tuple-element.38) | copy-start | bytes 3145732
  62.2 6.0 %collective-permute-start.6 = (bf16[384,1024]{1,0:T(8,128)(2,1)}, bf16[384,1024]{1,0:T(8,128)(2,1)S(1)}, u32[]{:S(2)}, u32[]{:S(2)}) collective-permute-start(bf16[384,1024]{1,0:T(8,128)(2,1)} %get-tuple-element.36), channel_id=1, source_target_pairs={{0,4},{4,0},{1,5},{5,1},{2,6},{6,2},{3,7},{7,3},{8,12},{12,8},{9,1... | collective-permute-start | bytes 2359304 | tf_op jit(solution)/shard_map/ppermute | solution.py:36
  64.1 19.8 %all-to-all-start.2 = ((bf16[4,256,512]{2,1,0:T(8,128)(2,1)}), bf16[4,256,512]{2,1,0:T(8,128)(2,1)S(1)}, u32[]{:S(2)}, u32[]{:S(2)}) async-start(bf16[4,256,512]{2,1,0:T(8,128)(2,1)} %copy-done), calls=%async_computation.2 | async-start | bytes 2097152 | tf_op jit(solution)/shard_map/all_to_all | solution.py:285
  68.4 28.1 %copy-start.7 = (bf16[128,512]{1,0:T(8,128)(2,1)S(1)}, bf16[128,512]{1,0:T(8,128)(2,1)}, u32[]{:S(2)}) copy-start(bf16[128,512]{1,0:T(8,128)(2,1)} %copy-done.6) | copy-start | bytes 393220
  68.4 15.5 %collective-permute-start.7 = (bf16[384,256]{1,0:T(8,128)(2,1)S(1)}, bf16[384,256]{1,0:T(8,128)(2,1)S(1)}, u32[]{:S(2)}, u32[]{:S(2)}) collective-permute-start(bf16[384,256]{1,0:T(8,128)(2,1)S(1)} %get-tuple-element.39), channel_id=1, source_target_pairs={{0,1},{1,2},{2,3},{3,0},{4,5},{5,6},{6,7},{7,4},{8,9},{9,10},{10,1... | collective-permute-start | bytes 589832 | tf_op jit(solution)/shard_map/ppermute | solution.py:297
  70.9 13.0 %collective-permute-start.8 = (bf16[384,256]{1,0:T(8,128)(2,1)S(1)}, bf16[384,256]{1,0:T(8,128)(2,1)S(1)}, u32[]{:S(2)}, u32[]{:S(2)}) collective-permute-start(bf16[384,256]{1,0:T(8,128)(2,1)S(1)} %get-tuple-element.40), channel_id=1, source_target_pairs={{0,3},{1,0},{2,1},{3,2},{4,7},{5,4},{6,5},{7,6},{8,11},{9,8},{10,9... | collective-permute-start | bytes 589832 | tf_op jit(solution)/shard_map/ppermute | solution.py:297
  84.8 27.3 %all-to-all-start.3 = ((bf16[16,16,512]{2,1,0:T(8,128)(2,1)}), bf16[16,16,512]{2,1,0:T(8,128)(2,1)S(1)}, u32[]{:S(2)}, u32[]{:S(2)}) async-start(bf16[16,16,512]{2,1,0:T(8,128)(2,1)} %bitcast.5), calls=%async_computation.3 | async-start | bytes 524288 | tf_op jit(solution)/shard_map/all_to_all | solution.py:303
  93.1 9.6 %collective-permute-start.9 = (bf16[384,256]{1,0:T(8,128)(2,1)S(1)}, bf16[384,256]{1,0:T(8,128)(2,1)S(1)}, u32[]{:S(2)}, u32[]{:S(2)}) collective-permute-start(bf16[384,256]{1,0:T(8,128)(2,1)S(1)} %get-tuple-element.43), channel_id=1, source_target_pairs={{0,2},{1,3},{2,0},{3,1},{4,6},{5,7},{6,4},{7,5},{8,10},{9,11},{10,... | collective-permute-start | bytes 589832 | tf_op jit(solution)/shard_map/ppermute | solution.py:297
  96.5 3.2 %collective-permute-start.5 = (bf16[128,512]{1,0:T(8,128)(2,1)S(1)}, bf16[128,512]{1,0:T(8,128)(2,1)S(1)}, u32[]{:S(2)}, u32[]{:S(2)}) collective-permute-start(bf16[128,512]{1,0:T(8,128)(2,1)S(1)} %copy-done.7), channel_id=1, source_target_pairs={{0,4},{4,0},{1,5},{5,1},{2,6},{6,2},{3,7},{7,3},{8,12},{12,8},{9,1... | collective-permute-start | bytes 393224 | tf_op jit(solution)/shard_map/ppermute | solution.py:36
  102.9 11.7 %collective-permute-start.10 = (bf16[128,256]{1,0:T(8,128)(2,1)S(1)}, bf16[128,256]{1,0:T(8,128)(2,1)S(1)}, u32[]{:S(2)}, u32[]{:S(2)}) collective-permute-start(bf16[128,256]{1,0:T(8,128)(2,1)S(1)} %get-tuple-element.46), channel_id=1, source_target_pairs={{0,8},{4,12},{8,16},{12,20},{16,24},{20,28},{24,32},{28,36},{32,40... | collective-permute-start | bytes 196616 | tf_op jit(solution)/shard_map/ppermute | solution.py:41
  106.4 8.2 %collective-permute-start.11 = (bf16[128,256]{1,0:T(8,128)(2,1)S(1)}, bf16[128,256]{1,0:T(8,128)(2,1)S(1)}, u32[]{:S(2)}, u32[]{:S(2)}) collective-permute-start(bf16[128,256]{1,0:T(8,128)(2,1)S(1)} %get-tuple-element.47), channel_id=1, source_target_pairs={{0,504},{4,508},{8,0},{12,4},{16,8},{20,12},{24,16},{28,20},{32,24... | collective-permute-start | bytes 196616 | tf_op jit(solution)/shard_map/ppermute | solution.py:41
  (1 other events, 0.9 us)

commit v7 on v5

--- a/solution.py
+++ b/solution.py
@@ -171,15 +171,10 @@
             acc_ref[block, vcols[i]] += vgrad[i][part, :]
     cb_ref[...] = acc_ref[...].astype(b16)
     copies = []
+    product = lax.dot_general(x_ref[...], cb_ref[...], TN, preferred_element_type=f32)
     for part in range(NY):
         size = out_ref.shape[1]
-        if part % 2 == 0:
-            product = lax.dot_general(
-                x_ref[:, part * size : (part + 2) * size], cb_ref[...], TN,
-                preferred_element_type=f32,
-            )
-        first = part % 2 * size
-        out_ref[part] = product[first : first + size, :].astype(b16)
+        out_ref[part] = product[part * size : (part + 1) * size, :].astype(b16)
         copies.append(pltpu.make_async_copy(out_ref.at[part], share_ref.at[part], sems.at[part]))
         copies[-1].start()
     for copy in copies:

time: 117 us -> 117 us (level)
  no operation moved by 1% of the time
where the time goes in v7:
time: 117 us; the launch traced here: 115 us
  starting transfers between devices  70.1 us (60%)
  waiting for transfers between devices  22.8 us (19%)
  Pallas kernels  13.4 us (11%)
  blocking collectives  3.89 us (3%)
  local copies, waits for them, and re-layouts  2.8 us (2%)
    ppermute x4, starting transfers between devices, shifted(): lax.ppermute(value, DP, [(i, (i + steps) % count) for i in range(count)])  18.6 us
    all_to_all x1, starting transfers between devices, per_device(): w = lax.all_to_all(copies, 'z', 0, 0).reshape(NZ * NC * PAD, SIDE)  15.2 us
    pallas_call x11, Pallas kernels, small_call(): pl.pallas_call(kernel, out_shape=outs, in_specs=[smem] * len(scalars) + [...  13.4 us
    ppermute x5, starting transfers between devices, swap_cores(): return lax.ppermute(value, 'c', [(0, 1), (1, 0)])  10.1 us
    all_to_all x1, waiting for transfers between devices, per_device(): parts = lax.all_to_all(share, 'y', 0, 0)  9.54 us
    ppermute x3, starting transfers between devices, per_device(): lax.ppermute(groups[step], 'x', [(i, (i + step) % NX) for i in range(NX)])  9.31 us
    all_to_all x1, starting transfers between devices, per_device(): parts = lax.all_to_all(total.reshape(NZ, NC * PAD, SIDE), 'z', 0, 0)  8.32 us
    all_to_all x1, waiting for transfers between devices, per_device(): w = lax.all_to_all(copies, 'z', 0, 0).reshape(NZ * NC * PAD, SIDE)  7.49 us
  transfers between devices with their start and end apart: 16, of which 6 were waited for; matrix products, arithmetic and copies ran while one was open for 2% of the time, Pallas kernels for 4%

profile of v7, /device:TPU:6, one launch (start us, length us, event | category | flops | bytes accessed | tf_op | source)
XLA Modules:
  0.0 115.0 jit_solution(14319290350384713004)
XLA Ops:
  0.6 2.0 %all-gather = bf16[14,2,512]{2,1,0:T(2,128)(2,1)S(1)} all-gather(bf16[7,2,512]{2,1,0:T(2,128)(2,1)} %param.7), channel_id=2, replica_groups=mesh['y'=4,'z'=16,'c'=2,'x'=4] {'c'}, dimensions={0}, use_global_device_ids=true | all-gather | bytes 43008 | tf_op jit(solution)/shard_map/all_gather | solution.py:239
  3.4 15.2 %all-to-all-start = ((bf16[16,16,512]{2,1,0:T(8,128)(2,1)}), bf16[16,16,512]{2,1,0:T(8,128)(2,1)S(1)}, u32[]{:S(2)}, u32[]{:S(2)}) async-start(bf16[16,16,512]{2,1,0:T(8,128)(2,1)} %shard_map.84), calls=%async_computation | async-start | bytes 524288 | tf_op jit(solution)/shard_map/all_to_all | solution.py:241
  18.6 7.5 %collective-permute-start.1 = (bf16[128,896]{1,0:T(8,128)(2,1)}, bf16[128,896]{1,0:T(8,128)(2,1)S(1)}, u32[]{:S(2)}, u32[]{:S(2)}) collective-permute-start(bf16[128,896]{1,0:T(8,128)(2,1)} %own_ref.1), channel_id=1, source_target_pairs={{0,504},{4,508},{8,0},{12,4},{16,8},{20,12},{24,16},{28,20},{32,24... | collective-permute-start | bytes 688136 | tf_op jit(solution)/shard_map/ppermute | solution.py:41
  26.1 1.9 %collective-permute-start.2 = (bf16[128,896]{1,0:T(8,128)(2,1)}, bf16[128,896]{1,0:T(8,128)(2,1)S(1)}, u32[]{:S(2)}, u32[]{:S(2)}) collective-permute-start(bf16[128,896]{1,0:T(8,128)(2,1)} %own_ref.1), channel_id=1, source_target_pairs={{0,8},{4,12},{8,16},{12,20},{16,24},{20,28},{24,32},{28,36},{32,40... | collective-permute-start | bytes 688136 | tf_op jit(solution)/shard_map/ppermute | solution.py:41
  28.0 1.9 %collective-permute-start = (s32[2,2]{1,0:T(2,128)}, s32[2,2]{1,0:T(2,128)S(1)}, u32[]{:S(2)}, u32[]{:S(2)}) collective-permute-start(s32[2,2]{1,0:T(2,128)} %param.8), channel_id=1, source_target_pairs={{0,4},{4,0},{1,5},{5,1},{2,6},{6,2},{3,7},{7,3},{8,12},{12,8},{9,1... | collective-permute-start | bytes 56 | tf_op jit(solution)/shard_map/ppermute | solution.py:36
  31.3 7.5 %all-to-all-done = bf16[16,16,512]{2,1,0:T(8,128)(2,1)S(1)} async-done(((bf16[16,16,512]{2,1,0:T(8,128)(2,1)}), bf16[16,16,512]{2,1,0:T(8,128)(2,1)S(1)}, u32[]{:S(2)}, u32[]{:S(2)}) %all-to-all-start) | async-done | bytes 262176 | tf_op jit(solution)/shard_map/all_to_all | solution.py:241
  39.8 4.6 %all-to-all-start.1 = ((bf16[4,256,512]{2,1,0:T(8,128)(2,1)}), bf16[4,256,512]{2,1,0:T(8,128)(2,1)S(1)}, u32[]{:S(2)}, u32[]{:S(2)}) async-start(bf16[4,256,512]{2,1,0:T(8,128)(2,1)} %shard_map.85), calls=%async_computation.1 | async-start | bytes 2097152 | tf_op jit(solution)/shard_map/all_to_all | solution.py:254
  45.4 1.9 %collective-permute-start.3 = (bf16[384,896]{1,0:T(8,128)(2,1)}, bf16[384,896]{1,0:T(8,128)(2,1)S(1)}, u32[]{:S(2)}, u32[]{:S(2)}) collective-permute-start(bf16[384,896]{1,0:T(8,128)(2,1)} %pad_maximum_fusion), channel_id=1, source_target_pairs={{0,4},{4,0},{1,5},{5,1},{2,6},{6,2},{3,7},{7,3},{8,12},{12,8},{9,1... | collective-permute-start | bytes 2064392 | tf_op jit(solution)/shard_map/ppermute | solution.py:36
  48.0 2.4 %collective-permute-start.4 = (bf16[128,512]{1,0:T(8,128)(2,1)}, bf16[128,512]{1,0:T(8,128)(2,1)}, u32[]{:S(2)}, u32[]{:S(2)}) collective-permute-start(bf16[128,512]{1,0:T(8,128)(2,1)} %get-tuple-element.29), channel_id=1, source_target_pairs={{0,4},{4,0},{1,5},{5,1},{2,6},{6,2},{3,7},{7,3},{8,12},{12,8},{9,1... | collective-permute-start | bytes 393224 | tf_op jit(solution)/shard_map/ppermute | solution.py:36
  52.6 1.9 %shard_map.86.x_ref = bf16[768,1024]{1,0:T(8,128)(2,1)S(1)} custom-call(bf16[128,896]{1,0:T(8,128)(2,1)S(1)} %copy-done.1, bf16[128,896]{1,0:T(8,128)(2,1)S(1)} %collective-permute-done.1.right_ref, bf16[128,896]{1,0:T(8,128)(2,1)S(1)} %collective-permute-done.2.left_ref, bf16[384,896]{1,0:T(8,128)(2,1)S(1)} %copy-done.3), custom_call_target="tpu_custom_call" | custom-call | flops 1000 | bytes 1000 | tf_op jit(solution)/shard_map/pallas_call | solution.py:52
  55.3 4.5 %shard_map.88 = (bf16[128,512]{1,0:T(8,128)(2,1)S(1)}, bf16[128,512]{1,0:T(8,128)(2,1)S(1)}, bf16[768,512]{1,0:T(8,128)(2,1)S(1)}, bf16[4,256,512]{2,1,0:T(8,128)(2,1)S(1)}) custom-call(s32[8]{0:T(128)S(1)} %fusion.sel_ref, bf16[768,1024]{1,0:T(8,128)(2,1)S(1)} %shard_map.86.x_ref, bf16[1024,512]{1,0:T(8,128)(2,1)S(1)} %bitcast.11, ...), custom_call_target="tpu_custom_call" | custom-call | flops 1000 | bytes 1000 | tf_op jit(solution)/shard_map/pallas_call | solution.py:52
  59.9 1.9 %shard_map.90 = (bf16[384,1024]{1,0:T(8,128)(2,1)S(1)}, bf16[384,1024]{1,0:T(8,128)(2,1)}) custom-call(bf16[1024,512]{1,0:T(8,128)(2,1)S(1)} %bitcast.12, bf16[768,512]{1,0:T(8,128)(2,1)S(1)} %get-tuple-element.34.cb_ref), custom_call_target="tpu_custom_call" | custom-call | flops 1000 | bytes 1000 | tf_op jit(solution)/shard_map/pallas_call | solution.py:52
  61.8 1.9 %collective-permute-start.6 = (bf16[384,1024]{1,0:T(8,128)(2,1)}, bf16[384,1024]{1,0:T(8,128)(2,1)S(1)}, u32[]{:S(2)}, u32[]{:S(2)}) collective-permute-start(bf16[384,1024]{1,0:T(8,128)(2,1)} %get-tuple-element.36), channel_id=1, source_target_pairs={{0,4},{4,0},{1,5},{5,1},{2,6},{6,2},{3,7},{7,3},{8,12},{12,8},{9,1... | collective-permute-start | bytes 2359304 | tf_op jit(solution)/shard_map/ppermute | solution.py:36
  63.7 4.0 %all-to-all-start.2 = ((bf16[4,256,512]{2,1,0:T(8,128)(2,1)}), bf16[4,256,512]{2,1,0:T(8,128)(2,1)S(1)}, u32[]{:S(2)}, u32[]{:S(2)}) async-start(bf16[4,256,512]{2,1,0:T(8,128)(2,1)} %copy-done), calls=%async_computation.2 | async-start | bytes 2097152 | tf_op jit(solution)/shard_map/all_to_all | solution.py:280
  68.0 2.5 %collective-permute-start.7 = (bf16[384,256]{1,0:T(8,128)(2,1)S(1)}, bf16[384,256]{1,0:T(8,128)(2,1)S(1)}, u32[]{:S(2)}, u32[]{:S(2)}) collective-permute-start(bf16[384,256]{1,0:T(8,128)(2,1)S(1)} %get-tuple-element.39), channel_id=1, source_target_pairs={{0,1},{1,2},{2,3},{3,0},{4,5},{5,6},{6,7},{7,4},{8,9},{9,10},{10,1... | collective-permute-start | bytes 589832 | tf_op jit(solution)/shard_map/ppermute | solution.py:292
  70.5 3.5 %collective-permute-start.8 = (bf16[384,256]{1,0:T(8,128)(2,1)S(1)}, bf16[384,256]{1,0:T(8,128)(2,1)S(1)}, u32[]{:S(2)}, u32[]{:S(2)}) collective-permute-start(bf16[384,256]{1,0:T(8,128)(2,1)S(1)} %get-tuple-element.40), channel_id=1, source_target_pairs={{0,3},{1,0},{2,1},{3,2},{4,7},{5,4},{6,5},{7,6},{8,11},{9,8},{10,9... | collective-permute-start | bytes 589832 | tf_op jit(solution)/shard_map/ppermute | solution.py:292
  74.0 9.5 %all-to-all-done.2.parts_ref = bf16[4,256,512]{2,1,0:T(8,128)(2,1)S(1)} async-done(((bf16[4,256,512]{2,1,0:T(8,128)(2,1)}), bf16[4,256,512]{2,1,0:T(8,128)(2,1)S(1)}, u32[]{:S(2)}, u32[]{:S(2)}) %all-to-all-start.2) | async-done | bytes 1048608 | tf_op jit(solution)/shard_map/all_to_all | solution.py:280
  84.3 8.3 %all-to-all-start.3 = ((bf16[16,16,512]{2,1,0:T(8,128)(2,1)}), bf16[16,16,512]{2,1,0:T(8,128)(2,1)S(1)}, u32[]{:S(2)}, u32[]{:S(2)}) async-start(bf16[16,16,512]{2,1,0:T(8,128)(2,1)} %bitcast.5), calls=%async_computation.3 | async-start | bytes 524288 | tf_op jit(solution)/shard_map/all_to_all | solution.py:298
  92.7 3.3 %collective-permute-start.9 = (bf16[384,256]{1,0:T(8,128)(2,1)S(1)}, bf16[384,256]{1,0:T(8,128)(2,1)S(1)}, u32[]{:S(2)}, u32[]{:S(2)}) collective-permute-start(bf16[384,256]{1,0:T(8,128)(2,1)S(1)} %get-tuple-element.43), channel_id=1, source_target_pairs={{0,2},{1,3},{2,0},{3,1},{4,6},{5,7},{6,4},{7,5},{8,10},{9,11},{10,... | collective-permute-start | bytes 589832 | tf_op jit(solution)/shard_map/ppermute | solution.py:292
  96.0 1.9 %collective-permute-start.5 = (bf16[128,512]{1,0:T(8,128)(2,1)S(1)}, bf16[128,512]{1,0:T(8,128)(2,1)S(1)}, u32[]{:S(2)}, u32[]{:S(2)}) collective-permute-start(bf16[128,512]{1,0:T(8,128)(2,1)S(1)} %copy-done.7), channel_id=1, source_target_pairs={{0,4},{4,0},{1,5},{5,1},{2,6},{6,2},{3,7},{7,3},{8,12},{12,8},{9,1... | collective-permute-start | bytes 393224 | tf_op jit(solution)/shard_map/ppermute | solution.py:36
  100.0 2.3 %collective-permute-done.9.c_ref = bf16[384,256]{1,0:T(8,128)(2,1)S(1)} collective-permute-done((bf16[384,256]{1,0:T(8,128)(2,1)S(1)}, bf16[384,256]{1,0:T(8,128)(2,1)S(1)}, u32[]{:S(2)}, u32[]{:S(2)}) %collective-permute-start.9) | collective-permute-done | bytes 196640 | tf_op jit(solution)/shard_map/ppermute | solution.py:292
  102.4 3.5 %collective-permute-start.10 = (bf16[128,256]{1,0:T(8,128)(2,1)S(1)}, bf16[128,256]{1,0:T(8,128)(2,1)S(1)}, u32[]{:S(2)}, u32[]{:S(2)}) collective-permute-start(bf16[128,256]{1,0:T(8,128)(2,1)S(1)} %get-tuple-element.46), channel_id=1, source_target_pairs={{0,8},{4,12},{8,16},{12,20},{16,24},{20,28},{24,32},{28,36},{32,40... | collective-permute-start | bytes 196616 | tf_op jit(solution)/shard_map/ppermute | solution.py:41
  106.0 5.6 %collective-permute-start.11 = (bf16[128,256]{1,0:T(8,128)(2,1)S(1)}, bf16[128,256]{1,0:T(8,128)(2,1)S(1)}, u32[]{:S(2)}, u32[]{:S(2)}) collective-permute-start(bf16[128,256]{1,0:T(8,128)(2,1)S(1)} %get-tuple-element.47), channel_id=1, source_target_pairs={{0,504},{4,508},{8,0},{12,4},{16,8},{20,12},{24,16},{28,20},{32,24... | collective-permute-start | bytes 196616 | tf_op jit(solution)/shard_map/ppermute | solution.py:41
  111.7 1.9 %all-gather.1 = f32[32,512]{1,0:T(8,128)S(1)} all-gather(f32[16,512]{1,0:T(8,128)S(1)} %convert_reduce_fusion), channel_id=3, replica_groups=mesh['y'=4,'z'=16,'c'=2,'x'=4] {'c'}, dimensions={0}, use_global_device_ids=true | all-gather | bytes 98304 | tf_op jit(solution)/shard_map/all_gather | solution.py:299
  (47 shorter events, 12.4 us)
Async XLA Ops:
  3.4 35.4 %all-to-all-start = ((bf16[16,16,512]{2,1,0:T(8,128)(2,1)}), bf16[16,16,512]{2,1,0:T(8,128)(2,1)S(1)}, u32[]{:S(2)}, u32[]{:S(2)}) async-start(bf16[16,16,512]{2,1,0:T(8,128)(2,1)} %shard_map.84), calls=%async_computation | async-start | bytes 524288 | tf_op jit(solution)/shard_map/all_to_all | solution.py:241
  18.6 25.8 %collective-permute-start.1 = (bf16[128,896]{1,0:T(8,128)(2,1)}, bf16[128,896]{1,0:T(8,128)(2,1)S(1)}, u32[]{:S(2)}, u32[]{:S(2)}) collective-permute-start(bf16[128,896]{1,0:T(8,128)(2,1)} %own_ref.1), channel_id=1, source_target_pairs={{0,504},{4,508},{8,0},{12,4},{16,8},{20,12},{24,16},{28,20},{32,24... | collective-permute-start | bytes 688136 | tf_op jit(solution)/shard_map/ppermute | solution.py:41
  26.1 18.4 %collective-permute-start.2 = (bf16[128,896]{1,0:T(8,128)(2,1)}, bf16[128,896]{1,0:T(8,128)(2,1)S(1)}, u32[]{:S(2)}, u32[]{:S(2)}) collective-permute-start(bf16[128,896]{1,0:T(8,128)(2,1)} %own_ref.1), channel_id=1, source_target_pairs={{0,8},{4,12},{8,16},{12,20},{16,24},{20,28},{24,32},{28,36},{32,40... | collective-permute-start | bytes 688136 | tf_op jit(solution)/shard_map/ppermute | solution.py:41
  28.0 3.2 %collective-permute-start = (s32[2,2]{1,0:T(2,128)}, s32[2,2]{1,0:T(2,128)S(1)}, u32[]{:S(2)}, u32[]{:S(2)}) collective-permute-start(s32[2,2]{1,0:T(2,128)} %param.8), channel_id=1, source_target_pairs={{0,4},{4,0},{1,5},{5,1},{2,6},{6,2},{3,7},{7,3},{8,12},{12,8},{9,1... | collective-permute-start | bytes 56 | tf_op jit(solution)/shard_map/ppermute | solution.py:36
  39.8 4.7 %copy-start.1 = (bf16[128,896]{1,0:T(8,128)(2,1)S(1)}, bf16[128,896]{1,0:T(8,128)(2,1)}, u32[]{:S(2)}) copy-start(bf16[128,896]{1,0:T(8,128)(2,1)} %own_ref.1) | copy-start | bytes 688132
  39.8 7.5 %copy-start.4 = (bf16[128,512]{1,0:T(8,128)(2,1)S(1)}, bf16[128,512]{1,0:T(8,128)(2,1)}, u32[]{:S(2)}) copy-start(bf16[128,512]{1,0:T(8,128)(2,1)} %q_ref.1) | copy-start | bytes 393220
  39.8 7.5 %copy-start.5 = (bf16[128,512]{1,0:T(8,128)(2,1)S(1)}, bf16[128,512]{1,0:T(8,128)(2,1)}, u32[]{:S(2)}) copy-start(bf16[128,512]{1,0:T(8,128)(2,1)} %g_ref.1) | copy-start | bytes 393220
  39.8 10.6 %copy-start.8 = (s32[2,2]{1,0:T(2,128)S(1)}, s32[2,2]{1,0:T(2,128)}, u32[]{:S(2)}) copy-start(s32[2,2]{1,0:T(2,128)} %param.8) | copy-start | bytes 52
  39.8 15.5 %all-to-all-start.1 = ((bf16[4,256,512]{2,1,0:T(8,128)(2,1)}), bf16[4,256,512]{2,1,0:T(8,128)(2,1)S(1)}, u32[]{:S(2)}, u32[]{:S(2)}) async-start(bf16[4,256,512]{2,1,0:T(8,128)(2,1)} %shard_map.85), calls=%async_computation.1 | async-start | bytes 2097152 | tf_op jit(solution)/shard_map/all_to_all | solution.py:254
  45.4 5.3 %collective-permute-start.3 = (bf16[384,896]{1,0:T(8,128)(2,1)}, bf16[384,896]{1,0:T(8,128)(2,1)S(1)}, u32[]{:S(2)}, u32[]{:S(2)}) collective-permute-start(bf16[384,896]{1,0:T(8,128)(2,1)} %pad_maximum_fusion), channel_id=1, source_target_pairs={{0,4},{4,0},{1,5},{5,1},{2,6},{6,2},{3,7},{7,3},{8,12},{12,8},{9,1... | collective-permute-start | bytes 2064392 | tf_op jit(solution)/shard_map/ppermute | solution.py:36
  48.0 6.6 %collective-permute-start.4 = (bf16[128,512]{1,0:T(8,128)(2,1)}, bf16[128,512]{1,0:T(8,128)(2,1)}, u32[]{:S(2)}, u32[]{:S(2)}) collective-permute-start(bf16[128,512]{1,0:T(8,128)(2,1)} %get-tuple-element.29), channel_id=1, source_target_pairs={{0,4},{4,0},{1,5},{5,1},{2,6},{6,2},{3,7},{7,3},{8,12},{12,8},{9,1... | collective-permute-start | bytes 393224 | tf_op jit(solution)/shard_map/ppermute | solution.py:36
  51.5 1.1 copy-start.3
  59.8 1.9 %copy-start.6 = (bf16[128,512]{1,0:T(8,128)(2,1)}, bf16[128,512]{1,0:T(8,128)(2,1)S(1)}, u32[]{:S(2)}) copy-start(bf16[128,512]{1,0:T(8,128)(2,1)S(1)} %get-tuple-element.31) | copy-start | bytes 393220
  59.9 3.9 %copy-start = (bf16[4,256,512]{2,1,0:T(8,128)(2,1)}, bf16[4,256,512]{2,1,0:T(8,128)(2,1)S(1)}, u32[]{:S(2)}) copy-start(bf16[4,256,512]{2,1,0:T(8,128)(2,1)S(1)} %get-tuple-element.38) | copy-start | bytes 3145732
  61.8 6.0 %collective-permute-start.6 = (bf16[384,1024]{1,0:T(8,128)(2,1)}, bf16[384,1024]{1,0:T(8,128)(2,1)S(1)}, u32[]{:S(2)}, u32[]{:S(2)}) collective-permute-start(bf16[384,1024]{1,0:T(8,128)(2,1)} %get-tuple-element.36), channel_id=1, source_target_pairs={{0,4},{4,0},{1,5},{5,1},{2,6},{6,2},{3,7},{7,3},{8,12},{12,8},{9,1... | collective-permute-start | bytes 2359304 | tf_op jit(solution)/shard_map/ppermute | solution.py:36
  63.7 19.8 %all-to-all-start.2 = ((bf16[4,256,512]{2,1,0:T(8,128)(2,1)}), bf16[4,256,512]{2,1,0:T(8,128)(2,1)S(1)}, u32[]{:S(2)}, u32[]{:S(2)}) async-start(bf16[4,256,512]{2,1,0:T(8,128)(2,1)} %copy-done), calls=%async_computation.2 | async-start | bytes 2097152 | tf_op jit(solution)/shard_map/all_to_all | solution.py:280
  68.0 28.1 %copy-start.7 = (bf16[128,512]{1,0:T(8,128)(2,1)S(1)}, bf16[128,512]{1,0:T(8,128)(2,1)}, u32[]{:S(2)}) copy-start(bf16[128,512]{1,0:T(8,128)(2,1)} %copy-done.6) | copy-start | bytes 393220
  68.0 15.5 %collective-permute-start.7 = (bf16[384,256]{1,0:T(8,128)(2,1)S(1)}, bf16[384,256]{1,0:T(8,128)(2,1)S(1)}, u32[]{:S(2)}, u32[]{:S(2)}) collective-permute-start(bf16[384,256]{1,0:T(8,128)(2,1)S(1)} %get-tuple-element.39), channel_id=1, source_target_pairs={{0,1},{1,2},{2,3},{3,0},{4,5},{5,6},{6,7},{7,4},{8,9},{9,10},{10,1... | collective-permute-start | bytes 589832 | tf_op jit(solution)/shard_map/ppermute | solution.py:292
  70.5 13.0 %collective-permute-start.8 = (bf16[384,256]{1,0:T(8,128)(2,1)S(1)}, bf16[384,256]{1,0:T(8,128)(2,1)S(1)}, u32[]{:S(2)}, u32[]{:S(2)}) collective-permute-start(bf16[384,256]{1,0:T(8,128)(2,1)S(1)} %get-tuple-element.40), channel_id=1, source_target_pairs={{0,3},{1,0},{2,1},{3,2},{4,7},{5,4},{6,5},{7,6},{8,11},{9,8},{10,9... | collective-permute-start | bytes 589832 | tf_op jit(solution)/shard_map/ppermute | solution.py:292
  84.3 27.3 %all-to-all-start.3 = ((bf16[16,16,512]{2,1,0:T(8,128)(2,1)}), bf16[16,16,512]{2,1,0:T(8,128)(2,1)S(1)}, u32[]{:S(2)}, u32[]{:S(2)}) async-start(bf16[16,16,512]{2,1,0:T(8,128)(2,1)} %bitcast.5), calls=%async_computation.3 | async-start | bytes 524288 | tf_op jit(solution)/shard_map/all_to_all | solution.py:298
  92.7 9.6 %collective-permute-start.9 = (bf16[384,256]{1,0:T(8,128)(2,1)S(1)}, bf16[384,256]{1,0:T(8,128)(2,1)S(1)}, u32[]{:S(2)}, u32[]{:S(2)}) collective-permute-start(bf16[384,256]{1,0:T(8,128)(2,1)S(1)} %get-tuple-element.43), channel_id=1, source_target_pairs={{0,2},{1,3},{2,0},{3,1},{4,6},{5,7},{6,4},{7,5},{8,10},{9,11},{10,... | collective-permute-start | bytes 589832 | tf_op jit(solution)/shard_map/ppermute | solution.py:292
  96.0 3.2 %collective-permute-start.5 = (bf16[128,512]{1,0:T(8,128)(2,1)S(1)}, bf16[128,512]{1,0:T(8,128)(2,1)S(1)}, u32[]{:S(2)}, u32[]{:S(2)}) collective-permute-start(bf16[128,512]{1,0:T(8,128)(2,1)S(1)} %copy-done.7), channel_id=1, source_target_pairs={{0,4},{4,0},{1,5},{5,1},{2,6},{6,2},{3,7},{7,3},{8,12},{12,8},{9,1... | collective-permute-start | bytes 393224 | tf_op jit(solution)/shard_map/ppermute | solution.py:36
  102.4 11.7 %collective-permute-start.10 = (bf16[128,256]{1,0:T(8,128)(2,1)S(1)}, bf16[128,256]{1,0:T(8,128)(2,1)S(1)}, u32[]{:S(2)}, u32[]{:S(2)}) collective-permute-start(bf16[128,256]{1,0:T(8,128)(2,1)S(1)} %get-tuple-element.46), channel_id=1, source_target_pairs={{0,8},{4,12},{8,16},{12,20},{16,24},{20,28},{24,32},{28,36},{32,40... | collective-permute-start | bytes 196616 | tf_op jit(solution)/shard_map/ppermute | solution.py:41
  106.0 8.2 %collective-permute-start.11 = (bf16[128,256]{1,0:T(8,128)(2,1)S(1)}, bf16[128,256]{1,0:T(8,128)(2,1)S(1)}, u32[]{:S(2)}, u32[]{:S(2)}) collective-permute-start(bf16[128,256]{1,0:T(8,128)(2,1)S(1)} %get-tuple-element.47), channel_id=1, source_target_pairs={{0,504},{4,508},{8,0},{12,4},{16,8},{20,12},{24,16},{28,20},{32,24... | collective-permute-start | bytes 196616 | tf_op jit(solution)/shard_map/ppermute | solution.py:41
  (1 other events, 0.9 us)
